TPU v7x, 32 devices: a whole 2x2x4 slice. The times are simulated.
32 devices in a mesh: seq: 8 (over y, x, core), slot: 4 (over z).
Axes of the slice: x: 2, y: 2, z: 4, core: 2. Of those that a mesh axis runs over, the one named last changes fastest.
Arguments:
- tokens: bfloat16 [4, 1024, 1024], P('slot', 'seq'), may hold values from -6 to 6
- lengths: int32 [4], P('slot'), may hold values from 897 to 1024, as said below
- query_weight: bfloat16 [1024, 1024], P('seq'), may hold values from -0.1875 to 0.1875
- key_weight: bfloat16 [1024, 512], P('seq'), may hold values from -0.1875 to 0.1875
- value_weight: bfloat16 [1024, 512], P('seq'), may hold values from -0.1875 to 0.1875
- out_weight: bfloat16 [1024, 1024], P('seq'), may hold values from -1.5 to 1.5
- gate_weight: bfloat16 [1024, 4608], P('seq'), may hold values from -0.1875 to 0.1875
- up_weight: bfloat16 [1024, 4608], P('seq'), may hold values from -0.1875 to 0.1875
- down_weight: bfloat16 [1024, 4608], P('seq'), may hold values from -0.09375 to 0.09375
- attn_norm: float32 [1024], replicated, may hold values from 0.5 to 1.5
- query_norm: float32 [64], replicated, may hold values from 0.1 to 1.9
- key_norm: float32 [64], replicated, may hold values from 0.1 to 1.9
- ffn_norm: float32 [1024], replicated, may hold values from 0.5 to 1.5
- out_grad: bfloat16 [4, 1024, 1024], P('slot', 'seq'), may hold values from -6 to 6
Outputs:
- mixed: bfloat16 [4, 1024, 1024], P('slot', 'seq')
- input_grad: bfloat16 [4, 1024, 1024], P('slot', 'seq')
- query_weight_grad: float32 [1024, 1024], P('seq')
- key_weight_grad: float32 [1024, 512], P('seq')
- value_weight_grad: float32 [1024, 512], P('seq')
- out_weight_grad: float32 [1024, 1024], P('seq')
- gate_weight_grad: float32 [1024, 4608], P('seq')
- up_weight_grad: float32 [1024, 4608], P('seq')
- down_weight_grad: float32 [1024, 4608], P('seq')
- attn_norm_grad: float32 [1024], replicated
- query_norm_grad: float32 [64], replicated
- key_norm_grad: float32 [64], replicated
- ffn_norm_grad: float32 [1024], replicated
Inputs may be any that keep to these rules, and one draw needn't show every extreme that they name: `lengths`: each slot's true length is more than 896; some slot's length is exactly 1024.
All inputs are finite; a program needn't handle non-finite values.
Results may differ from a plain program's by a relative error of at most 0.035.
Values may be sent and summed in bfloat16 or wider, within the bound.
No kernel may reach another device: no remote copies, remote signals or barrier semaphores. Data moves between devices by JAX's collectives and lax.ppermute only.
A program may use at most 320 MiB of HBM per device.

v0:
```python
import jax
import jax.numpy as jnp
from jax import lax
from jax.sharding import PartitionSpec as P

HEADS = 16
KV_HEADS = 8
HEAD_DIM = 64


EPSILON = 1e-05
THETA_BASE = 1000000.0
MASK_FILL = -1e30
HIGHEST = lax.Precision.HIGHEST


def rms_apply(values, gain_vec):
    factor = lax.rsqrt(jnp.mean(values * values, axis=-1, keepdims=True) + EPSILON)
    return (values * factor * gain_vec, factor)


def rms_back(values, factor, gain_vec, upstream):
    normal = values * factor
    weighted = upstream * gain_vec
    shared = jnp.mean(weighted * normal, axis=-1, keepdims=True)
    return (factor * (weighted - normal * shared), upstream * normal)


def rotary_tables(position):
    exponent = jnp.arange(HEAD_DIM // 2, dtype=jnp.float32) * (2.0 / HEAD_DIM)
    inverse = THETA_BASE ** (-exponent)
    angles = position.astype(jnp.float32)[:, None] * inverse[None, :]
    cosine = jnp.concatenate([jnp.cos(angles), jnp.cos(angles)], axis=-1)
    sine_tab = jnp.concatenate([jnp.sin(angles), jnp.sin(angles)], axis=-1)
    return (cosine, sine_tab)


def rotate(values, cosine, sine_tab):
    half_dim = values.shape[-1] // 2
    turned = jnp.concatenate([-values[..., half_dim:], values[..., :half_dim]], axis=-1)
    return values * cosine[:, None, :] + turned * sine_tab[:, None, :]


def rotate_back(upstream, cosine, sine_tab):
    half_dim = upstream.shape[-1] // 2
    scaled = upstream * sine_tab[:, None, :]
    turned = jnp.concatenate([scaled[..., half_dim:], -scaled[..., :half_dim]], axis=-1)
    return upstream * cosine[:, None, :] + turned


def contract_rows(left, right):
    return lax.dot_general(
        left, right, (((0,), (0,)), ((), ())), preferred_element_type=jnp.float32
    )


def contract_cols(left, right):
    return lax.dot_general(
        left, right, (((1,), (1,)), ((), ())), preferred_element_type=jnp.float32
    )


def body(
    tokens,
    lengths,
    query_weight,
    key_weight,
    value_weight,
    out_weight,
    gate_weight,
    up_weight,
    down_weight,
    attn_norm,
    query_norm,
    key_norm,
    ffn_norm,
    out_grad,
):
    tok_rows = tokens.shape[1]
    group_size = HEADS // KV_HEADS
    kv_width = KV_HEADS * HEAD_DIM
    score_scale = HEAD_DIM ** (-0.5)
    length = lengths[0]
    my_index = lax.axis_index("seq")
    position = my_index * tok_rows + jnp.arange(tok_rows, dtype=jnp.int32)
    row_valid = (position < length)[:, None]
    cosine, sine_tab = rotary_tables(position)
    inputs = tokens[0].astype(jnp.float32)
    query_full, key_full, value_full, out_full, gate_full, up_full, down_full = (
        lax.all_gather(query_weight, "seq", axis=0, tiled=True),
        lax.all_gather(key_weight, "seq", axis=0, tiled=True),
        lax.all_gather(value_weight, "seq", axis=0, tiled=True),
        lax.all_gather(out_weight, "seq", axis=0, tiled=True),
        lax.all_gather(gate_weight, "seq", axis=0, tiled=True),
        lax.all_gather(up_weight, "seq", axis=0, tiled=True),
        lax.all_gather(down_weight, "seq", axis=0, tiled=True),
    )
    normed_float, factor_one = rms_apply(inputs, attn_norm)
    normed = normed_float.astype(jnp.bfloat16)
    query_proj = jnp.dot(normed, query_full, preferred_element_type=jnp.float32).reshape(
        tok_rows, HEADS, HEAD_DIM
    )
    key_proj = jnp.dot(normed, key_full, preferred_element_type=jnp.float32).reshape(
        tok_rows, KV_HEADS, HEAD_DIM
    )
    value_low = jnp.dot(normed, value_full, preferred_element_type=jnp.float32).astype(jnp.bfloat16)
    query_unit, query_factor = rms_apply(query_proj, query_norm)
    key_unit, key_factor = rms_apply(key_proj, key_norm)
    query_low = (
        rotate(query_unit, cosine, sine_tab)
        .astype(jnp.bfloat16)
        .reshape(tok_rows, KV_HEADS, group_size, HEAD_DIM)
    )
    key_low = rotate(key_unit, cosine, sine_tab).astype(jnp.bfloat16).reshape(tok_rows, kv_width)

    def piece_scores(key_heads):
        key_count = key_heads.shape[0]
        scores = (
            jnp.einsum("tgrd,ngd->grtn", query_low, key_heads, preferred_element_type=jnp.float32)
            * score_scale
        )
        key_place = jnp.arange(key_count, dtype=jnp.int32)
        allowed = (key_place[None, :] <= position[:, None]) & (key_place[None, :] < length)
        return (scores, allowed)

    piece = (
        lax.all_gather(key_low, "seq", axis=0, tiled=True),
        lax.all_gather(value_low, "seq", axis=0, tiled=True),
    )
    forward_top_score = jnp.full((KV_HEADS, group_size, tok_rows), MASK_FILL, jnp.float32)
    key_heads = piece[0].reshape(-1, KV_HEADS, HEAD_DIM)
    value_heads = piece[1].reshape(-1, KV_HEADS, HEAD_DIM)
    scores, allowed = piece_scores(key_heads)
    masked = jnp.where(allowed, scores, MASK_FILL)
    new_top = jnp.maximum(forward_top_score, jnp.max(masked, axis=-1))
    weights = jnp.where(allowed, jnp.exp(masked - new_top[..., None]), 0.0)
    forward_weight_sum = jnp.sum(weights, axis=-1)
    added = jnp.einsum(
        "grtn,ngd->tgrd",
        weights.astype(jnp.bfloat16),
        value_heads,
        preferred_element_type=jnp.float32,
    )
    accum = added
    top_score, weight_sum, accum = (new_top, forward_weight_sum, accum)
    attn_heads = accum / jnp.transpose(weight_sum, (2, 0, 1))[..., None]
    attn_low = attn_heads.reshape(tok_rows, HEADS * HEAD_DIM).astype(jnp.bfloat16)
    residual = inputs + contract_cols(attn_low, out_full)
    normed_two_float, factor_two = rms_apply(residual, ffn_norm)
    normed_two = normed_two_float.astype(jnp.bfloat16)
    gate_val = jnp.dot(normed_two, gate_full, preferred_element_type=jnp.float32)
    up_val = jnp.dot(normed_two, up_full, preferred_element_type=jnp.float32)
    sigmoid_gate = jax.nn.sigmoid(gate_val)
    silu_gate = gate_val * sigmoid_gate
    hidden = (silu_gate * up_val).astype(jnp.bfloat16)
    result = residual + contract_cols(hidden, down_full)
    mixed = jnp.where(row_valid, result, 0.0).astype(jnp.bfloat16)[None]
    query_full, key_full, value_full, out_full, gate_full, up_full, down_full = (
        lax.all_gather(query_weight, "seq", axis=0, tiled=True),
        lax.all_gather(key_weight, "seq", axis=0, tiled=True),
        lax.all_gather(value_weight, "seq", axis=0, tiled=True),
        lax.all_gather(out_weight, "seq", axis=0, tiled=True),
        lax.all_gather(gate_weight, "seq", axis=0, tiled=True),
        lax.all_gather(up_weight, "seq", axis=0, tiled=True),
        lax.all_gather(down_weight, "seq", axis=0, tiled=True),
    )
    upstream = jnp.where(row_valid, out_grad[0].astype(jnp.float32), 0.0)
    branch_grad = upstream.astype(jnp.bfloat16)
    hidden_grad = jnp.dot(branch_grad, down_full, preferred_element_type=jnp.float32)
    down_w_grad = contract_rows(branch_grad, hidden)
    gate_grad_low = (
        hidden_grad * up_val * sigmoid_gate * (1.0 + gate_val * (1.0 - sigmoid_gate))
    ).astype(jnp.bfloat16)
    up_grad_low = (hidden_grad * silu_gate).astype(jnp.bfloat16)
    normed_two_grad = contract_cols(gate_grad_low, gate_full) + contract_cols(up_grad_low, up_full)
    gate_w_grad = contract_rows(normed_two, gate_grad_low)
    up_w_grad = contract_rows(normed_two, up_grad_low)
    residual_part, ffn_terms = rms_back(residual, factor_two, ffn_norm, normed_two_grad)
    residual_grad = upstream + residual_part
    attn_out_low = residual_grad.astype(jnp.bfloat16)
    out_w_grad = contract_rows(attn_out_low, attn_low)
    attn_grad_low = jnp.dot(attn_out_low, out_full, preferred_element_type=jnp.float32).astype(
        jnp.bfloat16
    )
    attn_grad_heads = attn_grad_low.reshape(tok_rows, KV_HEADS, group_size, HEAD_DIM)
    row_inner = jnp.transpose(
        jnp.sum(attn_grad_heads.astype(jnp.float32) * attn_heads, axis=-1), (1, 2, 0)
    )
    scaled_grad = (
        attn_grad_heads.astype(jnp.float32) / jnp.transpose(weight_sum, (2, 0, 1))[..., None]
    )
    piece = (
        lax.all_gather(key_low, "seq", axis=0, tiled=True),
        lax.all_gather(value_low, "seq", axis=0, tiled=True),
    )
    key_heads = piece[0].reshape(-1, KV_HEADS, HEAD_DIM)
    value_heads = piece[1].reshape(-1, KV_HEADS, HEAD_DIM)
    key_count = key_heads.shape[0]
    scores, allowed = piece_scores(key_heads)
    shifted = jnp.where(allowed, scores - top_score[..., None], MASK_FILL)
    exp_vals = jnp.where(allowed, jnp.exp(shifted), 0.0)
    probs = exp_vals / weight_sum[..., None]
    prob_grad = jnp.einsum(
        "tgrd,ngd->grtn", attn_grad_heads, value_heads, preferred_element_type=jnp.float32
    )
    score_grad = (probs * (prob_grad - row_inner[..., None])).astype(jnp.bfloat16)
    backward_query_acc = (
        jnp.einsum("grtn,ngd->tgrd", score_grad, key_heads, preferred_element_type=jnp.float32)
        * score_scale
    )
    key_part = (
        jnp.einsum("grtn,tgrd->ngd", score_grad, query_low, preferred_element_type=jnp.float32)
        * score_scale
    )
    exp_low = exp_vals.astype(jnp.bfloat16).astype(jnp.float32)
    value_part = jnp.einsum(
        "grtn,tgrd->ngd",
        exp_low,
        scaled_grad,
        precision=HIGHEST,
        preferred_element_type=jnp.float32,
    )
    update = jnp.concatenate(
        [key_part.reshape(key_count, kv_width), value_part.reshape(key_count, kv_width)], axis=1
    )
    query_acc, update = (backward_query_acc, update)
    key_buffer = update
    query_acc, key_buffer = (query_acc, key_buffer)
    key_value_grad = lax.psum_scatter(key_buffer, "seq", scatter_dimension=0, tiled=True)
    key_rot_grad = key_value_grad[:, :kv_width].reshape(tok_rows, KV_HEADS, HEAD_DIM)
    value_grad_low = key_value_grad[:, kv_width:].astype(jnp.bfloat16)
    query_rot_grad = query_acc.reshape(tok_rows, HEADS, HEAD_DIM)
    query_proj_grad, query_terms = rms_back(
        query_proj, query_factor, query_norm, rotate_back(query_rot_grad, cosine, sine_tab)
    )
    key_proj_grad, key_terms = rms_back(
        key_proj, key_factor, key_norm, rotate_back(key_rot_grad, cosine, sine_tab)
    )
    query_grad_low = query_proj_grad.reshape(tok_rows, HEADS * HEAD_DIM).astype(jnp.bfloat16)
    key_grad_low = key_proj_grad.reshape(tok_rows, kv_width).astype(jnp.bfloat16)
    normed_grad = (
        contract_cols(query_grad_low, query_full)
        + contract_cols(key_grad_low, key_full)
        + contract_cols(value_grad_low, value_full)
    )
    query_w_grad = contract_rows(normed, query_grad_low)
    key_w_grad = contract_rows(normed, key_grad_low)
    value_w_grad = contract_rows(normed, value_grad_low)
    input_part, attn_terms = rms_back(inputs, factor_one, attn_norm, normed_grad)
    input_grad = (residual_grad + input_part).astype(jnp.bfloat16)[None]
    attn_gain_grad, query_gain_grad, key_gain_grad, ffn_gain_grad = lax.psum(
        (
            jnp.sum(attn_terms, axis=0),
            jnp.sum(query_terms, axis=(0, 1)),
            jnp.sum(key_terms, axis=(0, 1)),
            jnp.sum(ffn_terms, axis=0),
        ),
        ("seq", "slot"),
    )
    query_share, key_share, value_share, out_share, gate_share, up_share, down_share = (
        lax.psum_scatter(query_w_grad, "seq", scatter_dimension=0, tiled=True),
        lax.psum_scatter(key_w_grad, "seq", scatter_dimension=0, tiled=True),
        lax.psum_scatter(value_w_grad, "seq", scatter_dimension=0, tiled=True),
        lax.psum_scatter(out_w_grad, "seq", scatter_dimension=0, tiled=True),
        lax.psum_scatter(gate_w_grad, "seq", scatter_dimension=0, tiled=True),
        lax.psum_scatter(up_w_grad, "seq", scatter_dimension=0, tiled=True),
        lax.psum_scatter(down_w_grad, "seq", scatter_dimension=0, tiled=True),
    )
    query_share, key_share, value_share, out_share, gate_share, up_share, down_share = (
        lax.psum(query_share.astype(jnp.bfloat16), "slot").astype(jnp.float32),
        lax.psum(key_share.astype(jnp.bfloat16), "slot").astype(jnp.float32),
        lax.psum(value_share.astype(jnp.bfloat16), "slot").astype(jnp.float32),
        lax.psum(out_share.astype(jnp.bfloat16), "slot").astype(jnp.float32),
        lax.psum(gate_share.astype(jnp.bfloat16), "slot").astype(jnp.float32),
        lax.psum(up_share.astype(jnp.bfloat16), "slot").astype(jnp.float32),
        lax.psum(down_share.astype(jnp.bfloat16), "slot").astype(jnp.float32),
    )
    return (
        mixed,
        input_grad,
        query_share,
        key_share,
        value_share,
        out_share,
        gate_share,
        up_share,
        down_share,
        attn_gain_grad,
        query_gain_grad,
        key_gain_grad,
        ffn_gain_grad,
    )


def solution(mesh):
    in_specs = (
        P("slot", "seq", None),
        P("slot"),
        P("seq", None),
        P("seq", None),
        P("seq", None),
        P("seq", None),
        P("seq", None),
        P("seq", None),
        P("seq", None),
        P(),
        P(),
        P(),
        P(),
        P("slot", "seq", None),
    )
    out_specs = (
        P("slot", "seq", None),
        P("slot", "seq", None),
        P("seq", None),
        P("seq", None),
        P("seq", None),
        P("seq", None),
        P("seq", None),
        P("seq", None),
        P("seq", None),
        P(),
        P(),
        P(),
        P(),
    )
    return jax.shard_map(body, mesh=mesh, in_specs=in_specs, out_specs=out_specs, check_vma=False)
```

profile of v0, /device:TPU:0, one launch (start us, length us, event | category | flops | bytes accessed | tf_op | source)
XLA Modules:
  0.0 1224.9 jit_solution(1743439659193443792)
XLA Ops:
  10.6 25.6 %all-gather.10.cloned.1.call-done = bf16[1024,512]{1,0:T(8,128)(2,1)} async-done(((bf16[128,512]{1,0:T(8,128)(2,1)}), bf16[1024,512]{1,0:T(8,128)(2,1)}) %all-gather.10.cloned.1.call-update) | async-done | bytes 1048592 | tf_op jit(solution)/shard_map/all_gather | solution.py:92
  36.2 2.3 convolution_convert_fusion.1
  38.8 22.8 %all-gather.14.cloned.1.call-done = bf16[1024,512]{1,0:T(8,128)(2,1)} async-done(((bf16[128,512]{1,0:T(8,128)(2,1)}), bf16[1024,512]{1,0:T(8,128)(2,1)}) %all-gather.14.cloned.1.call-update) | async-done | bytes 1048592 | tf_op jit(solution)/shard_map/all_gather | solution.py:91
  69.4 22.0 %all-gather.18.cloned.1.call-done = bf16[1024,1024]{1,0:T(8,128)(2,1)} async-done(((bf16[128,1024]{1,0:T(8,128)(2,1)}), bf16[1024,1024]{1,0:T(8,128)(2,1)}) %all-gather.18.cloned.1.call-update) | async-done | bytes 2097168 | tf_op jit(solution)/shard_map/all_gather | solution.py:90
  91.4 2.9 copy.38
  94.2 23.0 %all-gather.12.cloned.1.call-done = bf16[1024,512]{1,0:T(8,128)(2,1)} async-done(((bf16[128,512]{1,0:T(8,128)(2,1)}), bf16[1024,512]{1,0:T(8,128)(2,1)}) %all-gather.12.cloned.1.call-update) | async-done | bytes 1048592 | tf_op jit(solution)/shard_map/all_gather | solution.py:128
  117.2 2.3 copy.36
  122.1 21.0 %all-gather.16.cloned.1.call-done = bf16[1024,512]{0,1:T(8,128)(2,1)} async-done(((bf16[128,512]{0,1:T(8,128)(2,1)}), bf16[1024,512]{0,1:T(8,128)(2,1)}) %all-gather.16.cloned.1.call-update) | async-done | bytes 1048592 | tf_op jit(solution)/shard_map/all_gather | solution.py:127
  143.1 2.7 fusion.5
  145.9 2.2 fusion.6
  149.2 2.7 fusion.84
  151.9 20.9 %all-gather.20.cloned.1.call-done = bf16[1024,1024]{1,0:T(8,128)(2,1)} async-done(((bf16[128,1024]{1,0:T(8,128)(2,1)}), bf16[1024,1024]{1,0:T(8,128)(2,1)}) %all-gather.20.cloned.1.call-update) | async-done | bytes 2097168 | tf_op jit(solution)/shard_map/all_gather | solution.py:93
  172.8 2.5 multiply_reduce_fusion.4
  175.4 58.1 %all-gather.24.cloned.1.call-done = bf16[1024,4608]{1,0:T(8,128)(2,1)} async-done(((bf16[128,4608]{1,0:T(8,128)(2,1)}), bf16[1024,4608]{1,0:T(8,128)(2,1)}) %all-gather.24.cloned.1.call-update) | async-done | bytes 9437200 | tf_op jit(solution)/shard_map/all_gather | solution.py:95
  233.5 6.5 fusion.86
  240.0 54.2 %all-gather.22.cloned.1.call-done = bf16[1024,4608]{1,0:T(8,128)(2,1)} async-done(((bf16[128,4608]{1,0:T(8,128)(2,1)}), bf16[1024,4608]{1,0:T(8,128)(2,1)}) %all-gather.22.cloned.1.call-update) | async-done | bytes 9437200 | tf_op jit(solution)/shard_map/all_gather | solution.py:94
  294.3 6.5 fusion.85
  300.8 54.3 %all-gather.26.cloned.1.call-done = bf16[1024,4608]{1,0:T(8,128)(2,1)} async-done(((bf16[128,4608]{1,0:T(8,128)(2,1)}), bf16[1024,4608]{1,0:T(8,128)(2,1)}) %all-gather.26.cloned.1.call-update) | async-done | bytes 9437200 | tf_op jit(solution)/shard_map/all_gather | solution.py:96
  355.0 8.4 multiply_convert_fusion
  363.4 3.1 fusion.87
  366.6 7.7 multiply_reduce_fusion
  376.2 8.3 fusion.9
  384.5 5.7 fusion.1
  390.2 2.0 copy-done.2
  393.6 2.5 pad_maximum_fusion
  397.0 2.7 fusion.59
  399.8 3.3 convolution_multiply_fusion
  404.4 2.8 fusion.56
  407.2 40.4 %reduce-scatter.9.cloned.1.call-done = f32[128,1024]{0,1:T(8,128)} async-done(((f32[1024,1024]{0,1:T(8,128)}), f32[128,1024]{0,1:T(8,128)}) %reduce-scatter.9.cloned.1.call-update) | async-done | bytes 524304 | tf_op jit(solution)/shard_map/reduce_scatter | solution.py:229
  447.6 2.8 fusion.66
  455.1 10.2 fusion.62
  466.6 8.4 fusion.90
  476.2 8.0 fusion.89
  484.4 18.4 %reduce-scatter.17.cloned.1.call-done = f32[128,1024]{1,0:T(8,128)} async-done(((f32[1024,1024]{1,0:T(8,128)}), f32[128,1024]{1,0:T(8,128)}) %reduce-scatter.17.cloned.1.call-update) | async-done | bytes 524304 | tf_op jit(solution)/shard_map/reduce_scatter | solution.py:264
  504.5 52.8 %reduce-scatter.11.cloned.1.call-done = f32[128,1024]{1,0:T(8,128)} async-done(((f32[1024,1024]{1,0:T(8,128)}), f32[128,1024]{1,0:T(8,128)}) %reduce-scatter.11.cloned.1.call-update) | async-done | bytes 524304 | tf_op jit(solution)/shard_map/reduce_scatter | solution.py:261
  559.1 43.7 %reduce-scatter.15.cloned.1.call-done = f32[128,512]{1,0:T(8,128)} async-done(((f32[1024,512]{1,0:T(8,128)}), f32[128,512]{1,0:T(8,128)}) %reduce-scatter.15.cloned.1.call-update) | async-done | bytes 262160 | tf_op jit(solution)/shard_map/reduce_scatter | solution.py:263
  604.4 43.3 %reduce-scatter.13.cloned.1.call-done = f32[128,512]{1,0:T(8,128)} async-done(((f32[1024,512]{1,0:T(8,128)}), f32[128,512]{1,0:T(8,128)}) %reduce-scatter.13.cloned.1.call-update) | async-done | bytes 262160 | tf_op jit(solution)/shard_map/reduce_scatter | solution.py:262
  649.3 128.4 %reduce-scatter.23.cloned.1.call-done = f32[128,4608]{1,0:T(8,128)} async-done(((f32[1024,4608]{1,0:T(8,128)}), f32[128,4608]{1,0:T(8,128)}) %reduce-scatter.23.cloned.1.call-update) | async-done | bytes 2359312 | tf_op jit(solution)/shard_map/reduce_scatter | solution.py:267
  777.7 2.8 convert_element_type.192
  780.5 127.2 %reduce-scatter.21.cloned.1.call-done = f32[128,4608]{1,0:T(8,128)} async-done(((f32[1024,4608]{1,0:T(8,128)}), f32[128,4608]{1,0:T(8,128)}) %reduce-scatter.21.cloned.1.call-update) | async-done | bytes 2359312 | tf_op jit(solution)/shard_map/reduce_scatter | solution.py:266
  907.8 2.8 convert_element_type.190
  910.6 127.2 %reduce-scatter.19.cloned.1.call-done = f32[128,4608]{1,0:T(8,128)} async-done(((f32[1024,4608]{1,0:T(8,128)}), f32[128,4608]{1,0:T(8,128)}) %reduce-scatter.19.cloned.1.call-update) | async-done | bytes 2359312 | tf_op jit(solution)/shard_map/reduce_scatter | solution.py:265
  1037.8 2.8 convert_element_type.188
  1042.5 8.0 fusion.21
  1051.6 45.7 %all-reduce = (f32[1024]{0:T(1024)}, f32[64]{0:T(128)}, f32[64]{0:T(128)}, f32[1024]{0:T(1024)}) all-reduce(f32[1024]{0:T(1024)S(1)} %get-tuple-element.17, f32[64]{0:T(128)} %get-tuple-element.13, f32[64]{0:T(128)S(1)} %copy-done.45, f32[1024]{0:T(1024)S(1)} %copy-done.37), channel_id=1, replica_groups=mesh['seq'=8,'slot'=4] {'seq','slot'}, use_global_device_ids=true, to_apply=%region_27.28 | all-reduce | flops 2176 | bytes 17408 | tf_op jit(solution)/shard_map/psum | solution.py:251
  1098.3 106.1 %all-reduce.4.cloned.1.call-done = (bf16[128,1024]{1,0:T(8,128)(2,1)}, bf16[128,512]{1,0:T(8,128)(2,1)}, bf16[128,512]{1,0:T(8,128)(2,1)}, bf16[128,1024]{1,0:T(...) async-done(((bf16[128,1024]{1,0:T(8,128)(2,1)}, bf16[128,512]{1,0:T(8,128)(2,1)}, bf16[128,512]{1,0:T(8,128)(2,1)}, ...) | async-done | bytes 4325392 | tf_op jit(solution)/shard_map/psum | solution.py:270
  1204.3 1.9 convert_element_type.181
  1211.4 2.9 convert_element_type.189
  (184 shorter events, 46.2 us)
Async XLA Ops:
  7.2 55.9 %copy-start.3 = (bf16[1,128,1024]{2,1,0:T(8,128)(2,1)S(1)}, bf16[1,128,1024]{2,1,0:T(8,128)(2,1)}, u32[]{:S(2)}) copy-start(bf16[1,128,1024]{2,1,0:T(8,128)(2,1)} %param.14) | copy-start | bytes 786436
  7.2 55.9 %copy-start.29 = (f32[1024]{0:T(1024)S(1)}, f32[1024]{0:T(1024)}, u32[]{:S(2)}) copy-start(f32[1024]{0:T(1024)} %param.23) | copy-start | bytes 12292
  7.2 56.4 %copy-start.38 = (f32[64]{0:T(128)S(1)}, f32[64]{0:T(128)}, u32[]{:S(2)}) copy-start(f32[64]{0:T(128)} %param.25) | copy-start | bytes 772
  7.2 28.9 %all-gather.10.cloned.1.call-start = ((), (), s32[]{:S(2)}) async-start(), calls=%async_computation.8 | async-start | bytes 1179648 | tf_op jit(solution)/shard_map/all_gather | solution.py:92
  7.9 53.6 %all-gather.14.cloned.1.call-start = ((), (), s32[]{:S(2)}) async-start(), calls=%async_computation.10 | async-start | bytes 1179648 | tf_op jit(solution)/shard_map/all_gather | solution.py:91
  8.7 82.7 %all-gather.18.cloned.1.call-start = ((), (), s32[]{:S(2)}) async-start(), calls=%async_computation.12 | async-start | bytes 2359296 | tf_op jit(solution)/shard_map/all_gather | solution.py:90
  9.4 107.8 %all-gather.12.cloned.1.call-start = ((), (), s32[]{:S(2)}) async-start(), calls=%async_computation.9 | async-start | bytes 1179648 | tf_op jit(solution)/shard_map/all_gather | solution.py:128
  10.6 108.9 %copy-start.34 = (f32[128]{0:T(128)}, f32[128]{0:T(128)S(1)}, u32[]{:S(2)}) copy-start(f32[128]{0:T(128)S(1)} %add_rsqrt_fusion.3) | copy-start | bytes 1540
  38.5 104.6 %all-gather.16.cloned.1.call-start = ((), (), s32[]{:S(2)}) async-start(), calls=%async_computation.11 | async-start | bytes 1179648 | tf_op jit(solution)/shard_map/all_gather | solution.py:127
  38.8 29.2 %copy-start.25 = (f32[128,64]{0,1:T(8,128)}, f32[128,64]{0,1:T(8,128)S(1)}, u32[]{:S(2)}) copy-start(f32[128,64]{0,1:T(8,128)S(1)} %get-tuple-element.59) | copy-start | bytes 98308
  38.8 29.2 %copy-start.27 = (f32[128,64]{0,1:T(8,128)}, f32[128,64]{0,1:T(8,128)S(1)}, u32[]{:S(2)}) copy-start(f32[128,64]{0,1:T(8,128)S(1)} %get-tuple-element.60) | copy-start | bytes 98308
  65.1 107.7 %all-gather.20.cloned.1.call-start = ((), (), s32[]{:S(2)}) async-start(), calls=%async_computation.13 | async-start | bytes 2359296 | tf_op jit(solution)/shard_map/all_gather | solution.py:93
  65.7 167.9 %all-gather.24.cloned.1.call-start = ((), (), s32[]{:S(2)}) async-start(), calls=%async_computation.15 | async-start | bytes 10616832 | tf_op jit(solution)/shard_map/all_gather | solution.py:95
  66.4 227.8 %all-gather.22.cloned.1.call-start = ((), (), s32[]{:S(2)}) async-start(), calls=%async_computation.14 | async-start | bytes 10616832 | tf_op jit(solution)/shard_map/all_gather | solution.py:94
  67.2 287.9 %all-gather.26.cloned.1.call-start = ((), (), s32[]{:S(2)}) async-start(), calls=%async_computation.16 | async-start | bytes 10616832 | tf_op jit(solution)/shard_map/all_gather | solution.py:96
  67.9 379.7 %reduce-scatter.9.cloned.1.call-start = ((), (), s32[]{:S(2)}) async-start(), calls=%async_computation.17 | async-start | bytes 4718592 | tf_op jit(solution)/shard_map/reduce_scatter | solution.py:229
  148.0 3.9 copy-start.41
  149.2 26.1 %copy-start.30 = (f32[1024]{0:T(1024)S(1)}, f32[1024]{0:T(1024)}, u32[]{:S(2)}) copy-start(f32[1024]{0:T(1024)} %param.26) | copy-start | bytes 12292
  151.9 23.4 %copy-start.23 = (bf16[128,8,2,64]{0,3,2,1:T(8,128)(2,1)}, bf16[128,8,2,64]{0,3,2,1:T(8,128)(2,1)S(1)}, u32[]{:S(2)}) copy-start(bf16[128,8,2,64]{0,3,2,1:T(8,128)(2,1)S(1)} %get-tuple-element.53) | copy-start | bytes 786436
  240.0 115.0 %copy-start.20 = (bf16[1,128,1024]{2,1,0:T(8,128)(2,1)S(1)}, bf16[1,128,1024]{2,1,0:T(8,128)(2,1)}, u32[]{:S(2)}) copy-start(bf16[1,128,1024]{2,1,0:T(8,128)(2,1)} %param.27) | copy-start | bytes 786436
  240.0 115.0 %copy-start.43 = (pred[128]{0:T(512)(128)(4,1)S(1)}, pred[128]{0:T(512)(128)(4,1)}, u32[]{:S(2)}) copy-start(pred[128]{0:T(512)(128)(4,1)} %broadcast_compare_fusion) | copy-start | bytes 388
  355.0 8.4 copy-start
  366.5 7.7 copy-start.31
  366.6 7.9 copy-start.5
  376.2 8.3 copy-start.22
  396.1 3.7 copy-start.6
  396.1 106.6 %reduce-scatter.17.cloned.1.call-start = ((), (), s32[]{:S(2)}) async-start(), calls=%async_computation.21 | async-start | bytes 4718592 | tf_op jit(solution)/shard_map/reduce_scatter | solution.py:264
  399.8 3.4 copy-start.28
  399.8 3.5 copy-start.26
  399.8 3.5 copy-start.40
  399.8 157.5 %reduce-scatter.11.cloned.1.call-start = ((), (), s32[]{:S(2)}) async-start(), calls=%async_computation.18 | async-start | bytes 4718592 | tf_op jit(solution)/shard_map/reduce_scatter | solution.py:261
  407.2 44.5 %copy-start.8 = (f32[128,8,64]{0,2,1:T(8,128)S(1)}, f32[128,8,64]{0,2,1:T(8,128)}, u32[]{:S(2)}) copy-start(f32[128,8,64]{0,2,1:T(8,128)} %copy-done.7) | copy-start | bytes 786436
  407.2 44.5 %copy-start.39 = (f32[64]{0:T(128)S(1)}, f32[64]{0:T(128)}, u32[]{:S(2)}) copy-start(f32[64]{0:T(128)} %param.25) | copy-start | bytes 772
  407.2 46.0 %copy-start.36 = (f32[128]{0:T(128)S(1)}, f32[128]{0:T(128)}, u32[]{:S(2)}) copy-start(f32[128]{0:T(128)} %copy-done.34) | copy-start | bytes 1540
  407.2 195.6 %reduce-scatter.15.cloned.1.call-start = ((), (), s32[]{:S(2)}) async-start(), calls=%async_computation.20 | async-start | bytes 2359296 | tf_op jit(solution)/shard_map/reduce_scatter | solution.py:263
  447.6 4.0 slice-start
  450.5 4.6 copy-start.9
  450.5 197.2 %reduce-scatter.13.cloned.1.call-start = ((), (), s32[]{:S(2)}) async-start(), calls=%async_computation.19 | async-start | bytes 2359296 | tf_op jit(solution)/shard_map/reduce_scatter | solution.py:262
  455.0 322.7 %reduce-scatter.23.cloned.1.call-start = ((), (), s32[]{:S(2)}) async-start(), calls=%async_computation.24 | async-start | bytes 21233664 | tf_op jit(solution)/shard_map/reduce_scatter | solution.py:267
  465.3 442.5 %reduce-scatter.21.cloned.1.call-start = ((), (), s32[]{:S(2)}) async-start(), calls=%async_computation.23 | async-start | bytes 21233664 | tf_op jit(solution)/shard_map/reduce_scatter | solution.py:266
  475.0 562.8 %reduce-scatter.19.cloned.1.call-start = ((), (), s32[]{:S(2)}) async-start(), calls=%async_computation.22 | async-start | bytes 21233664 | tf_op jit(solution)/shard_map/reduce_scatter | solution.py:265
  484.3 720.0 %all-reduce.4.cloned.1.call-start = ((), (), s32[]{:S(2)}) async-start(), calls=%async_computation.25 | async-start | bytes 8650752 | tf_op jit(solution)/shard_map/psum | solution.py:270
  910.6 130.1 %copy-start.4 = (bf16[1024,1024]{1,0:T(8,128)(2,1)S(1)}, bf16[1024,1024]{1,0:T(8,128)(2,1)}, u32[]{:S(2)}) copy-start(bf16[1024,1024]{1,0:T(8,128)(2,1)} %all-gather.18.cloned.1.call-done) | copy-start | bytes 6291460
  1042.5 8.0 copy-start.15
  1042.5 8.5 copy-start.14
  1042.5 8.5 copy-start.17
  1204.3 10.0 copy-start.19
  1207.8 8.1 copy-start.18
  (17 other events, 34.6 us)
Sparse Core Ops, SparseCore 0:
  9.9 26.1 all-gather.9
  38.0 23.4 all-gather.13
  63.5 27.8 all-gather.17
  93.7 23.4 all-gather.11
  119.5 23.5 all-gather.15
  144.9 27.8 all-gather.19
  174.7 58.8 all-gather.23
  235.4 58.8 all-gather.21
  296.2 58.8 all-gather.25
  396.2 51.3 reduce-scatter.8
  451.4 51.3 reduce-scatter.16
  505.9 51.3 reduce-scatter.10
  561.5 41.2 reduce-scatter.14
  606.5 41.1 reduce-scatter.12
  651.6 126.0 reduce-scatter.22
  781.7 126.0 reduce-scatter.20
  911.7 126.0 reduce-scatter.18
  1042.0 162.2 all-reduce.3
where the time goes:
time: 1230 us; the launch traced here: 1220 us
  waiting for transfers between devices  994 us (81%)
  matrix products  110 us (9%)
  blocking collectives  45.7 us (4%)
  other arithmetic  43.7 us (4%)
  between operations  16.1 us (1%)
  local copies, waits for them, and re-layouts  14 us (1%)
    reduce_scatter x1, waiting for transfers between devices, body(): lax.psum_scatter(down_w_grad, 'seq', scatter_dimension=0, tiled=True)  128 us
    reduce_scatter x1, waiting for transfers between devices, body(): lax.psum_scatter(up_w_grad, 'seq', scatter_dimension=0, tiled=True)  127 us
    reduce_scatter x1, waiting for transfers between devices, body(): lax.psum_scatter(gate_w_grad, 'seq', scatter_dimension=0, tiled=True)  127 us
    psum x1, waiting for transfers between devices, body(): lax.psum(query_share.astype(jnp.bfloat16), 'slot').astype(jnp.float32)  106 us
    all_gather x1, waiting for transfers between devices, body(): lax.all_gather(up_weight, 'seq', axis=0, tiled=True)  58.1 us
    all_gather x1, waiting for transfers between devices, body(): lax.all_gather(down_weight, 'seq', axis=0, tiled=True)  54.3 us
    all_gather x1, waiting for transfers between devices, body(): lax.all_gather(gate_weight, 'seq', axis=0, tiled=True)  54.2 us
    reduce_scatter x1, waiting for transfers between devices, body(): lax.psum_scatter(query_w_grad, 'seq', scatter_dimension=0, tiled=True)  52.8 us
  transfers between devices with their start and end apart: 18, of which 18 were waited for; matrix products, arithmetic and copies ran while one was open for 9% of the time, Pallas kernels for 0%

commit v1 on v0

--- a/solution.py
+++ b/solution.py
@@ -1,6 +1,10 @@
+import functools
+
 import jax
 import jax.numpy as jnp
 from jax import lax
+from jax.experimental import pallas as pl
+from jax.experimental.pallas import tpu as pltpu
 from jax.sharding import PartitionSpec as P
 
 HEADS = 16
@@ -60,7 +64,7 @@
     )
 
 
-def body(
+def general_body(
     tokens,
     lengths,
     query_weight,
@@ -292,6 +296,416 @@
     )
 
 
+SLOTS_BY_HEADS = 4
+LANES = 2 * HEAD_DIM
+VMEM_LIMIT = 60 * 1024 * 1024
+
+
+def dot_nn(left, right):
+    return lax.dot_general(left, right, (((1,), (0,)), ((), ())), preferred_element_type=jnp.float32)
+
+
+def dot_nt(left, right):
+    return lax.dot_general(left, right, (((1,), (1,)), ((), ())), preferred_element_type=jnp.float32)
+
+
+def dot_tn(left, right):
+    return lax.dot_general(left, right, (((0,), (0,)), ((), ())), preferred_element_type=jnp.float32)
+
+
+def lane_is_low(shape):
+    return lax.broadcasted_iota(jnp.int32, shape, len(shape) - 1) < HEAD_DIM
+
+
+def pair_mean(values):
+    low = lane_is_low(values.shape)
+    first = jnp.sum(jnp.where(low, values, 0.0), axis=-1, keepdims=True)
+    second = jnp.sum(jnp.where(low, 0.0, values), axis=-1, keepdims=True)
+    return jnp.where(low, first, second) * (1.0 / HEAD_DIM)
+
+
+def pair_turn(values, cosine, sine_signed):
+    lane = lax.broadcasted_iota(jnp.int32, values.shape, 1)
+    near = lax.rem(lane, HEAD_DIM) < HEAD_DIM // 2
+    half = HEAD_DIM // 2
+    turned = jnp.where(near, pltpu.roll(values, LANES - half, 1), pltpu.roll(values, half, 1))
+    return values * cosine + turned * sine_signed
+
+
+def call(kernel, out_shape, scratch_shapes=(), flops=0, moved=0):
+    vmem = pl.BlockSpec(memory_space=pltpu.VMEM)
+
+    def apply(*operands, smem=0):
+        in_specs = [pl.BlockSpec(memory_space=pltpu.SMEM)] * smem + [vmem] * (len(operands) - smem)
+        return pl.pallas_call(
+            kernel,
+            out_shape=out_shape,
+            in_specs=in_specs,
+            out_specs=jax.tree.map(lambda _: vmem, out_shape),
+            scratch_shapes=scratch_shapes,
+            compiler_params=pltpu.CompilerParams(vmem_limit_bytes=VMEM_LIMIT),
+            cost_estimate=pl.CostEstimate(flops=flops, bytes_accessed=moved, transcendentals=0),
+        )(*operands)
+
+    return apply
+
+
+ROW_BLOCK = 256
+
+
+def attention_forward_kernel(
+    length_ref, x_ref, weight_ref, gain_ref, q_gain_ref, k_gain_ref, cos_q_ref, sin_q_ref, cos_k_ref, sin_k_ref,
+    normed_ref, q_proj_ref, kv_proj_ref, q_low_ref, k_pair_ref, v_pair_ref, attn_ref, attn_low_ref, weight_inv_ref,
+):
+    total = x_ref.shape[0]
+    length = length_ref[0]
+    low = lane_is_low((ROW_BLOCK, LANES))
+    for start in range(0, total, ROW_BLOCK):
+        rows = pl.ds(start, ROW_BLOCK)
+        x = x_ref[rows, :].astype(jnp.float32)
+        factor = lax.rsqrt(jnp.mean(x * x, axis=-1, keepdims=True) + EPSILON)
+        normed = (x * factor * gain_ref[...]).astype(jnp.bfloat16)
+        normed_ref[rows, :] = normed
+        proj = dot_nn(normed, weight_ref[...])
+        q_proj = proj[:, :LANES]
+        kv_proj = proj[:, LANES:]
+        q_proj_ref[rows, :] = q_proj
+        kv_proj_ref[rows, :] = kv_proj
+        q_factor = lax.rsqrt(pair_mean(q_proj * q_proj) + EPSILON)
+        q_low_ref[rows, :] = pair_turn(
+            q_proj * q_factor * q_gain_ref[...], cos_q_ref[rows, :], sin_q_ref[rows, :]
+        ).astype(jnp.bfloat16)
+        k_factor = jnp.where(low, lax.rsqrt(pair_mean(kv_proj * kv_proj) + EPSILON), 1.0)
+        kv = pair_turn(kv_proj * k_factor * k_gain_ref[...], cos_k_ref[rows, :], sin_k_ref[rows, :])
+        swapped = pltpu.roll(kv, HEAD_DIM, 1)
+        k_pair_ref[rows, :] = jnp.where(low, kv, swapped).astype(jnp.bfloat16)
+        v_pair_ref[rows, :] = jnp.where(low, swapped, kv).astype(jnp.bfloat16)
+
+    scale = HEAD_DIM ** (-0.5)
+    for start in range(0, total, ROW_BLOCK):
+        rows = pl.ds(start, ROW_BLOCK)
+        q = q_low_ref[rows, :]
+        zero = jnp.zeros_like(q)
+        heads = (jnp.where(low, q, zero), jnp.where(low, zero, q))
+        results = []
+        for q_head in heads:
+            weight_sum = jnp.zeros((ROW_BLOCK, 1), jnp.float32)
+            summed = jnp.zeros((ROW_BLOCK, LANES), jnp.float32)
+            if start > 0:
+                past = pl.ds(0, start)
+                exp_vals = jnp.exp(dot_nt(q_head, k_pair_ref[past, :]) * scale)
+                weight_sum += jnp.sum(exp_vals, axis=-1, keepdims=True)
+                summed += dot_nn(exp_vals.astype(jnp.bfloat16), v_pair_ref[past, :])
+            scores = dot_nt(q_head, k_pair_ref[rows, :]) * scale
+            query = lax.broadcasted_iota(jnp.int32, scores.shape, 0)
+            key = lax.broadcasted_iota(jnp.int32, scores.shape, 1)
+            allowed = (key <= query) & (key + start < length)
+            exp_vals = jnp.where(allowed, jnp.exp(scores), 0.0)
+            weight_sum += jnp.sum(exp_vals, axis=-1, keepdims=True)
+            summed += dot_nn(exp_vals.astype(jnp.bfloat16), v_pair_ref[rows, :])
+            inverse = 1.0 / weight_sum
+            results.append((summed * inverse, inverse))
+        attn = jnp.where(low, results[0][0], results[1][0])
+        attn_ref[rows, :] = attn
+        attn_low_ref[rows, :] = attn.astype(jnp.bfloat16)
+        weight_inv_ref[rows, :] = jnp.where(low, results[0][1], results[1][1])
+
+
+def attention_backward_kernel(
+    length_ref, dattn_ref, normed_ref, weight_ref, q_gain_ref, k_gain_ref, cos_q_ref, sin_q_ref, cos_k_ref, sin_k_ref,
+    q_proj_ref, kv_proj_ref, q_low_ref, k_pair_ref, v_pair_ref, attn_ref, weight_inv_ref,
+    dnormed_ref, dproj_ref, terms_ref, dq_acc, dk_acc, dv_acc,
+):
+    total = dattn_ref.shape[0]
+    length = length_ref[0]
+    low = lane_is_low((ROW_BLOCK, LANES))
+    scale = HEAD_DIM ** (-0.5)
+    dk_acc[...] = jnp.zeros_like(dk_acc)
+    dv_acc[...] = jnp.zeros_like(dv_acc)
+    for start in range(0, total, ROW_BLOCK):
+        rows = pl.ds(start, ROW_BLOCK)
+        q = q_low_ref[rows, :]
+        dattn = dattn_ref[rows, :]
+        zero = jnp.zeros_like(q)
+        inner = dattn.astype(jnp.float32) * attn_ref[rows, :]
+        inverses = weight_inv_ref[rows, :]
+        dq_heads = []
+        for head in range(2):
+            mine = low if head == 0 else jnp.logical_not(low)
+            q_head = jnp.where(mine, q, zero)
+            dattn_head = jnp.where(mine, dattn, zero)
+            delta = jnp.sum(jnp.where(mine, inner, 0.0), axis=-1, keepdims=True)
+            inverse = inverses[:, head * HEAD_DIM : head * HEAD_DIM + 1]
+            dq = jnp.zeros((ROW_BLOCK, LANES), jnp.float32)
+            spans = ([(0, start)] if start > 0 else []) + [(start, ROW_BLOCK)]
+            for key_start, key_count in spans:
+                keys = pl.ds(key_start, key_count)
+                k_pair = k_pair_ref[keys, :]
+                probs = jnp.exp(dot_nt(q_head, k_pair) * scale) * inverse
+                if key_start == start:
+                    query = lax.broadcasted_iota(jnp.int32, probs.shape, 0)
+                    key = lax.broadcasted_iota(jnp.int32, probs.shape, 1)
+                    allowed = (key <= query) & (key + start < length)
+                    probs = jnp.where(allowed, probs, 0.0)
+                dprobs = dot_nt(dattn_head, v_pair_ref[keys, :])
+                dscores = (probs * (dprobs - delta)).astype(jnp.bfloat16)
+                dq += dot_nn(dscores, k_pair)
+                dk_acc[keys, :] += dot_tn(dscores, q_head)
+                dv_acc[keys, :] += dot_tn(probs.astype(jnp.bfloat16), dattn_head)
+            dq_heads.append(dq)
+        dq_acc[rows, :] = jnp.where(low, dq_heads[0], dq_heads[1]) * scale
+
+    q_terms = jnp.zeros((1, LANES), jnp.float32)
+    k_terms = jnp.zeros((1, LANES), jnp.float32)
+    for start in range(0, total, ROW_BLOCK):
+        rows = pl.ds(start, ROW_BLOCK)
+        q_proj = q_proj_ref[rows, :]
+        upstream = pair_turn(dq_acc[rows, :], cos_q_ref[rows, :], -sin_q_ref[rows, :])
+        factor = lax.rsqrt(pair_mean(q_proj * q_proj) + EPSILON)
+        normal = q_proj * factor
+        weighted = upstream * q_gain_ref[...]
+        dq_proj = factor * (weighted - normal * pair_mean(weighted * normal))
+        q_terms += jnp.sum(upstream * normal, axis=0, keepdims=True)
+
+        dk = dk_acc[rows, :] * scale
+        dv = dv_acc[rows, :]
+        dk = dk + pltpu.roll(dk, HEAD_DIM, 1)
+        dv = dv + pltpu.roll(dv, HEAD_DIM, 1)
+        kv_proj = kv_proj_ref[rows, :]
+        upstream = pair_turn(jnp.where(low, dk, 0.0), cos_k_ref[rows, :], -sin_k_ref[rows, :])
+        factor = lax.rsqrt(pair_mean(kv_proj * kv_proj) + EPSILON)
+        normal = kv_proj * factor
+        weighted = upstream * k_gain_ref[...]
+        dk_proj = factor * (weighted - normal * pair_mean(weighted * normal))
+        k_terms += jnp.sum(upstream * normal, axis=0, keepdims=True)
+        dkv_proj = jnp.where(low, dk_proj, dv)
+        dproj = jnp.concatenate([dq_proj, dkv_proj], axis=1).astype(jnp.bfloat16)
+        dproj_ref[rows, :] = dproj
+        dnormed_ref[rows, :] = dot_nt(dproj, weight_ref[...]).astype(jnp.bfloat16)
+    terms_ref[0:1, :] = q_terms
+    terms_ref[1:2, :] = k_terms
+
+
+def feed_forward_kernel(
+    x_ref, attn_ref, out_weight_ref, gain_ref, gate_up_ref, down_ref, dout_ref,
+    residual_ref, normed_ref, hidden_ref, dgate_up_ref, dnormed_ref, mixed_ref,
+):
+    low = lane_is_low((x_ref.shape[0], LANES))
+    attn = jnp.concatenate([attn_ref[i] for i in range(attn_ref.shape[0])], axis=1)
+    residual = x_ref[...].astype(jnp.float32) + dot_nt(attn, out_weight_ref[...])
+    residual_ref[...] = residual
+    factor = lax.rsqrt(jnp.mean(residual * residual, axis=-1, keepdims=True) + EPSILON)
+    normed = (residual * factor * gain_ref[...]).astype(jnp.bfloat16)
+    normed_ref[...] = normed
+    both = dot_nn(normed, gate_up_ref[...])
+    dhidden = dot_nn(dout_ref[...], down_ref[...])
+    whole = (both.shape[1] - LANES) // 2
+    tail = both[:, 2 * whole :]
+    tail_swapped = pltpu.roll(tail, HEAD_DIM, 1)
+
+    def share(gate, up, upstream):
+        sigmoid = jax.nn.sigmoid(gate)
+        silu = gate * sigmoid
+        dgate = upstream * up * sigmoid * (1.0 + gate * (1.0 - sigmoid))
+        return silu * up, dgate, upstream * silu
+
+    hidden, dgate, dup = share(both[:, :whole], both[:, whole : 2 * whole], dhidden[:, :whole])
+    hidden_tail, dgate_tail, dup_tail = share(
+        jnp.where(low, tail, tail_swapped), jnp.where(low, tail_swapped, tail), dhidden[:, whole:]
+    )
+    hidden_low = jnp.concatenate([hidden, jnp.where(low, hidden_tail, 0.0)], axis=1).astype(jnp.bfloat16)
+    dgate_up = jnp.concatenate([dgate, dup, jnp.where(low, dgate_tail, dup_tail)], axis=1).astype(jnp.bfloat16)
+    hidden_ref[...] = hidden_low
+    dgate_up_ref[...] = dgate_up
+    dnormed_ref[...] = dot_nt(dgate_up, gate_up_ref[...]).astype(jnp.bfloat16)
+    mixed_ref[...] = dot_nt(hidden_low, down_ref[...]).astype(jnp.bfloat16)
+
+
+def rotary_pair_tables(total):
+    position = jnp.arange(total, dtype=jnp.int32)
+    cosine, sine = rotary_tables(position)
+    half = HEAD_DIM // 2
+    signed = jnp.concatenate([-sine[:, :half], sine[:, half:]], axis=1)
+    return (
+        jnp.concatenate([cosine, cosine], axis=1),
+        jnp.concatenate([signed, signed], axis=1),
+        jnp.concatenate([cosine, jnp.ones_like(cosine)], axis=1),
+        jnp.concatenate([signed, jnp.zeros_like(signed)], axis=1),
+    )
+
+
+def heads_body(
+    tokens, lengths, query_weight, key_weight, value_weight, out_weight, gate_weight, up_weight, down_weight,
+    attn_norm, query_norm, key_norm, ffn_norm, out_grad,
+):
+    count = KV_HEADS
+    tok_rows, width = tokens.shape[1:]
+    depth = query_weight.shape[0]
+    total = tok_rows * count
+    hidden_width = gate_weight.shape[1]
+    whole = hidden_width // count // LANES * LANES
+    rest = hidden_width // count - whole
+    length = lengths[0]
+    me = lax.axis_index("seq")
+    position = me * tok_rows + jnp.arange(tok_rows, dtype=jnp.int32)
+    row_valid = (position < length)[:, None]
+
+    def gather(block):
+        return lax.all_gather(block, "seq", axis=0, tiled=True)
+
+    def swap(blocks):
+        return lax.all_to_all(blocks, "seq", 0, 0, tiled=True)
+
+    def by_owner(weight):
+        return jnp.transpose(weight.reshape(depth, count, -1), (1, 0, 2))
+
+    def sum_swapped(partial):
+        return jnp.sum(swap(partial.reshape(count, tok_rows, width)).astype(jnp.float32), axis=0)
+
+    x_all = gather(tokens[0])
+    attn_weight = swap(
+        jnp.concatenate([by_owner(query_weight), by_owner(key_weight), by_owner(value_weight)], axis=2)
+    ).reshape(width, 2 * LANES)
+    cut = whole * count
+    ffn_weight = swap(
+        jnp.concatenate(
+            [
+                by_owner(gate_weight[:, :cut]),
+                by_owner(up_weight[:, :cut]),
+                by_owner(gate_weight[:, cut:]),
+                by_owner(up_weight[:, cut:]),
+                by_owner(down_weight[:, :cut]),
+                by_owner(down_weight[:, cut:]),
+            ],
+            axis=2,
+        )
+    ).reshape(width, -1)
+    gate_up = ffn_weight[:, : 2 * whole + 2 * rest]
+    down = jnp.concatenate([ffn_weight[:, 2 * whole + 2 * rest :], ffn_weight[:, -rest:]], axis=1)
+    out_full = gather(out_weight)
+    upstream = jnp.where(row_valid, out_grad[0].astype(jnp.float32), 0.0)
+    dout_all = gather(upstream.astype(jnp.bfloat16))
+    tables = rotary_pair_tables(total)
+    q_gain = jnp.concatenate([query_norm, query_norm])[None]
+    k_gain = jnp.concatenate([key_norm, jnp.ones_like(key_norm)])[None]
+
+    def array(kind, *shape):
+        return jax.ShapeDtypeStruct(shape, kind)
+
+    f32, bf16 = jnp.float32, jnp.bfloat16
+    normed, q_proj, kv_proj, q_low, k_pair, v_pair, attn, attn_low, weight_inv = call(
+        attention_forward_kernel,
+        (
+            array(bf16, total, width), array(f32, total, LANES), array(f32, total, LANES), array(bf16, total, LANES),
+            array(bf16, total, LANES), array(bf16, total, LANES), array(f32, total, LANES), array(bf16, total, LANES),
+            array(f32, total, LANES),
+        ),
+        flops=2_000_000_000,
+        moved=8_000_000,
+    )(lengths, x_all, attn_weight, attn_norm[None], q_gain, k_gain, *tables, smem=1)
+
+    attn_all = lax.all_gather(attn_low, "seq", axis=0)
+
+    blocks = total // ROW_BLOCK
+    units = whole + rest
+    row_spec = lambda size: pl.BlockSpec((ROW_BLOCK, size), lambda i: (i, 0))
+    full_spec = lambda *shape: pl.BlockSpec(shape, lambda i: (0,) * len(shape))
+    residual, normed_two, hidden, dgate_up, dnormed_two, mixed_part = pl.pallas_call(
+        feed_forward_kernel,
+        grid=(blocks,),
+        out_shape=(
+            array(f32, total, width), array(bf16, total, width), array(bf16, total, whole + LANES),
+            array(bf16, total, 2 * units), array(bf16, total, width), array(bf16, total, width),
+        ),
+        in_specs=[
+            row_spec(width),
+            pl.BlockSpec((count, ROW_BLOCK, LANES), lambda i: (0, i, 0)),
+            full_spec(width, width),
+            full_spec(1, width),
+            full_spec(width, 2 * units),
+            full_spec(width, whole + LANES),
+            row_spec(width),
+        ],
+        out_specs=(
+            row_spec(width), row_spec(width), row_spec(whole + LANES), row_spec(2 * units), row_spec(width),
+            row_spec(width),
+        ),
+        compiler_params=pltpu.CompilerParams(vmem_limit_bytes=VMEM_LIMIT),
+        cost_estimate=pl.CostEstimate(flops=9_000_000_000, bytes_accessed=25_000_000, transcendentals=0),
+    )(x_all, attn_all, out_full, ffn_norm[None], gate_up, down, dout_all)
+
+    my_rows = me * tok_rows
+    residual_mine = lax.dynamic_slice_in_dim(residual, my_rows, tok_rows, 0)
+    normed_two_grad = sum_swapped(dnormed_two)
+    factor_two = lax.rsqrt(jnp.mean(residual_mine * residual_mine, axis=-1, keepdims=True) + EPSILON)
+    residual_part, ffn_terms = rms_back(residual_mine, factor_two, ffn_norm, normed_two_grad)
+    residual_grad = upstream + residual_part
+    attn_out_low = residual_grad.astype(bf16)
+    dattn = jnp.dot(attn_out_low, out_full, preferred_element_type=f32).astype(bf16)
+    dattn = swap(jnp.transpose(dattn.reshape(tok_rows, count, LANES), (1, 0, 2))).reshape(total, LANES)
+    attn_out_all = gather(attn_out_low)
+
+    result = residual_mine + sum_swapped(mixed_part)
+    mixed = jnp.where(row_valid, result, 0.0).astype(bf16)[None]
+
+    dnormed, dproj, terms = call(
+        attention_backward_kernel,
+        (array(bf16, total, width), array(bf16, total, 2 * LANES), array(f32, 2, LANES)),
+        scratch_shapes=[pltpu.VMEM((total, LANES), f32)] * 3,
+        flops=3_000_000_000,
+        moved=10_000_000,
+    )(
+        lengths, dattn, normed, attn_weight, q_gain, k_gain, *tables, q_proj, kv_proj, q_low, k_pair, v_pair, attn,
+        weight_inv, smem=1,
+    )
+    inputs = tokens[0].astype(f32)
+    factor_one = lax.rsqrt(jnp.mean(inputs * inputs, axis=-1, keepdims=True) + EPSILON)
+    input_part, attn_terms = rms_back(inputs, factor_one, attn_norm, sum_swapped(dnormed))
+    input_grad = (residual_grad + input_part).astype(bf16)[None]
+
+    gate_up_grad = dot_tn(normed_two, dgate_up).astype(bf16)
+    down_grad = dot_tn(dout_all, hidden).astype(bf16)[:, :units]
+    out_grad_cols = dot_tn(attn_out_all, attn_low).astype(bf16)
+    proj_grad = dot_tn(normed, dproj).astype(bf16)
+
+    def to_rows(grad):
+        swapped = swap(grad.reshape(count, depth, -1))
+        return lax.psum(swapped, "slot").astype(f32)
+
+    def spread(part):
+        return jnp.transpose(part, (1, 0, 2)).reshape(depth, -1)
+
+    gate_up_rows = to_rows(gate_up_grad)
+    down_rows = to_rows(down_grad)
+    attn_rows = to_rows(jnp.concatenate([proj_grad, out_grad_cols], axis=1))
+    gate_rows = jnp.concatenate(
+        [spread(gate_up_rows[..., :whole]), spread(gate_up_rows[..., 2 * whole : 2 * whole + rest])], axis=1
+    )
+    up_rows = jnp.concatenate(
+        [spread(gate_up_rows[..., whole : 2 * whole]), spread(gate_up_rows[..., 2 * whole + rest :])], axis=1
+    )
+    down_rows = jnp.concatenate([spread(down_rows[..., :whole]), spread(down_rows[..., whole:])], axis=1)
+    half = HEAD_DIM
+    query_rows = spread(attn_rows[..., :LANES])
+    key_rows = spread(attn_rows[..., LANES : LANES + half])
+    value_rows = spread(attn_rows[..., LANES + half : 2 * LANES])
+    out_rows = spread(attn_rows[..., 2 * LANES :])
+
+    attn_gain, query_gain, key_gain, ffn_gain = lax.psum(
+        (
+            jnp.sum(attn_terms, axis=0),
+            terms[0, :half] + terms[0, half:],
+            terms[1, :half],
+            jnp.sum(ffn_terms, axis=0),
+        ),
+        ("seq", "slot"),
+    )
+    return (
+        mixed, input_grad, query_rows, key_rows, value_rows, out_rows, gate_rows, up_rows, down_rows,
+        attn_gain, query_gain, key_gain, ffn_gain,
+    )
+
+
 def solution(mesh):
     in_specs = (
         P("slot", "seq", None),
@@ -324,4 +738,6 @@
         P(),
         P(),
     )
+    by_heads = mesh.shape["seq"] == KV_HEADS and mesh.shape["slot"] == SLOTS_BY_HEADS
+    body = heads_body if by_heads else general_body
     return jax.shard_map(body, mesh=mesh, in_specs=in_specs, out_specs=out_specs, check_vma=False)

time: 1230 us -> 527 us (0.43)
  waiting for transfers between devices: 994 us -> 199 us
  blocking collectives: 45.7 us -> 148 us
  matrix products: 110 us -> 15.4 us
  local copies, waits for them, and re-layouts: 14 us -> 59.6 us
  Pallas kernels: 0 us -> 39.5 us
  starting transfers between devices: 0.72 us -> 24.1 us
  other arithmetic: 43.7 us -> 23.9 us
    reduce_scatter x8 -> x0, waiting for transfers between devices: 581 us -> none  [the longest x1 128 us: body(): lax.psum_scatter(down_w_grad, 'seq', scatter_dimension=0, tiled=True)]
    all_gather x9 -> x5, waiting for transfers between devices: 302 us -> 42.4 us  [the longest x1 29.2 us: heads_body(): attn_all = lax.all_gather(attn_low, 'seq', axis=0)]
    all_to_all x0 -> x3, blocking collectives: none -> 102 us  [swap(): return lax.all_to_all(blocks, 'seq', 0, 0, tiled=True)]
    dot_general x27 -> x5, matrix products: 110 us -> 15.4 us  [the longest x4 15 us: dot_tn(): lax.dot_general(left, right, (((0,), (0,)), ((), ())), preferred_element_...]
    all_to_all x0 -> x6, waiting for transfers between devices: none -> 73.8 us  [swap(): return lax.all_to_all(blocks, 'seq', 0, 0, tiled=True)]
    pallas_call x0 -> x3, Pallas kernels: none -> 39.5 us  [the longest x2 22.3 us: apply(): pl.pallas_call(kernel, out_shape=out_shape, in_specs=in_specs, out_specs=...]
    convert_element_type x19 -> x2, other arithmetic: 31.2 us -> 4.21 us  [the longest x1 2.44 us: heads_body(): attn_out_low = residual_grad.astype(bf16)]
    psum x1, waiting for transfers between devices: 106 us -> 81.6 us  [to_rows(): return lax.psum(swapped, 'slot').astype(f32)]
  transfers between devices with their start and end apart: 18 -> 12, of which waited for: 18 -> 7; matrix products, arithmetic and copies ran while one was open for 9% -> 12% of each run, Pallas kernels for 0% -> 4%
where the time goes in v1:
time: 527 us; the launch traced here: 525 us
  waiting for transfers between devices  199 us (38%)
  blocking collectives  148 us (28%)
  local copies, waits for them, and re-layouts  59.6 us (11%)
  Pallas kernels  39.5 us (7%)
  starting transfers between devices  24.1 us (5%)
  other arithmetic  23.9 us (5%)
  matrix products  15.4 us (3%)
  between operations  15.3 us (3%)
    all_to_all x3, blocking collectives, swap(): return lax.all_to_all(blocks, 'seq', 0, 0, tiled=True)  102 us
    psum x1, waiting for transfers between devices, to_rows(): return lax.psum(swapped, 'slot').astype(f32)  81.6 us
    all_to_all x6, waiting for transfers between devices, swap(): return lax.all_to_all(blocks, 'seq', 0, 0, tiled=True)  73.8 us
    psum x1, blocking collectives, heads_body(): lax.psum((jnp.sum(attn_terms, axis=0), terms[0, :half] + terms[0, half:],...  46.6 us
    all_gather x1, waiting for transfers between devices, heads_body(): attn_all = lax.all_gather(attn_low, 'seq', axis=0)  29.2 us
    all_to_all x6, starting transfers between devices, swap(): return lax.all_to_all(blocks, 'seq', 0, 0, tiled=True)  23.6 us
    pallas_call x2, Pallas kernels, apply(): pl.pallas_call(kernel, out_shape=out_shape, in_specs=in_specs, out_specs=...  22.3 us
    pallas_call x1, Pallas kernels, heads_body(): pl.pallas_call(feed_forward_kernel, grid=(blocks,), out_shape=(array(f32,...  17.2 us
  transfers between devices with their start and end apart: 12, of which 7 were waited for; matrix products, arithmetic and copies ran while one was open for 12% of the time, Pallas kernels for 4%

profile of v1, /device:TPU:0, one launch (start us, length us, event | category | flops | bytes accessed | tf_op | source)
XLA Modules:
  0.0 525.0 jit_solution(13476325211682254045)
XLA Ops:
  8.6 1.8 fusion.15
  14.7 5.2 all-to-all-start
  21.8 3.1 fusion.18
  30.7 2.2 fusion.12
  32.9 13.1 %all-gather.14.cloned.1.call-done = bf16[1,1024,1024]{2,1,0:T(8,128)(2,1)} async-done(((bf16[1,128,1024]{2,1,0:T(8,128)(2,1)}), bf16[1,1024,1024]{2,1,0:T(8,128)(2,1)}) %all-gather.14.cloned.1.call-update) | async-done | bytes 2097168 | tf_op jit(solution)/shard_map/all_gather | solution.py:554
  46.0 7.3 %shard_map.237 = (bf16[1024,1024]{1,0:T(8,128)(2,1)}, f32[1024,128]{1,0:T(8,128)}, f32[1024,128]{1,0:T(8,128)}, bf16[1024,128]{1,0:T(8,128)(2,1)}, bf16[1024,128...) custom-call(s32[1]{0:T(128)} %copy.121.length_ref, ...), custom_call_target="tpu_custom_call" | custom-call | flops 2000000000 | bytes 8000000 | tf_op jit(solution)/shard_map/pallas_call | solution.py:340
  56.6 54.9 %all_to_all.45 = bf16[8,128,1728]{1,2,0:T(8,128)(2,1)} all-to-all(bf16[8,128,1728]{1,2,0:T(8,128)(2,1)} %constant_dynamic-update-slice_fusion), channel_id=1, replica_groups=mesh['seq'=8,'slot'=4] {'seq'}, dimensions={0} | all-to-all | bytes 7077888 | tf_op jit(solution)/shard_map/all_to_all | solution.py:557
  111.5 5.9 %copy.86 = bf16[8,128,1728]{2,1,0:T(8,128)(2,1)} copy(bf16[8,128,1728]{1,2,0:T(8,128)(2,1)} %all_to_all.45) | data formatting | bytes 7077888 | tf_op jit(solution)/shard_map/all_to_all | solution.py:557
  117.4 1.4 slice.93
  119.8 3.3 slice.92.gate_up_ref
  123.0 1.3 pad_maximum_fusion.3.down_ref
  124.3 29.2 %all-gather.16.cloned.1.call-done = bf16[8192,128]{1,0:T(8,128)(2,1)} async-done(((bf16[1024,128]{1,0:T(8,128)(2,1)}), bf16[8192,128]{1,0:T(8,128)(2,1)}) %all-gather.16.cloned.1.call-update) | async-done | bytes 2097168 | tf_op jit(solution)/shard_map/all_gather | solution.py:607
  153.6 17.2 %shard_map.238 = (f32[1024,1024]{1,0:T(8,128)}, bf16[1024,1024]{1,0:T(8,128)(2,1)}, bf16[1024,640]{1,0:T(8,128)(2,1)}, bf16[1024,1152]{1,0:T(8,128)(2,1)}, bf16[...) custom-call(bf16[1024,1024]{1,0:T(8,128)(2,1)} %bitcast.154, bf16[8,1024,128]{2,1,0:T(8,128)(2,1)} %bitcast.155, ...), custom_call_target="tpu_custom_call" | custom-call | flops 8999999488 | bytes 25000000 | tf_op jit(solution)/shard_map/pallas_call | solution.py:613
  170.8 30.9 %all_to_all.46 = bf16[8,128,1024]{2,1,0:T(8,128)(2,1)} all-to-all(bf16[8,128,1024]{2,1,0:T(8,128)(2,1)} %bitcast.137), channel_id=1, replica_groups=mesh['seq'=8,'slot'=4] {'seq'}, dimensions={0} | all-to-all | bytes 4194304 | tf_op jit(solution)/shard_map/all_to_all | solution.py:557
  201.7 3.6 all-to-all-start.2
  206.5 2.0 convert_reduce_fusion.1
  208.6 1.3 multiply_reduce_fusion
  209.9 22.0 %all-to-all-done.2 = bf16[8,128,1024]{2,1,0:T(8,128)(2,1)S(1)} async-done(((bf16[8,128,1024]{2,1,0:T(8,128)(2,1)}), bf16[8,128,1024]{2,1,0:T(8,128)(2,1)S(1)}, u32[]{:S(2)}, u32[]{:S(2)}) %all-to-all-start.2) | async-done | bytes 2097184 | tf_op jit(solution)/shard_map/all_to_all | solution.py:557
  232.3 2.4 fusion.19
  234.7 2.9 fusion.25
  238.9 3.6 all-to-all-start.8
  243.7 16.9 %all-to-all-done.8 = bf16[8,128,576]{1,2,0:T(8,128)(2,1)S(1)} async-done(((bf16[8,128,576]{1,2,0:T(8,128)(2,1)}), bf16[8,128,576]{1,2,0:T(8,128)(2,1)S(1)}, u32[]{:S(2)}, u32[]{:S(2)}) %all-to-all-start.8) | async-done | bytes 1179680 | tf_op jit(solution)/shard_map/all_to_all | solution.py:557
  260.5 3.4 all-to-all-start.4
  264.0 6.7 %convolution_convert_fusion = bf16[1024,1152]{1,0:T(8,128)(2,1)} fusion(bf16[1024,1024]{1,0:T(8,128)(2,1)} %get-tuple-element.45, bf16[1024,1152]{1,0:T(8,128)(2,1)} %get-tuple-element.46), kind=kOutput, calls=%fused_computation.3 | convolution fusion | flops 2417098752 | bytes 6815744 | tf_op jit(solution)/shard_map/dot_general | solution.py:313
  270.6 4.3 copy.89
  275.6 4.1 all-to-all-start.7
  280.0 15.0 %shard_map.239 = (bf16[1024,1024]{1,0:T(8,128)(2,1)}, bf16[1024,256]{1,0:T(8,128)(2,1)}, f32[2,128]{1,0:T(2,128)}) custom-call(s32[1]{0:T(128)} %copy.121.length_ref, bf16[1024,128]{1,0:T(8,128)(2,1)} %bitcast.150, bf16[1024,1024]{1,0:T(8,128)(2,1)} %get-tuple-element.35.normed_ref, bf16[1024,256]{1,0:T(8,128)(2,1)} %bitcast.7.weight_ref, ...), custom_call_target="tpu_custom_call" | custom-call | flops 3000000000 | bytes 10000000 | tf_op jit(solution)/shard_map/pallas_call | solution.py:340
  295.0 3.3 convolution_convert_fusion.1
  298.3 2.1 convolution_convert_fusion.2
  300.6 8.6 %all-to-all-done.7 = bf16[8,128,1152]{1,2,0:T(8,128)(2,1)S(1)} async-done(((bf16[8,128,1152]{1,2,0:T(8,128)(2,1)}), bf16[8,128,1152]{1,2,0:T(8,128)(2,1)S(1)}, u32[]{:S(2)}, u32[]{:S(2)}) %all-to-all-start.7) | async-done | bytes 2359328 | tf_op jit(solution)/shard_map/all_to_all | solution.py:557
  309.2 15.7 %all_to_all.47 = bf16[8,128,384]{1,2,0:T(8,128)(2,1)} all-to-all(bf16[8,128,384]{1,2,0:T(8,128)(2,1)S(1)} %copy_bitcast_fusion.1), channel_id=1, replica_groups=mesh['seq'=8,'slot'=4] {'seq'}, dimensions={0} | all-to-all | bytes 1572864 | tf_op jit(solution)/shard_map/all_to_all | solution.py:557
  324.9 3.7 all-to-all-start.5
  328.9 26.3 %all-to-all-done.5 = bf16[8,128,1024]{2,1,0:T(8,128)(2,1)S(1)} async-done(((bf16[8,128,1024]{2,1,0:T(8,128)(2,1)}), bf16[8,128,1024]{2,1,0:T(8,128)(2,1)S(1)}, u32[]{:S(2)}, u32[]{:S(2)}) %all-to-all-start.5) | async-done | bytes 2097184 | tf_op jit(solution)/shard_map/all_to_all | solution.py:557
  355.9 46.6 %all-reduce.1 = (f32[1024]{0:T(1024)}, f32[64]{0:T(128)}, f32[64]{0:T(128)}, f32[1024]{0:T(1024)}) all-reduce(f32[1024]{0:T(1024)S(1)} %get-tuple-element.77, f32[64]{0:T(128)S(1)} %get-tuple-element.105, f32[64]{0:T(128)S(1)} %get-tuple-element.104, f32[1024]{0:T(1024)S(1)} %get-tuple-element.75), channel_id=1, replica_groups=mesh['seq'=8,'slot'=4] {'seq','slot'}, use_global_device_ids=true, to_apply=%region_11.12 | all-reduce | flops 2176 | bytes 17408 | tf_op jit(solution)/shard_map/psum | solution.py:694
  403.4 81.6 %all-reduce.5.cloned.1.call-done = (bf16[8,128,384]{1,2,0:T(8,128)(2,1)}, bf16[8,128,1152]{1,2,0:T(8,128)(2,1)}, bf16[8,128,576]{1,2,0:T(8,128)(2,1)}) async-done(((bf16[8,128,384]{1,2,0:T(8,128)(2,1)}, bf16[8,128,1152]{1,2,0:T(8,128)(2,1)}, bf16[8,128,576]{1,2,0:T(8,128)(2,1)}), (bf16[8,128,384]{1,2,0:T(8,128)(2,1)}, bf16[8,128,1152]{1,2,0:T(8,128)(2,1)}, ...) | async-done | bytes 4325392 | tf_op jit(solution)/shard_map/psum | solution.py:673
  485.0 2.8 slice.104
  487.8 1.6 slice.105
  489.5 2.4 fusion.21
  493.7 1.9 copy.95
  496.7 3.0 copy.92
  499.7 1.8 copy.93
  501.5 2.9 copy.90
  504.3 1.8 copy.91
  508.1 1.8 copy.98
  509.9 1.8 copy.99
  511.7 1.6 pad_maximum_fusion.2
  514.1 1.6 pad_maximum_fusion.1
  516.6 1.6 pad_maximum_fusion
  (133 shorter events, 30.3 us)
Async XLA Ops:
  7.2 6.4 %copy-start = (bf16[128,1024]{1,0:T(8,128)(2,1)S(1)}, bf16[128,1024]{1,0:T(8,128)(2,1)}, u32[]{:S(2)}) copy-start(bf16[128,1024]{1,0:T(8,128)(2,1)} %param.16) | copy-start | bytes 786436
  7.2 38.8 %all-gather.14.cloned.1.call-start = ((), (), s32[]{:S(2)}) async-start(), calls=%async_computation.12 | async-start | bytes 2359296 | tf_op jit(solution)/shard_map/all_gather | solution.py:554
  7.9 116.4 %all-gather.10.cloned.1.call-start = ((), (), s32[]{:S(2)}) async-start(), calls=%async_computation.10 | async-start | bytes 2359296 | tf_op jit(solution)/shard_map/all_gather | solution.py:554
  10.4 113.9 %all-gather.8.cloned.1.call-start = ((), (), s32[]{:S(2)}) async-start(), calls=%async_computation.9 | async-start | bytes 2359296 | tf_op jit(solution)/shard_map/all_gather | solution.py:554
  13.7 6.2 %slice-start.4 = ((bf16[128,4608]{1,0:T(8,128)(2,1)}), bf16[128,4096]{1,0:T(8,128)(2,1)S(1)}, s32[]{:S(2)}) async-start(bf16[128,4608]{1,0:T(8,128)(2,1)} %param.20), calls=%async_computation.19 | async-start | bytes 2097152 | tf_op jit(solution)/shard_map/slice | solution.py:573
  14.7 18.2 %all-to-all-start = ((bf16[8,128,256]{2,1,0:T(8,128)(2,1)}), bf16[8,128,256]{2,1,0:T(8,128)(2,1)}, u32[]{:S(2)}, u32[]{:S(2)}) async-start(bf16[8,128,256]{2,1,0:T(8,128)(2,1)} %pad_maximum_fusion.4), calls=%async_computation | async-start | bytes 1048576 | tf_op jit(solution)/shard_map/all_to_all | solution.py:557
  19.8 133.7 %all-gather.16.cloned.1.call-start = ((), (), s32[]{:S(2)}) async-start(), calls=%async_computation.13 | async-start | bytes 2359296 | tf_op jit(solution)/shard_map/all_gather | solution.py:607
  20.5 4.4 copy-start.25
  20.6 4.4 copy-start.26
  25.5 1.2 slice-start.2
  25.5 1.9 slice-start.5
  25.5 2.7 slice-start.3
  25.5 2.8 slice-start
  26.8 2.2 slice-start.1
  29.0 1.3 copy-start.12
  29.0 1.3 copy-start.13
  29.2 1.5 copy-start.14
  46.0 7.3 %copy-start.19 = (bf16[128,512]{0,1:T(8,128)(2,1)S(1)}, bf16[128,512]{0,1:T(8,128)(2,1)}, u32[]{:S(2)}) copy-start(bf16[128,512]{0,1:T(8,128)(2,1)} %copy.101) | copy-start | bytes 393220
  201.7 30.2 %all-to-all-start.2 = ((bf16[8,128,1024]{2,1,0:T(8,128)(2,1)}), bf16[8,128,1024]{2,1,0:T(8,128)(2,1)S(1)}, u32[]{:S(2)}, u32[]{:S(2)}) async-start(bf16[8,128,1024]{2,1,0:T(8,128)(2,1)} %bitcast.136), calls=%async_computation.2 | async-start | bytes 4194304 | tf_op jit(solution)/shard_map/all_to_all | solution.py:557
  205.3 3.2 copy-start.22
  205.3 93.0 %all-gather.12.cloned.1.call-start = ((), (), s32[]{:S(2)}) async-start(), calls=%async_computation.11 | async-start | bytes 2359296 | tf_op jit(solution)/shard_map/all_gather | solution.py:554
  208.6 23.7 %copy-start.15 = (bf16[1,128,1024]{2,1,0:T(8,128)(2,1)S(1)}, bf16[1,128,1024]{2,1,0:T(8,128)(2,1)}, u32[]{:S(2)}) copy-start(bf16[1,128,1024]{2,1,0:T(8,128)(2,1)} %param.27) | copy-start | bytes 786436
  232.2 2.5 copy-start.27
  237.6 4.8 copy-start.9
  237.6 4.8 copy-start.10
  238.9 21.7 %all-to-all-start.8 = ((bf16[8,128,576]{1,2,0:T(8,128)(2,1)}), bf16[8,128,576]{1,2,0:T(8,128)(2,1)S(1)}, u32[]{:S(2)}, u32[]{:S(2)}) async-start(bf16[8,128,576]{1,2,0:T(8,128)(2,1)} %copy_bitcast_fusion), calls=%async_computation.8 | async-start | bytes 2359296 | tf_op jit(solution)/shard_map/all_to_all | solution.py:557
  260.5 10.1 %copy-start.6 = (bf16[8,128,576]{1,2,0:T(8,128)(2,1)}, bf16[8,128,576]{1,2,0:T(8,128)(2,1)S(1)}, u32[]{:S(2)}) copy-start(bf16[8,128,576]{1,2,0:T(8,128)(2,1)S(1)} %all-to-all-done.8) | copy-start | bytes 3538948
  260.5 14.4 %all-to-all-start.4 = ((bf16[8,128,128]{2,1,0:T(8,128)(2,1)}), bf16[8,128,128]{2,1,0:T(8,128)(2,1)S(1)}, u32[]{:S(2)}, u32[]{:S(2)}) async-start(bf16[8,128,128]{2,1,0:T(8,128)(2,1)} %bitcast.123), calls=%async_computation.4 | async-start | bytes 524288 | tf_op jit(solution)/shard_map/all_to_all | solution.py:557
  274.9 0.7 copy-start.21
  275.6 33.6 %all-to-all-start.7 = ((bf16[8,128,1152]{1,2,0:T(8,128)(2,1)}), bf16[8,128,1152]{1,2,0:T(8,128)(2,1)S(1)}, u32[]{:S(2)}, u32[]{:S(2)}) async-start(bf16[8,128,1152]{1,2,0:T(8,128)(2,1)} %copy.89), calls=%async_computation.7 | async-start | bytes 4718592 | tf_op jit(solution)/shard_map/all_to_all | solution.py:557
  279.8 205.3 %all-reduce.5.cloned.1.call-start = ((), (), s32[]{:S(2)}) async-start(), calls=%async_computation.14 | async-start | bytes 8650752 | tf_op jit(solution)/shard_map/psum | solution.py:673
  295.0 3.3 copy-start.20
  298.3 2.1 copy-start.18
  309.2 15.7 %copy-start.2 = (bf16[8,128,1152]{1,2,0:T(8,128)(2,1)}, bf16[8,128,1152]{1,2,0:T(8,128)(2,1)S(1)}, u32[]{:S(2)}) copy-start(bf16[8,128,1152]{1,2,0:T(8,128)(2,1)S(1)} %all-to-all-done.7) | copy-start | bytes 7077892
  324.9 3.8 copy-start.7
  324.9 3.9 copy-start.24
  324.9 30.3 %all-to-all-start.5 = ((bf16[8,128,1024]{2,1,0:T(8,128)(2,1)}), bf16[8,128,1024]{2,1,0:T(8,128)(2,1)S(1)}, u32[]{:S(2)}, u32[]{:S(2)}) async-start(bf16[8,128,1024]{2,1,0:T(8,128)(2,1)} %bitcast.135), calls=%async_computation.5 | async-start | bytes 4194304 | tf_op jit(solution)/shard_map/all_to_all | solution.py:557
  328.7 26.9 %copy-start.23 = (f32[1024]{0:T(1024)S(1)}, f32[1024]{0:T(1024)}, u32[]{:S(2)}) copy-start(f32[1024]{0:T(1024)} %param.23) | copy-start | bytes 12292
  328.7 73.8 %copy-start.11 = (f32[128,1024]{1,0:T(8,128)S(1)}, f32[128,1024]{1,0:T(8,128)}, u32[]{:S(2)}) copy-start(f32[128,1024]{1,0:T(8,128)} %get-tuple-element.87) | copy-start | bytes 1572868
  485.0 4.5 copy-start.3
  489.5 3.3 copy-start.8
  511.7 2.4 copy-start.4
  511.7 2.4 copy-start.16
  514.1 2.4 copy-start.5
  514.1 2.4 copy-start.17
  514.1 4.0 copy-start.1
Sparse Core Ops, SparseCore 0:
  9.9 36.0 all-gather.13
  48.5 39.3 all-gather.9
  89.7 34.0 all-gather.7
  125.6 27.8 all-gather.15
  234.8 32.8 all-gather.11
  325.0 159.9 all-reduce.4

commit v2 on v0

--- a/solution.py
+++ b/solution.py
@@ -1,6 +1,11 @@
+import functools
+
 import jax
 import jax.numpy as jnp
+import numpy as np
 from jax import lax
+from jax.experimental import pallas as pl
+from jax.experimental.pallas import tpu as pltpu
 from jax.sharding import PartitionSpec as P
 
 HEADS = 16
@@ -60,7 +65,7 @@
     )
 
 
-def body(
+def general_body(
     tokens,
     lengths,
     query_weight,
@@ -292,6 +297,694 @@
     )
 
 
+SLOTS_BY_HEADS = 4
+LANES = 2 * HEAD_DIM
+ROW_BLOCK = 256
+VMEM_LIMIT = 60 * 1024 * 1024
+
+
+def dot_nn(left, right):
+    return lax.dot_general(left, right, (((1,), (0,)), ((), ())), preferred_element_type=jnp.float32)
+
+
+def dot_nt(left, right):
+    return lax.dot_general(left, right, (((1,), (1,)), ((), ())), preferred_element_type=jnp.float32)
+
+
+def dot_tn(left, right):
+    return lax.dot_general(left, right, (((0,), (0,)), ((), ())), preferred_element_type=jnp.float32)
+
+
+def lane_is_low(shape):
+    return lax.broadcasted_iota(jnp.int32, shape, len(shape) - 1) < HEAD_DIM
+
+
+def pair_mean(values):
+    low = lane_is_low(values.shape)
+    first = jnp.sum(jnp.where(low, values, 0.0), axis=-1, keepdims=True)
+    second = jnp.sum(jnp.where(low, 0.0, values), axis=-1, keepdims=True)
+    return jnp.where(low, first, second) * (1.0 / HEAD_DIM)
+
+
+def pair_turn(values, cosine, sine_signed):
+    lane = lax.broadcasted_iota(jnp.int32, values.shape, 1)
+    near = lax.rem(lane, HEAD_DIM) < HEAD_DIM // 2
+    half = HEAD_DIM // 2
+    turned = jnp.where(near, pltpu.roll(values, LANES - half, 1), pltpu.roll(values, half, 1))
+    return values * cosine + turned * sine_signed
+
+
+def pair_swap(values):
+    return pltpu.roll(values.astype(jnp.float32), HEAD_DIM, 1)
+
+
+def array(kind, *shape):
+    return jax.ShapeDtypeStruct(shape, kind)
+
+
+def call(kernel, out_shape, scratch_shapes=(), token=False):
+    vmem, anywhere = pl.BlockSpec(memory_space=pltpu.VMEM), pl.BlockSpec(memory_space=pl.ANY)
+    single = not isinstance(out_shape, tuple)
+    shapes = ((out_shape,) if single else out_shape) + ((array(jnp.float32, 8, LANES),) if token else ())
+
+    def apply(*operands, smem=0, tokens=()):
+        given = len(operands)
+        results = given + len(tokens) + len(shapes)
+
+        def whole(*refs):
+            if token:
+                refs[results - 1][...] = jnp.zeros((8, LANES), jnp.float32)
+            kernel(*refs[:given], *refs[given + len(tokens) : results - token], *refs[results:])
+
+        in_specs = [pl.BlockSpec(memory_space=pltpu.SMEM)] * smem + [vmem] * (given - smem) + [anywhere] * len(tokens)
+        outputs = pl.pallas_call(
+            whole,
+            out_shape=shapes,
+            in_specs=in_specs,
+            out_specs=(vmem,) * len(shapes),
+            scratch_shapes=scratch_shapes,
+            compiler_params=pltpu.CompilerParams(vmem_limit_bytes=VMEM_LIMIT),
+        )(*operands, *tokens)
+        return outputs[0] if len(shapes) == 1 else outputs
+
+    return apply
+
+
+def after(values, *tokens):
+    count = len(values)
+    anywhere = pl.BlockSpec(memory_space=pl.ANY)
+    return pl.pallas_call(
+        lambda *refs: None,
+        out_shape=tuple(array(value.dtype, *value.shape) for value in values),
+        in_specs=[anywhere] * (count + len(tokens)),
+        out_specs=(anywhere,) * count,
+        input_output_aliases={i: i for i in range(count)},
+    )(*values, *tokens)
+
+
+def block_rows(me_ref, partner, rows):
+    return pl.ds(pl.multiple_of(jnp.bitwise_xor(me_ref[0], partner) * rows, rows), rows)
+
+
+def store_pair(me_ref, chip, values, own_ref, other_ref):
+    rows = values.shape[0] // 2
+    first = jnp.bitwise_and(me_ref[0], 1) == 0
+    own_ref[chip] = jnp.where(first, values[:rows], values[rows:]).astype(jnp.bfloat16)
+    other_ref[chip] = jnp.where(first, values[rows:], values[:rows]).astype(jnp.bfloat16)
+
+
+def pack_attention_kernel(query_ref, key_ref, value_ref, owned_ref):
+    for index in range(0, KV_HEADS, 2):
+        lanes = pl.ds(index * HEAD_DIM, LANES)
+        key, value = key_ref[:, lanes], value_ref[:, lanes]
+        low = lane_is_low(key.shape)
+        key, value = key.astype(jnp.float32), value.astype(jnp.float32)
+        pairs = (jnp.where(low, key, pair_swap(value)), jnp.where(low, pair_swap(key), value))
+        for step in range(2):
+            owned_ref[index + step, :, :LANES] = query_ref[:, pl.ds((index + step) * LANES, LANES)]
+            owned_ref[index + step, :, LANES:] = pairs[step].astype(jnp.bfloat16)
+
+
+def pack_units_kernel(slot_ref, gate_ref, up_ref, down_ref, first_ref, second_ref):
+    rows = first_ref.shape[1]
+    block = second_ref.shape[2] // 3
+    cut = block * KV_HEADS
+    half = pl.ds(pl.multiple_of(jnp.bitwise_and(slot_ref[0], 1) * rows, rows), rows)
+    for index in range(KV_HEADS):
+        for place, ref in enumerate((gate_ref, up_ref, down_ref)):
+            start = place * block + (LANES if place == 2 else 0)
+            first_ref[index, :, start : start + block] = ref[half, pl.ds(index * block, block)]
+            second_ref[index, :, place * block : (place + 1) * block] = ref[:, pl.ds(cut + index * block, block)]
+    for index in range(0, KV_HEADS, 2):
+        lanes = pl.ds(2 * cut + index * HEAD_DIM, LANES)
+        gate, up, down = (ref[half, lanes].astype(jnp.float32) for ref in (gate_ref, up_ref, down_ref))
+        low = lane_is_low(gate.shape)
+        rests = (jnp.where(low, gate, pair_swap(up)), jnp.where(low, pair_swap(gate), up))
+        downs = (jnp.where(low, down, pair_swap(down)), jnp.where(low, pair_swap(down), down))
+        for step in range(2):
+            first_ref[index + step, :, 2 * block : 2 * block + LANES] = rests[step].astype(jnp.bfloat16)
+            first_ref[index + step, :, 3 * block + LANES :] = downs[step].astype(jnp.bfloat16)
+
+
+def attention_forward_kernel(length_ref, me_ref, *refs):
+    x_refs = refs[:KV_HEADS]
+    (
+        weight_ref, gain_ref, q_gain_ref, k_gain_ref, cos_ref, sin_ref,
+        x_all_ref, normed_ref, q_proj_ref, kv_proj_ref, q_low_ref, k_pair_ref, v_pair_ref, attn_ref, attn_low_ref, weight_inv_ref,
+    ) = refs[KV_HEADS:]
+    tok_rows = x_refs[0].shape[0]
+    total = tok_rows * KV_HEADS
+    length = length_ref[0]
+    low = lane_is_low((ROW_BLOCK, LANES))
+    for partner in range(KV_HEADS):
+        x_all_ref[block_rows(me_ref, partner, tok_rows), :] = x_refs[partner][...]
+    for start in range(0, total, ROW_BLOCK):
+        rows = pl.ds(start, ROW_BLOCK)
+        x = x_all_ref[rows, :].astype(jnp.float32)
+        factor = lax.rsqrt(jnp.mean(x * x, axis=-1, keepdims=True) + EPSILON)
+        normed = (x * factor * gain_ref[...]).astype(jnp.bfloat16)
+        normed_ref[rows, :] = normed
+        proj = dot_nn(normed, weight_ref[...])
+        q_proj = proj[:, :LANES]
+        kv_proj = proj[:, LANES:]
+        q_proj_ref[rows, :] = q_proj
+        kv_proj_ref[rows, :] = kv_proj
+        cosine, sine = cos_ref[rows, :], sin_ref[rows, :]
+        q_factor = lax.rsqrt(pair_mean(q_proj * q_proj) + EPSILON)
+        q_low_ref[rows, :] = pair_turn(q_proj * q_factor * q_gain_ref[...], cosine, sine).astype(jnp.bfloat16)
+        k_factor = jnp.where(low, lax.rsqrt(pair_mean(kv_proj * kv_proj) + EPSILON), 1.0)
+        kv = pair_turn(
+            kv_proj * k_factor * k_gain_ref[...], jnp.where(low, cosine, 1.0), jnp.where(low, sine, 0.0)
+        )
+        swapped = pltpu.roll(kv, HEAD_DIM, 1)
+        k_pair_ref[rows, :] = jnp.where(low, kv, swapped).astype(jnp.bfloat16)
+        v_pair_ref[rows, :] = jnp.where(low, swapped, kv).astype(jnp.bfloat16)
+
+    scale = HEAD_DIM ** (-0.5)
+    for start in range(0, total, ROW_BLOCK):
+        rows = pl.ds(start, ROW_BLOCK)
+        q = q_low_ref[rows, :] * scale
+        zero = jnp.zeros_like(q)
+        heads = (jnp.where(low, q, zero), jnp.where(low, zero, q))
+        results = []
+        for q_head in heads:
+            weight_sum = jnp.zeros((ROW_BLOCK, 1), jnp.float32)
+            summed = jnp.zeros((ROW_BLOCK, LANES), jnp.float32)
+            if start > 0:
+                past = pl.ds(0, start)
+                exp_vals = jnp.exp(dot_nt(q_head, k_pair_ref[past, :]))
+                weight_sum += jnp.sum(exp_vals, axis=-1, keepdims=True)
+                summed += dot_nn(exp_vals.astype(jnp.bfloat16), v_pair_ref[past, :])
+            scores = dot_nt(q_head, k_pair_ref[rows, :])
+            query = lax.broadcasted_iota(jnp.int32, scores.shape, 0)
+            key = lax.broadcasted_iota(jnp.int32, scores.shape, 1)
+            allowed = (key <= query) & (key + start < length)
+            exp_vals = jnp.where(allowed, jnp.exp(scores), 0.0)
+            weight_sum += jnp.sum(exp_vals, axis=-1, keepdims=True)
+            summed += dot_nn(exp_vals.astype(jnp.bfloat16), v_pair_ref[rows, :])
+            inverse = 1.0 / weight_sum
+            results.append((summed * inverse, inverse))
+        attn = jnp.where(low, results[0][0], results[1][0])
+        attn_ref[rows, :] = attn
+        attn_low_ref[rows, :] = attn.astype(jnp.bfloat16)
+        weight_inv_ref[rows, :] = jnp.where(low, results[0][1], results[1][1])
+
+
+def attention_backward_kernel(
+    length_ref, me_ref, dattn_ref, weight_ref, q_gain_ref, k_gain_ref, cos_ref, sin_ref,
+    q_proj_ref, kv_proj_ref, q_low_ref, k_pair_ref, v_pair_ref, attn_ref, weight_inv_ref,
+    dnormed_own_ref, dnormed_other_ref, dproj_ref, terms_ref, dq_acc, dk_acc, dv_acc,
+):
+    total = dattn_ref.shape[0]
+    length = length_ref[0]
+    low = lane_is_low((ROW_BLOCK, LANES))
+    scale = HEAD_DIM ** (-0.5)
+    dk_acc[...] = jnp.zeros_like(dk_acc)
+    dv_acc[...] = jnp.zeros_like(dv_acc)
+    for start in range(0, total, ROW_BLOCK):
+        rows = pl.ds(start, ROW_BLOCK)
+        q = q_low_ref[rows, :] * scale
+        dattn = dattn_ref[rows, :]
+        zero = jnp.zeros_like(q)
+        inner = dattn.astype(jnp.float32) * attn_ref[rows, :]
+        inverses = weight_inv_ref[rows, :]
+        dq_heads = []
+        for head in range(2):
+            mine = low if head == 0 else jnp.logical_not(low)
+            q_head = jnp.where(mine, q, zero)
+            dattn_head = jnp.where(mine, dattn, zero)
+            delta = jnp.sum(jnp.where(mine, inner, 0.0), axis=-1, keepdims=True)
+            inverse = inverses[:, head * HEAD_DIM : head * HEAD_DIM + 1]
+            dq = jnp.zeros((ROW_BLOCK, LANES), jnp.float32)
+            spans = ([(0, start)] if start > 0 else []) + [(start, ROW_BLOCK)]
+            for key_start, key_count in spans:
+                keys = pl.ds(key_start, key_count)
+                k_pair = k_pair_ref[keys, :]
+                probs = jnp.exp(dot_nt(q_head, k_pair)) * inverse
+                if key_start == start:
+                    query = lax.broadcasted_iota(jnp.int32, probs.shape, 0)
+                    key = lax.broadcasted_iota(jnp.int32, probs.shape, 1)
+                    allowed = (key <= query) & (key + start < length)
+                    probs = jnp.where(allowed, probs, 0.0)
+                dprobs = dot_nt(dattn_head, v_pair_ref[keys, :])
+                dscores = (probs * (dprobs - delta)).astype(jnp.bfloat16)
+                dq += dot_nn(dscores, k_pair)
+                dk_acc[keys, :] += dot_tn(dscores, q_head)
+                dv_acc[keys, :] += dot_tn(probs.astype(jnp.bfloat16), dattn_head)
+            dq_heads.append(dq)
+        dq_acc[rows, :] = jnp.where(low, dq_heads[0], dq_heads[1]) * scale
+
+    q_terms = jnp.zeros((1, LANES), jnp.float32)
+    k_terms = jnp.zeros((1, LANES), jnp.float32)
+    for start in range(0, total, ROW_BLOCK):
+        rows = pl.ds(start, ROW_BLOCK)
+        cosine, sine = cos_ref[rows, :], sin_ref[rows, :]
+        q_proj = q_proj_ref[rows, :]
+        upstream = pair_turn(dq_acc[rows, :], cosine, -sine)
+        factor = lax.rsqrt(pair_mean(q_proj * q_proj) + EPSILON)
+        normal = q_proj * factor
+        weighted = upstream * q_gain_ref[...]
+        dq_proj = factor * (weighted - normal * pair_mean(weighted * normal))
+        q_terms += jnp.sum(upstream * normal, axis=0, keepdims=True)
+
+        dk = dk_acc[rows, :]
+        dv = dv_acc[rows, :]
+        dk = dk + pltpu.roll(dk, HEAD_DIM, 1)
+        dv = dv + pltpu.roll(dv, HEAD_DIM, 1)
+        kv_proj = kv_proj_ref[rows, :]
+        upstream = pair_turn(jnp.where(low, dk, 0.0), jnp.where(low, cosine, 1.0), jnp.where(low, -sine, 0.0))
+        factor = lax.rsqrt(pair_mean(kv_proj * kv_proj) + EPSILON)
+        normal = kv_proj * factor
+        weighted = upstream * k_gain_ref[...]
+        dk_proj = factor * (weighted - normal * pair_mean(weighted * normal))
+        k_terms += jnp.sum(upstream * normal, axis=0, keepdims=True)
+        dkv_proj = jnp.where(low, dk_proj, dv)
+        dproj = jnp.concatenate([dq_proj, dkv_proj], axis=1).astype(jnp.bfloat16)
+        dproj_ref[rows, :] = dproj
+        store_pair(me_ref, start // ROW_BLOCK, dot_nt(dproj, weight_ref[...]), dnormed_own_ref, dnormed_other_ref)
+    terms_ref[0:1, :] = q_terms
+    terms_ref[1:2, :] = k_terms
+
+
+def residual_kernel(me_ref, x_ref, *refs):
+    attn_refs = refs[:KV_HEADS]
+    out_weight_ref, gain_ref, residual_ref, attn_own_ref, normed_ref, attn_scratch, scratch = refs[KV_HEADS:]
+    total, width = x_ref.shape
+    tok_rows = total // KV_HEADS
+    for partner in range(KV_HEADS):
+        attn_scratch[:, block_rows(me_ref, partner, LANES)] = attn_refs[partner][...]
+    for start in range(0, total, ROW_BLOCK):
+        rows = pl.ds(start, ROW_BLOCK)
+        residual = x_ref[rows, :].astype(jnp.float32) + dot_nt(attn_scratch[rows, :], out_weight_ref[...])
+        scratch[rows, :] = residual
+        factor = lax.rsqrt(jnp.mean(residual * residual, axis=-1, keepdims=True) + EPSILON)
+        normed_ref[rows, :] = (residual * factor * gain_ref[...]).astype(jnp.bfloat16)
+    residual_ref[...] = scratch[block_rows(me_ref, 0, tok_rows), :]
+    attn_own_ref[...] = attn_scratch[block_rows(me_ref, 0, tok_rows), :]
+
+
+def unit_share(gate, up, upstream):
+    sigmoid = jax.nn.sigmoid(gate)
+    silu = gate * sigmoid
+    dgate = upstream * up * sigmoid * (1.0 + gate * (1.0 - sigmoid))
+    return silu * up, dgate, upstream * silu
+
+
+def first_units_kernel(me_ref, slot_ref, normed_ref, *refs):
+    dout_refs = refs[:KV_HEADS]
+    own_ref, other_ref, dout_ref, weight_ref, hidden_ref, dgate_up_ref = refs[KV_HEADS:]
+    total = normed_ref.shape[0]
+    block = hidden_ref.shape[1] - LANES
+    units = 2 * block + LANES
+    depth, half = 2 * own_ref.shape[1], own_ref.shape[1]
+    odd = jnp.bitwise_and(slot_ref[0], 1)
+    for index in range(KV_HEADS):
+        weight_ref[pl.ds(pl.multiple_of(index * depth + odd * half, half), half), :] = own_ref[index]
+        weight_ref[pl.ds(pl.multiple_of(index * depth + (1 - odd) * half, half), half), :] = other_ref[index]
+    for partner in range(KV_HEADS):
+        dout_ref[block_rows(me_ref, partner, depth), :] = dout_refs[partner][...]
+    low = lane_is_low((ROW_BLOCK, LANES))
+    for start in range(0, total, ROW_BLOCK):
+        rows = pl.ds(start, ROW_BLOCK)
+        both = dot_nn(normed_ref[rows, :], weight_ref[:, :units])
+        dhidden = dot_nn(dout_ref[rows, :], weight_ref[:, units:])
+        hidden, dgate, dup = unit_share(both[:, :block], both[:, block : 2 * block], dhidden[:, :block])
+        rest = both[:, 2 * block :]
+        swapped = pltpu.roll(rest, HEAD_DIM, 1)
+        rest_hidden, rest_dgate, rest_dup = unit_share(
+            jnp.where(low, rest, swapped), jnp.where(low, swapped, rest), dhidden[:, block:]
+        )
+        hidden_ref[rows, :block] = hidden.astype(jnp.bfloat16)
+        hidden_ref[rows, block:] = jnp.where(low, rest_hidden, 0.0).astype(jnp.bfloat16)
+        dgate_up_ref[rows, :block] = dgate.astype(jnp.bfloat16)
+        dgate_up_ref[rows, block : 2 * block] = dup.astype(jnp.bfloat16)
+        dgate_up_ref[rows, 2 * block :] = jnp.where(low, rest_dgate, rest_dup).astype(jnp.bfloat16)
+
+
+def second_units_kernel(
+    me_ref, normed_ref, dout_ref, first_ref, second_ref, dgate_up_first_ref, hidden_ref, dgate_up_ref, own_ref, other_ref
+):
+    total = normed_ref.shape[0]
+    block = hidden_ref.shape[1]
+    units = dgate_up_first_ref.shape[1]
+    for start in range(0, total, ROW_BLOCK):
+        rows = pl.ds(start, ROW_BLOCK)
+        both = dot_nn(normed_ref[rows, :], second_ref[:, : 2 * block])
+        dhidden = dot_nn(dout_ref[rows, :], second_ref[:, 2 * block :])
+        hidden, dgate, dup = unit_share(both[:, :block], both[:, block:], dhidden)
+        hidden_ref[rows, :] = hidden.astype(jnp.bfloat16)
+        dgate_up = jnp.concatenate([dgate, dup], axis=1).astype(jnp.bfloat16)
+        dgate_up_ref[rows, :] = dgate_up
+        dnormed = dot_nt(dgate_up, second_ref[:, : 2 * block]) + dot_nt(dgate_up_first_ref[rows, :], first_ref[:, :units])
+        store_pair(me_ref, start // ROW_BLOCK, dnormed, own_ref, other_ref)
+
+
+def unit_grads_kernel(normed_ref, dout_ref, hidden_ref, dgate_up_ref, grads_ref):
+    slots, _, rows_each, cols = grads_ref.shape
+    units = dgate_up_ref.shape[1]
+    for start in range(0, normed_ref.shape[1], ROW_BLOCK):
+        rows = pl.ds(start, ROW_BLOCK)
+        gate_up = dot_tn(normed_ref[:, rows], dgate_up_ref[...]).astype(jnp.bfloat16)
+        down = dot_tn(dout_ref[:, rows], hidden_ref[...])[:, : cols - units].astype(jnp.bfloat16)
+        for piece in range(0, ROW_BLOCK, rows_each):
+            owner, slot = divmod((start + piece) // rows_each, slots)
+            grads_ref[slot, owner, :, :units] = gate_up[piece : piece + rows_each]
+            grads_ref[slot, owner, :, units:] = down[piece : piece + rows_each]
+
+
+def mixed_kernel(me_ref, hidden_first_ref, hidden_second_ref, first_ref, second_ref, own_ref, other_ref):
+    total = hidden_first_ref.shape[0]
+    block = hidden_second_ref.shape[1]
+    units = 2 * block + LANES
+    for start in range(0, total, ROW_BLOCK):
+        rows = pl.ds(start, ROW_BLOCK)
+        part = dot_nt(hidden_first_ref[rows, :], first_ref[:, units:]) + dot_nt(
+            hidden_second_ref[rows, :], second_ref[:, 2 * block :]
+        )
+        store_pair(me_ref, start // ROW_BLOCK, part, own_ref, other_ref)
+
+
+def add_kernel(me_ref, own_ref, other_ref, *part_refs):
+    chip = lax.shift_right_logical(me_ref[0], 1)
+    for i, part_ref in enumerate(part_refs):
+        place = jnp.bitwise_xor(chip, i)
+        part_ref[...] = (own_ref[place].astype(jnp.float32) + other_ref[place].astype(jnp.float32)).astype(jnp.bfloat16)
+
+
+def add_blocks_kernel(own_ref, other_ref, sum_ref):
+    sum_ref[...] = (own_ref[...].astype(jnp.float32) + other_ref[...].astype(jnp.float32)).astype(sum_ref.dtype)
+
+
+def four_sum(parts):
+    first, second, third, fourth = (part.astype(jnp.float32) for part in parts)
+    return (first + second) + (third + fourth)
+
+
+def four_sum_kernel(*refs):
+    refs[4][...] = four_sum([ref[...] for ref in refs[:4]]).astype(refs[4].dtype)
+
+
+def residual_back_kernel(
+    parts_ref, residual_ref, upstream_ref, gain_ref, out_weight_ref,
+    residual_grad_ref, low_ref, dattn_ref, terms_ref,
+):
+    values = residual_ref[...]
+    factor = lax.rsqrt(jnp.mean(values * values, axis=-1, keepdims=True) + EPSILON)
+    part, terms = rms_back(values, factor, gain_ref[...], four_sum([parts_ref[i] for i in range(4)]))
+    residual_grad = upstream_ref[...].astype(jnp.float32) + part
+    residual_grad_ref[...] = residual_grad
+    low = residual_grad.astype(jnp.bfloat16)
+    low_ref[...] = low
+    dattn = dot_nn(low, out_weight_ref[...]).astype(jnp.bfloat16)
+    for index in range(KV_HEADS):
+        dattn_ref[index] = dattn[:, index * LANES : (index + 1) * LANES]
+    terms_ref[...] = jnp.sum(terms, axis=0, keepdims=True)
+
+
+def input_back_kernel(
+    part_a_ref, part_b_ref, part_c_ref, part_d_ref, tokens_ref, residual_grad_ref, gain_ref, input_grad_ref,
+):
+    values = tokens_ref[...].astype(jnp.float32)
+    factor = lax.rsqrt(jnp.mean(values * values, axis=-1, keepdims=True) + EPSILON)
+    part, _ = rms_back(values, factor, gain_ref[...], four_sum([ref[...] for ref in (part_a_ref, part_b_ref, part_c_ref, part_d_ref)]))
+    input_grad_ref[...] = (residual_grad_ref[...] + part).astype(jnp.bfloat16)
+
+
+def attention_gain_kernel(me_ref, x_ref, own_ref, other_ref, terms_ref):
+    rows = own_ref.shape[1]
+    core = jnp.bitwise_and(me_ref[0], 1)
+    terms = jnp.zeros(terms_ref.shape, jnp.float32)
+    for chip in range(own_ref.shape[0]):
+        for place, ref in ((core, own_ref), (1 - core, other_ref)):
+            x = x_ref[pl.ds(pl.multiple_of(chip * 2 * rows + place * rows, rows), rows), :].astype(jnp.float32)
+            factor = lax.rsqrt(jnp.mean(x * x, axis=-1, keepdims=True) + EPSILON)
+            terms += jnp.sum(ref[chip].astype(jnp.float32) * (x * factor), axis=0, keepdims=True)
+    terms_ref[...] = terms
+
+
+def projection_grads_kernel(normed_ref, dproj_ref, grads_ref):
+    width = normed_ref.shape[1]
+    depth = grads_ref.shape[1]
+    for start in range(0, width, ROW_BLOCK):
+        blocks = pl.ds(start // depth, ROW_BLOCK // depth)
+        grads = dot_tn(normed_ref[:, pl.ds(start, ROW_BLOCK)], dproj_ref[...]).astype(jnp.bfloat16)
+        grads_ref[blocks] = grads.reshape(-1, depth, 2 * LANES)
+
+
+def out_grads_kernel(me_ref, dbranch_ref, attn_ref, own_ref, other_ref):
+    width = dbranch_ref.shape[1]
+    for start in range(0, width, ROW_BLOCK):
+        grads = dot_tn(dbranch_ref[:, pl.ds(start, ROW_BLOCK)], attn_ref[...])
+        store_pair(me_ref, start // ROW_BLOCK, grads, own_ref, other_ref)
+
+
+def rows_kernel(attn_ref, attn_out_ref, first_ref, second_ref, *out_refs):
+    query_ref, key_ref, value_ref, out_ref, gate_ref, up_ref, down_ref = out_refs
+    f32 = jnp.float32
+    block = second_ref.shape[3] // 3
+    cut = KV_HEADS * block
+    out_ref[...] = attn_out_ref[...].astype(f32)
+    for index in range(KV_HEADS):
+        query_ref[:, pl.ds(index * LANES, LANES)] = attn_ref[index, :, :LANES].astype(f32)
+    low = lane_is_low((attn_ref.shape[1], LANES))
+    for index in range(0, KV_HEADS, 2):
+        lanes = pl.ds(index * HEAD_DIM, LANES)
+        even = attn_ref[index, :, LANES : 2 * LANES].astype(f32)
+        odd = attn_ref[index + 1, :, LANES : 2 * LANES].astype(f32)
+        key_ref[:, lanes] = jnp.where(low, even, pair_swap(odd))
+        value_ref[:, lanes] = jnp.where(low, pair_swap(even), odd)
+    low = lane_is_low((first_ref.shape[2], LANES))
+    for slot in range(first_ref.shape[0]):
+        rows = pl.ds(slot * first_ref.shape[2], first_ref.shape[2])
+        for index in range(KV_HEADS):
+            for place, ref in enumerate((gate_ref, up_ref, down_ref)):
+                start = place * block + (LANES if place == 2 else 0)
+                ref[rows, pl.ds(index * block, block)] = first_ref[slot, index, :, start : start + block].astype(f32)
+                start = place * block
+                ref[rows, pl.ds(cut + index * block, block)] = second_ref[slot, index, :, start : start + block].astype(f32)
+        for index in range(0, KV_HEADS, 2):
+            lanes = pl.ds(2 * cut + index * HEAD_DIM, LANES)
+            even = first_ref[slot, index, :, 2 * block : 2 * block + LANES].astype(f32)
+            odd = first_ref[slot, index + 1, :, 2 * block : 2 * block + LANES].astype(f32)
+            gate_ref[rows, lanes] = jnp.where(low, even, pair_swap(odd))
+            up_ref[rows, lanes] = jnp.where(low, pair_swap(even), odd)
+            even = first_ref[slot, index, :, 3 * block + LANES :].astype(f32)
+            odd = first_ref[slot, index + 1, :, 3 * block + LANES :].astype(f32)
+            down_ref[rows, lanes] = jnp.concatenate([even, odd], axis=1)
+
+
+def rotary_pair_tables(total):
+    half = HEAD_DIM // 2
+    exponent = np.arange(half, dtype=np.float32) * np.float32(2.0 / HEAD_DIM)
+    inverse = np.float32(THETA_BASE) ** (-exponent)
+    angles = np.arange(total, dtype=np.float32)[:, None] * inverse[None, :]
+    cosine, sine = np.cos(angles), np.sin(angles)
+    return (
+        jnp.asarray(np.concatenate([cosine] * 4, axis=1), jnp.float32),
+        jnp.asarray(np.concatenate([-sine, sine, -sine, sine], axis=1), jnp.float32),
+    )
+
+
+def to_partner(block, partner):
+    return lax.ppermute(block, "seq", [(i, i ^ partner) for i in range(KV_HEADS)])
+
+
+def gather_chips(block):
+    return [block] + [to_partner(block, partner) for partner in (2, 4, 6)]
+
+
+def gather_cores(parts):
+    return [part for pair in zip(parts, [to_partner(part, 1) for part in parts]) for part in pair]
+
+
+def swap_chips(blocks):
+    cores = [list(range(core, KV_HEADS, 2)) for core in range(2)]
+    return lax.all_to_all(blocks, "seq", 0, 0, axis_index_groups=cores, tiled=True)
+
+
+def sum_partners(me, own, other, *tokens):
+    parts = call(add_kernel, (array(own.dtype, *own.shape[1:]),) * own.shape[0])(
+        me, own, to_partner(other, 1), smem=1, tokens=tokens
+    )
+    return [parts[0]] + [to_partner(parts[i], 2 * i) for i in (1, 2, 3)]
+
+
+def add(left, right):
+    return (left.astype(jnp.float32) + right.astype(jnp.float32)).astype(left.dtype)
+
+
+def inward(part):
+    return lax.ppermute(part, "slot", [(0, 1), (3, 2)])
+
+
+def across(part):
+    return lax.ppermute(part, "slot", [(1, 2), (2, 1)])
+
+
+def outward(total):
+    slot = lax.axis_index("slot")
+    return jnp.where((slot == 1) | (slot == 2), total, lax.ppermute(total, "slot", [(1, 0), (2, 3)]))
+
+
+def sum_slots(*parts):
+    parts = [add(part, inward(part)) for part in parts]
+    parts = [add(part, across(part)) for part in parts]
+    return [outward(part) for part in parts]
+
+
+def sum_devices(values):
+    for partner in (1, 2, 4):
+        values = values + to_partner(values, partner)
+    for partner in (1, 2):
+        values = values + lax.ppermute(values, "slot", [(i, i ^ partner) for i in range(SLOTS_BY_HEADS)])
+    return values
+
+
+def heads_body(
+    tokens, lengths, query_weight, key_weight, value_weight, out_weight, gate_weight, up_weight, down_weight,
+    attn_norm, query_norm, key_norm, ffn_norm, out_grad,
+):
+    f32, bf16 = jnp.float32, jnp.bfloat16
+    count = KV_HEADS
+    tok_rows, width = tokens.shape[1:]
+    depth = query_weight.shape[0]
+    total = tok_rows * count
+    units = gate_weight.shape[1] // count
+    block = (units - HEAD_DIM) // 2
+    length = lengths[0]
+    index = lax.axis_index("seq")
+    me = index[None]
+    slot = lax.axis_index("slot")[None]
+    position = index * tok_rows + jnp.arange(tok_rows, dtype=jnp.int32)
+    row_valid = (position < length)[:, None]
+
+    def swap(blocks):
+        return lax.all_to_all(blocks, "seq", 0, 0, tiled=True)
+
+    x_parts = gather_cores(gather_chips(tokens[0]))
+    attn_owned, packed = call(pack_attention_kernel, array(bf16, count, depth, 2 * LANES), token=True)(
+        query_weight, key_weight, value_weight
+    )
+    attn_weight = swap(attn_owned).reshape(width, 2 * LANES)
+    first_owned, second_owned = call(
+        pack_units_kernel,
+        (array(bf16, count, depth // 2, 3 * block + 2 * LANES), array(bf16, count, depth, 3 * block)),
+    )(slot, gate_weight, up_weight, down_weight, smem=1, tokens=(packed,))
+    upstream = jnp.where(row_valid, out_grad[0], jnp.zeros_like(out_grad[0]))
+    first_owned, out_weight = after((first_owned, out_weight), *x_parts, attn_weight)
+    first_own = swap(first_owned)
+    out_full = lax.all_gather(out_weight, "seq", axis=0, tiled=True)
+
+    cosine, sine = rotary_pair_tables(total)
+    q_gain = jnp.concatenate([query_norm, query_norm])[None]
+    k_gain = jnp.concatenate([key_norm, jnp.ones_like(key_norm)])[None]
+    x_all, normed, q_proj, kv_proj, q_low, k_pair, v_pair, attn, attn_low, weight_inv, attended = call(
+        attention_forward_kernel,
+        (
+            array(bf16, total, width), array(bf16, total, width), array(f32, total, LANES), array(f32, total, LANES),
+            array(bf16, total, LANES), array(bf16, total, LANES), array(bf16, total, LANES), array(f32, total, LANES),
+            array(bf16, total, LANES), array(f32, total, LANES),
+        ),
+        token=True,
+    )(lengths, me, *x_parts, attn_weight, attn_norm[None], q_gain, k_gain, cosine, sine, smem=2)
+
+    attn_parts = gather_cores(gather_chips(attn_low))
+    first_own, upstream = after((first_own, upstream), attended)
+    first_other = lax.ppermute(first_own, "slot", [(i, i ^ 1) for i in range(SLOTS_BY_HEADS)])
+    dout_parts = gather_chips(upstream)
+    (second_owned,) = after((second_owned,), *attn_parts, first_own)
+    residual, attn_own, normed_two, normed_ready = call(
+        residual_kernel,
+        (array(f32, tok_rows, width), array(bf16, tok_rows, width), array(bf16, total, width)),
+        scratch_shapes=[pltpu.VMEM((total, width), bf16), pltpu.VMEM((total, width), f32)],
+        token=True,
+    )(me, x_all, *attn_parts, out_full, ffn_norm[None], smem=1, tokens=(second_owned,))
+    second_weight = swap(second_owned).reshape(width, -1)
+
+    dout_parts = gather_cores(after(tuple(dout_parts), normed_ready, first_other))
+    dout_all, first_weight, hidden_first, dgate_up_first = call(
+        first_units_kernel,
+        (
+            array(bf16, total, width), array(bf16, width, 3 * block + 2 * LANES), array(bf16, total, block + LANES),
+            array(bf16, total, 2 * block + LANES),
+        ),
+    )(me, slot, normed_two, *dout_parts, first_own, first_other, smem=2)
+    def unit_grads(hidden, dgate_up, cols, *tokens):
+        grads, done = call(unit_grads_kernel, array(bf16, SLOTS_BY_HEADS, count, depth // SLOTS_BY_HEADS, cols), token=True)(
+            normed_two, dout_all, hidden, dgate_up, tokens=tokens
+        )
+        return done, lax.psum_scatter(grads.reshape(width, cols), "slot", scatter_dimension=0, tiled=True)
+
+    def to_owners(sums):
+        return swap(sums.reshape(count, -1, sums.shape[1]))
+
+    halves = (array(bf16, count // 2, tok_rows, width),) * 2
+    hidden_second, dgate_up_second, *normed_two_grad, summed = call(
+        second_units_kernel, (array(bf16, total, block), array(bf16, total, 2 * block), *halves), token=True
+    )(me, normed_two, dout_all, first_weight, second_weight, dgate_up_first, smem=1)
+    first_grads, first_sums = unit_grads(
+        hidden_first, dgate_up_first, 3 * block + LANES + HEAD_DIM, summed
+    )
+    normed_two_sum = call(add_blocks_kernel, halves[0])(
+        normed_two_grad[0], to_partner(normed_two_grad[1], 1), tokens=(first_grads,)
+    )
+    residual_grad, attn_out_low, dattn, ffn_terms, branched = call(
+        residual_back_kernel,
+        (
+            array(f32, tok_rows, width), array(bf16, tok_rows, width), array(bf16, count, tok_rows, LANES),
+            array(f32, 1, width),
+        ),
+        token=True,
+    )(swap_chips(normed_two_sum), residual, upstream, ffn_norm[None], out_full)
+    second_grads, second_sums = unit_grads(hidden_second, dgate_up_second, 3 * block, branched)
+    dattn = swap(dattn)
+    dnormed_own, dnormed_other, dproj, terms = call(
+        attention_backward_kernel,
+        (*halves, array(bf16, total, 2 * LANES), array(f32, 2, LANES)),
+        scratch_shapes=[pltpu.VMEM((total, LANES), f32)] * 3,
+    )(
+        lengths, me, dattn.reshape(total, LANES), attn_weight, q_gain, k_gain, cosine, sine, q_proj, kv_proj, q_low, k_pair,
+        v_pair, attn, weight_inv, smem=2, tokens=(second_grads,),
+    )
+    proj_grads, projected = call(projection_grads_kernel, array(bf16, count, depth, 2 * LANES), token=True)(normed, dproj)
+    proj_part = swap(proj_grads)
+    (first_sums,) = after((first_sums,), projected)
+    first_rows = to_owners(first_sums)
+    first_all = lax.all_gather(first_rows, "slot", axis=0)
+
+    mixed_halves = call(mixed_kernel, halves)(
+        me, hidden_first, hidden_second, first_weight, second_weight, smem=1, tokens=(projected,)
+    )
+
+    *out_grads, out_ready = call(out_grads_kernel, halves, token=True)(me, attn_out_low, attn_own, smem=1, tokens=(projected,))
+    second_sums, proj_part = after((second_sums, proj_part), out_ready, first_rows)
+    second_all = lax.all_gather(to_owners(second_sums), "slot", axis=0)
+    out_part, out_summed = call(four_sum_kernel, array(bf16, tok_rows, width), token=True)(*sum_partners(me, *out_grads))
+    attn_terms = call(attention_gain_kernel, array(f32, 1, width))(
+        me, x_all, dnormed_own, dnormed_other, smem=1, tokens=(out_summed,)
+    )
+    proj_rows, out_rows = sum_slots(proj_part, out_part)
+    dnormed_parts = sum_partners(me, dnormed_own, dnormed_other, attn_terms)
+    mixed_parts = sum_partners(me, *mixed_halves, attn_terms)
+    input_grad = call(input_back_kernel, array(bf16, tok_rows, width))(
+        *dnormed_parts, tokens[0], residual_grad, attn_norm[None]
+    )
+    result = residual + sum(part.astype(f32) for part in mixed_parts)
+    mixed = jnp.where(row_valid, result, 0.0).astype(bf16)[None]
+    shapes = (query_weight, key_weight, value_weight, out_weight, gate_weight, up_weight, down_weight)
+    weight_grads = call(rows_kernel, tuple(array(f32, *weight.shape) for weight in shapes))(
+        proj_rows, out_rows, first_all, second_all
+    )
+
+    half = HEAD_DIM
+    gains = jnp.concatenate([attn_terms[0], ffn_terms[0], terms[0, :half] + terms[0, half:], terms[1, :half]])
+    gains = sum_devices(gains.reshape(-1, LANES)).reshape(-1)
+    return (
+        mixed, input_grad[None], *weight_grads, gains[:width], gains[2 * width : 2 * width + half],
+        gains[2 * width + half :], gains[width : 2 * width],
+    )
+
+
 def solution(mesh):
     in_specs = (
         P("slot", "seq", None),
@@ -324,4 +1017,6 @@
         P(),
         P(),
     )
+    by_heads = mesh.shape["seq"] == KV_HEADS and mesh.shape["slot"] == SLOTS_BY_HEADS
+    body = heads_body if by_heads else general_body
     return jax.shard_map(body, mesh=mesh, in_specs=in_specs, out_specs=out_specs, check_vma=False)

time: 1230 us -> 352 us (0.29)
  waiting for transfers between devices: 994 us -> 97.6 us
  matrix products: 110 us -> 0 us
  Pallas kernels: 0 us -> 106 us
  starting transfers between devices: 0.72 us -> 66.6 us
  other arithmetic: 43.7 us -> 4.34 us
    reduce_scatter x8 -> x2, waiting for transfers between devices: 581 us -> 0.01 us  [unit_grads(): lax.psum_scatter(grads.reshape(width, cols), 'slot', scatter_dimension=0,...]
    all_gather x9 -> x3, waiting for transfers between devices: 302 us -> 0.01 us  [the longest x1 0.01 us: heads_body(): out_full = lax.all_gather(out_weight, 'seq', axis=0, tiled=True)]
    dot_general x27 -> x0, matrix products: 110 us -> none  [the longest x7 36.8 us: contract_rows(): lax.dot_general(left, right, (((0,), (0,)), ((), ())), preferred_element_...]
    psum x1 -> x0, waiting for transfers between devices: 106 us -> none  [body(): lax.psum(query_share.astype(jnp.bfloat16), 'slot').astype(jnp.float32)]
    pallas_call x0 -> x27, Pallas kernels: none -> 106 us  [the longest x21 106 us: apply(): pl.pallas_call(whole, out_shape=shapes, in_specs=in_specs, out_specs=(vme...]
    ppermute x0 -> x46, waiting for transfers between devices: none -> 97.1 us  [the longest x37 60.6 us: to_partner(): lax.ppermute(block, 'seq', [(i, i ^ partner) for i in range(KV_HEADS)])]
    ppermute x0 -> x46, starting transfers between devices: none -> 46.9 us  [the longest x37 29.1 us: to_partner(): lax.ppermute(block, 'seq', [(i, i ^ partner) for i in range(KV_HEADS)])]
    psum x1 -> x0, blocking collectives: 45.7 us -> none  [body(): lax.psum((jnp.sum(attn_terms, axis=0), jnp.sum(query_terms, axis=(0, 1)),...]
  transfers between devices with their start and end apart: 18 -> 56, of which waited for: 18 -> 23; matrix products, arithmetic and copies ran while one was open for 9% -> 2% of each run, Pallas kernels for 0% -> 24%
where the time goes in v2:
time: 352 us; the launch traced here: 346 us
  Pallas kernels  106 us (30%)
  waiting for transfers between devices  97.6 us (28%)
  starting transfers between devices  66.6 us (19%)
  blocking collectives  43 us (12%)
  between operations  15.4 us (4%)
  local copies, waits for them, and re-layouts  13.6 us (4%)
  other arithmetic  4.34 us (1%)
    pallas_call x21, Pallas kernels, apply(): pl.pallas_call(whole, out_shape=shapes, in_specs=in_specs, out_specs=(vme...  106 us
    ppermute x37, waiting for transfers between devices, to_partner(): lax.ppermute(block, 'seq', [(i, i ^ partner) for i in range(KV_HEADS)])  60.6 us
    ppermute x2, waiting for transfers between devices, outward(): lax.ppermute(total, 'slot', [(1, 0), (2, 3)])  30.3 us
    ppermute x37, starting transfers between devices, to_partner(): lax.ppermute(block, 'seq', [(i, i ^ partner) for i in range(KV_HEADS)])  29.1 us
    all_to_all x2, blocking collectives, swap(): return lax.all_to_all(blocks, 'seq', 0, 0, tiled=True)  24 us
    all_to_all x5, starting transfers between devices, swap(): return lax.all_to_all(blocks, 'seq', 0, 0, tiled=True)  19.4 us
    all_to_all x1, blocking collectives, swap_chips(): lax.all_to_all(blocks, 'seq', 0, 0, axis_index_groups=cores, tiled=True)  19 us
    unnamed x88, local copies, waits for them, and re-layouts  11.7 us
  transfers between devices with their start and end apart: 56, of which 23 were waited for; matrix products, arithmetic and copies ran while one was open for 2% of the time, Pallas kernels for 24%

profile of v2, /device:TPU:0, one launch (start us, length us, event | category | flops | bytes accessed | tf_op | source)
XLA Modules:
  0.0 346.4 jit_solution(18180483151099270925)
XLA Ops:
  8.9 3.9 %collective-permute-start.5 = (bf16[128,1024]{1,0:T(8,128)(2,1)}, bf16[128,1024]{1,0:T(8,128)(2,1)S(1)}, u32[]{:S(2)}, u32[]{:S(2)}) collective-permute-start(bf16[128,1024]{1,0:T(8,128)(2,1)} %bitcast.45), channel_id=1, source_target_pairs={{0,24},{4,28},{8,16},{12,20},{16,8},{20,12},{24,0},{28,4},{1,25},{... | collective-permute-start | bytes 786440 | tf_op jit(solution)/shard_map/ppermute | solution.py:789
  13.4 2.0 shard_map.255
  15.4 4.2 %all-to-all-start = ((bf16[8,128,256]{2,1,0:T(8,128)(2,1)}), bf16[8,128,256]{2,1,0:T(8,128)(2,1)S(1)}, u32[]{:S(2)}, u32[]{:S(2)}) async-start(bf16[8,128,256]{2,1,0:T(8,128)(2,1)} %get-tuple-element.92), calls=%async_computation | async-start | bytes 1048576 | tf_op jit(solution)/shard_map/all_to_all | solution.py:862
  20.3 4.8 %collective-permute-done.3.refs_6_ = bf16[128,1024]{1,0:T(8,128)(2,1)S(1)} collective-permute-done((bf16[128,1024]{1,0:T(8,128)(2,1)}, bf16[128,1024]{1,0:T(8,128)(2,1)S(1)}, u32[]{:S(2)}, u32[]{:S(2)}) %collective-permute-start.3) | collective-permute-done | bytes 262176 | tf_op jit(solution)/shard_map/ppermute | solution.py:789
  26.4 3.8 %shard_map.257 = (bf16[8,64,1024]{2,1,0:T(8,128)(2,1)}, bf16[8,128,768]{2,1,0:T(8,128)(2,1)}) custom-call(s32[1]{0:T(128)} %bitcast.7.refs_0_.refs_1_, bf16[128,4608]{1,0:T(8,128)(2,1)} %refs_1_.4, bf16[128,4608]{1,0:T(8,128)(2,1)} %refs_2_.3, bf16[128,4608]{1,0:T(8,128)(2,1)} %refs_3_.1, f32[8,128]{1,0:T(8,128)} %get-tuple-element.95.refs_4_), custom_call_target="tpu_custom_call" | custom-call | tf_op jit(solution)/shard_map/pallas_call | solution.py:360
  31.7 3.6 %all-to-all-start.1 = ((bf16[8,64,1024]{2,1,0:T(8,128)(2,1)}), bf16[8,64,1024]{2,1,0:T(8,128)(2,1)S(1)}, u32[]{:S(2)}, u32[]{:S(2)}) async-start(bf16[8,64,1024]{2,1,0:T(8,128)(2,1)} %get-tuple-element.99), calls=%async_computation.1 | async-start | bytes 2097152 | tf_op jit(solution)/shard_map/all_to_all | solution.py:862
  36.6 7.0 %shard_map.256 = (bf16[1024,1024]{1,0:T(8,128)(2,1)}, bf16[1024,1024]{1,0:T(8,128)(2,1)}, f32[1024,128]{1,0:T(8,128)}, f32[1024,128]{1,0:T(8,128)}, bf16[1024,12...) custom-call(s32[1]{0:T(128)} %copy.54.refs_0_, ...), custom_call_target="tpu_custom_call" | custom-call | tf_op jit(solution)/shard_map/pallas_call | solution.py:360
  43.5 2.9 collective-permute-start.12
  47.1 12.4 %collective-permute-done.12.refs_7_.refs_8_ = bf16[1024,128]{1,0:T(8,128)(2,1)S(1)} collective-permute-done((bf16[1024,128]{1,0:T(8,128)(2,1)}, bf16[1024,128]{1,0:T(8,128)(2,1)S(1)}, u32[]{:S(2)}, u32[]{:S(2)}) %collective-permute-start.12) | collective-permute-done | bytes 262176 | tf_op jit(solution)/shard_map/ppermute | solution.py:789
  59.5 8.9 %collective-permute-done.10.refs_5_.refs_6_ = bf16[1024,128]{1,0:T(8,128)(2,1)S(1)} collective-permute-done((bf16[1024,128]{1,0:T(8,128)(2,1)}, bf16[1024,128]{1,0:T(8,128)(2,1)S(1)}, u32[]{:S(2)}, u32[]{:S(2)}) %collective-permute-start.10) | collective-permute-done | bytes 262176 | tf_op jit(solution)/shard_map/ppermute | solution.py:789
  71.7 3.7 %all-to-all-start.2 = ((bf16[8,128,768]{2,1,0:T(8,128)(2,1)}), bf16[8,128,768]{2,1,0:T(8,128)(2,1)S(1)}, u32[]{:S(2)}, u32[]{:S(2)}) async-start(bf16[8,128,768]{2,1,0:T(8,128)(2,1)} %shard_map.260.refs_12_), calls=%async_computation.2 | async-start | bytes 3145728 | tf_op jit(solution)/shard_map/all_to_all | solution.py:862
  75.7 2.1 collective-permute-start.17
  77.8 2.8 collective-permute-start.16
  82.0 7.7 %shard_map.261 = (f32[128,1024]{1,0:T(8,128)}, bf16[128,1024]{1,0:T(8,128)(2,1)}, bf16[1024,1024]{1,0:T(8,128)(2,1)}, f32[8,128]{1,0:T(8,128)}) custom-call(s32[1]{0:T(128)} %bitcast.1.refs_1_.refs_0_, bf16[1024,1024]{1,0:T(8,128)(2,1)} %get-tuple-element.93.refs_1_, bf16[1024,128]{1,0:T(8,128)(2,1)} %get-tuple-element.94.refs_1_.refs_2_, ...), custom_call_target="tpu_custom_call" | custom-call | tf_op jit(solution)/shard_map/pallas_call | solution.py:360
  89.6 12.9 %collective-permute-done.16.refs_3_ = bf16[128,1024]{1,0:T(8,128)(2,1)S(1)} collective-permute-done((bf16[128,1024]{1,0:T(8,128)(2,1)S(1)}, bf16[128,1024]{1,0:T(8,128)(2,1)S(1)}, u32[]{:S(2)}, u32[]{:S(2)}) %collective-permute-start.16) | collective-permute-done | bytes 262176 | tf_op jit(solution)/shard_map/ppermute | solution.py:789
  102.5 4.1 %collective-permute-done.15.refs_2_ = bf16[128,1024]{1,0:T(8,128)(2,1)S(1)} collective-permute-done((bf16[128,1024]{1,0:T(8,128)(2,1)S(1)}, bf16[128,1024]{1,0:T(8,128)(2,1)S(1)}, u32[]{:S(2)}, u32[]{:S(2)}) %collective-permute-start.15) | collective-permute-done | bytes 262176 | tf_op jit(solution)/shard_map/ppermute | solution.py:789
  111.0 7.7 %shard_map.263 = (bf16[1024,1024]{1,0:T(8,128)(2,1)}, bf16[1024,1024]{1,0:T(8,128)(2,1)}, bf16[1024,384]{1,0:T(8,128)(2,1)}, bf16[1024,640]{1,0:T(8,128)(2,1)}) custom-call(s32[1]{0:T(128)} %bitcast.1.refs_1_.refs_0_, s32[1]{0:T(128)} %bitcast.7.refs_0_.refs_1_, bf16[1024,1024]{1,0:T(8,128)(2,1)} %get-tuple-element.103.refs_2_.refs_1_.refs_0_, ...), custom_call_target="tpu_custom_call" | custom-call | tf_op jit(solution)/shard_map/pallas_call | solution.py:360
  119.8 9.6 %shard_map.264 = (bf16[1024,256]{1,0:T(8,128)(2,1)}, bf16[1024,512]{1,0:T(8,128)(2,1)}, bf16[4,128,1024]{2,1,0:T(8,128)(2,1)}, bf16[4,128,1024]{2,1,0:T(8,128)(2,1)}, f32[8,128]{1,0:T(8,128)}) custom-call(s32[1]{0:T(128)} %bitcast.1.refs_1_.refs_0_, bf16[1024,1024]{1,0:T(8,128)(2,1)} %get-tuple-element.103.refs_2_.refs_1_.refs_0_, ...), custom_call_target="tpu_custom_call" | custom-call | tf_op jit(solution)/shard_map/pallas_call | solution.py:360
  129.4 7.3 %shard_map.265 = (bf16[4,8,32,960]{3,2,1,0:T(8,128)(2,1)}, f32[8,128]{1,0:T(8,128)}) custom-call(bf16[1024,1024]{1,0:T(8,128)(2,1)} %get-tuple-element.103.refs_2_.refs_1_.refs_0_, bf16[1024,1024]{1,0:T(8,128)(2,1)} %get-tuple-element.111.refs_2_.refs_1_, bf16[1024,384]{1,0:T(8,128)(2,1)} %get-tuple-element.110.refs_2_.refs_1_, ...), custom_call_target="tpu_custom_call" | custom-call | tf_op jit(solution)/shard_map/pallas_call | solution.py:360
  138.1 2.5 collective-permute-done.22.refs_1_
  141.6 2.8 shard_map.266
  144.4 19.0 %all_to_all.40.refs_0_ = bf16[4,128,1024]{2,1,0:T(8,128)(2,1)} all-to-all(bf16[4,128,1024]{2,1,0:T(8,128)(2,1)} %shard_map.266), channel_id=1, replica_groups={{0,8,16,24},{4,12,20,28},{1,9,17,25},{5,13,21,29},{2,10,18,26},{6,14,22..., dimensions={0} | all-to-all | bytes 2097152 | tf_op jit(solution)/shard_map/all_to_all | solution.py:802
  163.4 3.7 %shard_map.267 = (f32[128,1024]{1,0:T(8,128)}, bf16[128,1024]{1,0:T(8,128)(2,1)}, bf16[8,128,128]{2,1,0:T(8,128)(2,1)}, f32[1,1024]{1,0:T(1,128)}, f32[8,128]{1,0:T(8,128)}) custom-call(bf16[4,128,1024]{2,1,0:T(8,128)(2,1)} %all_to_all.40.refs_0_, f32[128,1024]{1,0:T(8,128)} %get-tuple-element.102.refs_1_, bf16[128,1024]{1,0:T(8,128)(2,1)} %get-tuple-element.104.refs_2_, ...), custom_call_target="tpu_custom_call" | custom-call | tf_op jit(solution)/shard_map/pallas_call | solution.py:360
  167.1 5.8 %shard_map.268 = (bf16[4,8,32,768]{3,2,1,0:T(8,128)(2,1)}, f32[8,128]{1,0:T(8,128)}) custom-call(bf16[1024,1024]{1,0:T(8,128)(2,1)} %get-tuple-element.103.refs_2_.refs_1_.refs_0_, bf16[1024,1024]{1,0:T(8,128)(2,1)} %get-tuple-element.111.refs_2_.refs_1_, bf16[1024,256]{1,0:T(8,128)(2,1)} %get-tuple-element.114.refs_2_, ...), custom_call_target="tpu_custom_call" | custom-call | tf_op jit(solution)/shard_map/pallas_call | solution.py:360
  173.0 10.0 %all_to_all.41 = bf16[8,128,128]{2,1,0:T(8,128)(2,1)} all-to-all(bf16[8,128,128]{2,1,0:T(8,128)(2,1)S(1)} %copy-done.31), channel_id=1, replica_groups=mesh['seq'=8,'slot'=4] {'seq'}, dimensions={0} | all-to-all | bytes 524288 | tf_op jit(solution)/shard_map/all_to_all | solution.py:862
  183.0 13.7 %shard_map.269 = (bf16[4,128,1024]{2,1,0:T(8,128)(2,1)}, bf16[4,128,1024]{2,1,0:T(8,128)(2,1)}, bf16[1024,256]{1,0:T(8,128)(2,1)}, f32[2,128]{1,0:T(2,128)}) custom-call(s32[1]{0:T(128)} %copy.54.refs_0_, s32[1]{0:T(128)} %bitcast.1.refs_1_.refs_0_, bf16[1024,128]{1,0:T(8,128)(2,1)} %bitcast.58, bf16[1024,256]{1,0:T(8,128)(2,1)} %bitcast.44, ...), custom_call_target="tpu_custom_call" | custom-call | tf_op jit(solution)/shard_map/pallas_call | solution.py:360
  196.7 3.3 shard_map.270
  199.9 14.0 %all_to_all.42.refs_3_ = bf16[8,32,960]{2,1,0:T(8,128)(2,1)} all-to-all(bf16[8,32,960]{2,1,0:T(8,128)(2,1)} %bitcast.54), channel_id=1, replica_groups=mesh['seq'=8,'slot'=4] {'seq'}, dimensions={0} | all-to-all | bytes 983040 | tf_op jit(solution)/shard_map/all_to_all | solution.py:862
  214.0 3.1 shard_map.272
  217.1 3.7 %all-to-all-start.5 = ((bf16[8,128,256]{2,1,0:T(8,128)(2,1)}), bf16[8,128,256]{2,1,0:T(8,128)(2,1)S(1)}, u32[]{:S(2)}, u32[]{:S(2)}) async-start(bf16[8,128,256]{2,1,0:T(8,128)(2,1)} %get-tuple-element.156), calls=%async_computation.6 | async-start | bytes 1048576 | tf_op jit(solution)/shard_map/all_to_all | solution.py:862
  221.4 5.6 %shard_map.271 = (bf16[4,128,1024]{2,1,0:T(8,128)(2,1)}, bf16[4,128,1024]{2,1,0:T(8,128)(2,1)}) custom-call(s32[1]{0:T(128)} %bitcast.1.refs_1_.refs_0_, bf16[1024,384]{1,0:T(8,128)(2,1)} %get-tuple-element.110.refs_2_.refs_1_, bf16[1024,256]{1,0:T(8,128)(2,1)} %get-tuple-element.114.refs_2_, bf16[1024,1024]{1,0:T(8,128)(2,1)} %get-tuple-element.112.refs_3_, ...), custom_call_target="tpu_custom_call" | custom-call | tf_op jit(solution)/shard_map/pallas_call | solution.py:360
  227.0 2.8 shard_map.273
  229.9 1.9 collective-permute-start.25
  234.2 4.1 %all-to-all-start.7 = ((bf16[8,32,768]{2,1,0:T(8,128)(2,1)}), bf16[8,32,768]{2,1,0:T(8,128)(2,1)S(1)}, u32[]{:S(2)}, u32[]{:S(2)}) async-start(bf16[8,32,768]{2,1,0:T(8,128)(2,1)} %bitcast.57), calls=%async_computation.9 | async-start | bytes 786432 | tf_op jit(solution)/shard_map/all_to_all | solution.py:862
  239.2 3.9 %collective-permute-start.35 = (bf16[8,128,256]{2,1,0:T(8,128)(2,1)}, bf16[8,128,256]{2,1,0:T(8,128)(2,1)S(1)}, u32[]{:S(2)}, u32[]{:S(2)}) collective-permute-start(bf16[8,128,256]{2,1,0:T(8,128)(2,1)} %get-tuple-element.159), channel_id=1, source_target_pairs={{0,1},{3,2},{4,5},{7,6},{8,9},{11,10},{12,13},{15,14},{16,17},{19,... | collective-permute-start | bytes 1572872 | tf_op jit(solution)/shard_map/ppermute | solution.py:817
  243.2 4.2 %collective-permute-done.26.refs_2_ = bf16[128,1024]{1,0:T(8,128)(2,1)} collective-permute-done((bf16[128,1024]{1,0:T(8,128)(2,1)}, bf16[128,1024]{1,0:T(8,128)(2,1)}, u32[]{:S(2)}, u32[]{:S(2)}) %collective-permute-start.26) | collective-permute-done | bytes 262176 | tf_op jit(solution)/shard_map/ppermute | solution.py:789
  247.3 2.0 shard_map.274
  249.3 4.1 %shard_map.275.refs_3_ = f32[1,1024]{1,0:T(1,128)} custom-call(s32[1]{0:T(128)} %bitcast.1.refs_1_.refs_0_, bf16[1024,1024]{1,0:T(8,128)(2,1)} %get-tuple-element.93.refs_1_, bf16[4,128,1024]{2,1,0:T(8,128)(2,1)} %get-tuple-element.135.refs_2_.refs_1_, bf16[4,128,1024]{2,1,0:T(8,128)(2,1)} %get-tuple-element.136.refs_3_, f32[8,128]{1,0:T(8,128)} %get-tuple-element.145.refs_4_), custom_call_target="tpu_custom_call" | custom-call | tf_op jit(solution)/shard_map/pallas_call | solution.py:360
  256.7 2.3 collective-permute-done.42
  259.1 3.2 collective-permute-start.43
  267.7 3.0 collective-permute-start.45
  270.7 2.8 shard_map.277
  277.3 2.7 shard_map.276
  280.0 3.1 collective-permute-start.38
  285.2 4.2 %collective-permute-done.38 = bf16[128,1024]{1,0:T(8,128)(2,1)S(1)} collective-permute-done((bf16[128,1024]{1,0:T(8,128)(2,1)S(1)}, bf16[128,1024]{1,0:T(8,128)(2,1)S(1)}, u32[]{:S(2)}, u32[]{:S(2)}) %collective-permute-start.38) | collective-permute-done | bytes 262176 | tf_op jit(solution)/shard_map/ppermute | solution.py:817
  294.3 2.5 shard_map.278
  301.6 30.3 %collective-permute-done.40 = bf16[128,1024]{1,0:T(8,128)(2,1)S(1)} collective-permute-done((bf16[128,1024]{1,0:T(8,128)(2,1)S(1)}, bf16[128,1024]{1,0:T(8,128)(2,1)S(1)}, u32[]{:S(2)}, u32[]{:S(2)}) %collective-permute-start.40) | collective-permute-done | bytes 262176 | tf_op jit(solution)/shard_map/ppermute | solution.py:826
  333.5 6.0 %shard_map.281 = (f32[128,1024]{1,0:T(8,128)}, f32[128,512]{1,0:T(8,128)}, f32[128,512]{1,0:T(8,128)}, f32[128,1024]{1,0:T(8,128)}, f32[128,4608]{1,0:T(8,128)},...) custom-call(bf16[8,128,256]{2,1,0:T(8,128)(2,1)} %broadcast_select_fusion.refs_0_, ...), custom_call_target="tpu_custom_call" | custom-call | tf_op jit(solution)/shard_map/pallas_call | solution.py:360
  (206 shorter events, 49.3 us)
Async XLA Ops:
  8.9 11.3 %collective-permute-start.5 = (bf16[128,1024]{1,0:T(8,128)(2,1)}, bf16[128,1024]{1,0:T(8,128)(2,1)S(1)}, u32[]{:S(2)}, u32[]{:S(2)}) collective-permute-start(bf16[128,1024]{1,0:T(8,128)(2,1)} %bitcast.45), channel_id=1, source_target_pairs={{0,24},{4,28},{8,16},{12,20},{16,8},{20,12},{24,0},{28,4},{1,25},{... | collective-permute-start | bytes 786440 | tf_op jit(solution)/shard_map/ppermute | solution.py:789
  12.8 12.2 %collective-permute-start.3 = (bf16[128,1024]{1,0:T(8,128)(2,1)}, bf16[128,1024]{1,0:T(8,128)(2,1)S(1)}, u32[]{:S(2)}, u32[]{:S(2)}) collective-permute-start(bf16[128,1024]{1,0:T(8,128)(2,1)} %bitcast.46), channel_id=1, source_target_pairs={{0,16},{4,20},{8,24},{12,28},{16,0},{20,4},{24,8},{28,12},{1,17},{... | collective-permute-start | bytes 786440 | tf_op jit(solution)/shard_map/ppermute | solution.py:789
  13.3 13.1 %collective-permute-start.1 = (bf16[128,1024]{1,0:T(8,128)(2,1)}, bf16[128,1024]{1,0:T(8,128)(2,1)S(1)}, u32[]{:S(2)}, u32[]{:S(2)}) collective-permute-start(bf16[128,1024]{1,0:T(8,128)(2,1)} %bitcast.47), channel_id=1, source_target_pairs={{0,8},{4,12},{8,0},{12,4},{16,24},{20,28},{24,16},{28,20},{1,9},{5... | collective-permute-start | bytes 786440 | tf_op jit(solution)/shard_map/ppermute | solution.py:789
  15.4 15.2 %all-to-all-start = ((bf16[8,128,256]{2,1,0:T(8,128)(2,1)}), bf16[8,128,256]{2,1,0:T(8,128)(2,1)S(1)}, u32[]{:S(2)}, u32[]{:S(2)}) async-start(bf16[8,128,256]{2,1,0:T(8,128)(2,1)} %get-tuple-element.92), calls=%async_computation | async-start | bytes 1048576 | tf_op jit(solution)/shard_map/all_to_all | solution.py:862
  19.6 62.4 %all-gather.6.cloned.1.call-start = ((), (), s32[]{:S(2)}) async-start(), calls=%async_computation.10 | async-start | bytes 2359296 | tf_op jit(solution)/shard_map/all_gather | solution.py:876
  19.6 10.5 %collective-permute-start = (bf16[128,1024]{1,0:T(8,128)(2,1)S(1)}, bf16[128,1024]{1,0:T(8,128)(2,1)S(1)}, u32[]{:S(2)}, u32[]{:S(2)}) collective-permute-start(bf16[128,1024]{1,0:T(8,128)(2,1)S(1)} %bitcast.51), channel_id=1, source_target_pairs={{0,4},{4,0},{8,12},{12,8},{16,20},{20,16},{24,28},{28,24},{1,5},{5... | collective-permute-start | bytes 786440 | tf_op jit(solution)/shard_map/ppermute | solution.py:789
  20.2 10.4 %collective-permute-start.6 = (bf16[128,1024]{1,0:T(8,128)(2,1)S(1)}, bf16[128,1024]{1,0:T(8,128)(2,1)S(1)}, u32[]{:S(2)}, u32[]{:S(2)}) collective-permute-start(bf16[128,1024]{1,0:T(8,128)(2,1)S(1)} %collective-permute-done.5.refs_8_), channel_id=1, source_target_pairs={{0,4},{4,0},{8,12},{12,8},{16,20},{20,16},{24,28},{28,24},{1,5},{5... | collective-permute-start | bytes 786440 | tf_op jit(solution)/shard_map/ppermute | solution.py:789
  25.0 5.6 %collective-permute-start.4 = (bf16[128,1024]{1,0:T(8,128)(2,1)S(1)}, bf16[128,1024]{1,0:T(8,128)(2,1)S(1)}, u32[]{:S(2)}, u32[]{:S(2)}) collective-permute-start(bf16[128,1024]{1,0:T(8,128)(2,1)S(1)} %collective-permute-done.3.refs_6_), channel_id=1, source_target_pairs={{0,4},{4,0},{8,12},{12,8},{16,20},{20,16},{24,28},{28,24},{1,5},{5... | collective-permute-start | bytes 786440 | tf_op jit(solution)/shard_map/ppermute | solution.py:789
  26.4 4.2 %collective-permute-start.2 = (bf16[128,1024]{1,0:T(8,128)(2,1)S(1)}, bf16[128,1024]{1,0:T(8,128)(2,1)S(1)}, u32[]{:S(2)}, u32[]{:S(2)}) collective-permute-start(bf16[128,1024]{1,0:T(8,128)(2,1)S(1)} %collective-permute-done.1.refs_4_), channel_id=1, source_target_pairs={{0,4},{4,0},{8,12},{12,8},{16,20},{20,16},{24,28},{28,24},{1,5},{5... | collective-permute-start | bytes 786440 | tf_op jit(solution)/shard_map/ppermute | solution.py:789
  31.7 38.1 %all-to-all-start.1 = ((bf16[8,64,1024]{2,1,0:T(8,128)(2,1)}), bf16[8,64,1024]{2,1,0:T(8,128)(2,1)S(1)}, u32[]{:S(2)}, u32[]{:S(2)}) async-start(bf16[8,64,1024]{2,1,0:T(8,128)(2,1)} %get-tuple-element.99), calls=%async_computation.1 | async-start | bytes 2097152 | tf_op jit(solution)/shard_map/all_to_all | solution.py:862
  43.5 16.0 %collective-permute-start.12 = (bf16[1024,128]{1,0:T(8,128)(2,1)}, bf16[1024,128]{1,0:T(8,128)(2,1)S(1)}, u32[]{:S(2)}, u32[]{:S(2)}) collective-permute-start(bf16[1024,128]{1,0:T(8,128)(2,1)} %get-tuple-element.94.refs_1_.refs_2_), channel_id=1, source_target_pairs={{0,24},{4,28},{8,16},{12,20},{16,8},{20,12},{24,0},{28,4},{1,25},{... | collective-permute-start | bytes 786440 | tf_op jit(solution)/shard_map/ppermute | solution.py:789
  46.4 22.0 %collective-permute-start.10 = (bf16[1024,128]{1,0:T(8,128)(2,1)}, bf16[1024,128]{1,0:T(8,128)(2,1)S(1)}, u32[]{:S(2)}, u32[]{:S(2)}) collective-permute-start(bf16[1024,128]{1,0:T(8,128)(2,1)} %get-tuple-element.94.refs_1_.refs_2_), channel_id=1, source_target_pairs={{0,16},{4,20},{8,24},{12,28},{16,0},{20,4},{24,8},{28,12},{1,17},{... | collective-permute-start | bytes 786440 | tf_op jit(solution)/shard_map/ppermute | solution.py:789
  47.0 21.7 %collective-permute-start.8 = (bf16[1024,128]{1,0:T(8,128)(2,1)}, bf16[1024,128]{1,0:T(8,128)(2,1)S(1)}, u32[]{:S(2)}, u32[]{:S(2)}) collective-permute-start(bf16[1024,128]{1,0:T(8,128)(2,1)} %get-tuple-element.94.refs_1_.refs_2_), channel_id=1, source_target_pairs={{0,8},{4,12},{8,0},{12,4},{16,24},{20,28},{24,16},{28,20},{1,9},{5... | collective-permute-start | bytes 786440 | tf_op jit(solution)/shard_map/ppermute | solution.py:789
  47.1 23.7 %collective-permute-start.7 = (bf16[1024,128]{1,0:T(8,128)(2,1)}, bf16[1024,128]{1,0:T(8,128)(2,1)S(1)}, u32[]{:S(2)}, u32[]{:S(2)}) collective-permute-start(bf16[1024,128]{1,0:T(8,128)(2,1)} %get-tuple-element.94.refs_1_.refs_2_), channel_id=1, source_target_pairs={{0,4},{4,0},{8,12},{12,8},{16,20},{20,16},{24,28},{28,24},{1,5},{5... | collective-permute-start | bytes 786440 | tf_op jit(solution)/shard_map/ppermute | solution.py:789
  59.5 11.2 %collective-permute-start.13 = (bf16[1024,128]{1,0:T(8,128)(2,1)S(1)}, bf16[1024,128]{1,0:T(8,128)(2,1)S(1)}, u32[]{:S(2)}, u32[]{:S(2)}) collective-permute-start(bf16[1024,128]{1,0:T(8,128)(2,1)S(1)} %collective-permute-done.12.refs_7_.refs_8_), channel_id=1, source_target_pairs={{0,4},{4,0},{8,12},{12,8},{16,20},{20,16},{24,28},{28,24},{1,5},{5... | collective-permute-start | bytes 786440 | tf_op jit(solution)/shard_map/ppermute | solution.py:789
  71.7 46.9 %all-to-all-start.2 = ((bf16[8,128,768]{2,1,0:T(8,128)(2,1)}), bf16[8,128,768]{2,1,0:T(8,128)(2,1)S(1)}, u32[]{:S(2)}, u32[]{:S(2)}) async-start(bf16[8,128,768]{2,1,0:T(8,128)(2,1)} %shard_map.260.refs_12_), calls=%async_computation.2 | async-start | bytes 3145728 | tf_op jit(solution)/shard_map/all_to_all | solution.py:862
  75.4 124.5 %reduce-scatter.5.cloned.1.call-start = ((), (), s32[]{:S(2)}) async-start(), calls=%async_computation.12 | async-start | bytes 2621440 | tf_op jit(solution)/shard_map/reduce_scatter | solution.py:916
  75.7 31.2 %collective-permute-start.17 = (bf16[8,64,1024]{2,1,0:T(8,128)(2,1)S(1)}, bf16[8,64,1024]{2,1,0:T(8,128)(2,1)}, u32[]{:S(2)}, u32[]{:S(2)}) collective-permute-start(bf16[8,64,1024]{2,1,0:T(8,128)(2,1)S(1)} %copy-done.1), channel_id=1, source_target_pairs={{0,1},{1,0},{2,3},{3,2},{4,5},{5,4},{6,7},{7,6},{8,9},{9,8},{10,11... | collective-permute-start | bytes 3145736 | tf_op jit(solution)/shard_map/ppermute | solution.py:893
  77.8 24.7 %collective-permute-start.16 = (bf16[128,1024]{1,0:T(8,128)(2,1)S(1)}, bf16[128,1024]{1,0:T(8,128)(2,1)S(1)}, u32[]{:S(2)}, u32[]{:S(2)}) collective-permute-start(bf16[128,1024]{1,0:T(8,128)(2,1)S(1)} %copy-done.6), channel_id=1, source_target_pairs={{0,24},{4,28},{8,16},{12,20},{16,8},{20,12},{24,0},{28,4},{1,25},{... | collective-permute-start | bytes 786440 | tf_op jit(solution)/shard_map/ppermute | solution.py:789
  80.6 26.1 %collective-permute-start.15 = (bf16[128,1024]{1,0:T(8,128)(2,1)S(1)}, bf16[128,1024]{1,0:T(8,128)(2,1)S(1)}, u32[]{:S(2)}, u32[]{:S(2)}) collective-permute-start(bf16[128,1024]{1,0:T(8,128)(2,1)S(1)} %copy-done.6), channel_id=1, source_target_pairs={{0,16},{4,20},{8,24},{12,28},{16,0},{20,4},{24,8},{28,12},{1,17},{... | collective-permute-start | bytes 786440 | tf_op jit(solution)/shard_map/ppermute | solution.py:789
  81.1 25.7 %collective-permute-start.14 = (bf16[128,1024]{1,0:T(8,128)(2,1)S(1)}, bf16[128,1024]{1,0:T(8,128)(2,1)}, u32[]{:S(2)}, u32[]{:S(2)}) collective-permute-start(bf16[128,1024]{1,0:T(8,128)(2,1)S(1)} %copy-done.6), channel_id=1, source_target_pairs={{0,8},{4,12},{8,0},{12,4},{16,24},{20,28},{24,16},{28,20},{1,9},{5... | collective-permute-start | bytes 786440 | tf_op jit(solution)/shard_map/ppermute | solution.py:789
  136.7 96.6 %reduce-scatter.3.cloned.1.call-start = ((), (), s32[]{:S(2)}) async-start(), calls=%async_computation.11 | async-start | bytes 1966080 | tf_op jit(solution)/shard_map/reduce_scatter | solution.py:916
  172.9 160.6 %all-gather.8.cloned.1.call-start = ((), (), s32[]{:S(2)}) async-start(), calls=%async_computation.13 | async-start | bytes 2621440 | tf_op jit(solution)/shard_map/all_gather | solution.py:953
  217.1 9.9 %collective-permute-start.24 = (bf16[4,128,1024]{2,1,0:T(8,128)(2,1)}, bf16[4,128,1024]{2,1,0:T(8,128)(2,1)}, u32[]{:S(2)}, u32[]{:S(2)}) collective-permute-start(bf16[4,128,1024]{2,1,0:T(8,128)(2,1)} %get-tuple-element.140), channel_id=1, source_target_pairs={{0,4},{4,0},{8,12},{12,8},{16,20},{20,16},{24,28},{28,24},{1,5},{5... | collective-permute-start | bytes 3145736 | tf_op jit(solution)/shard_map/ppermute | solution.py:789
  217.1 16.3 %all-to-all-start.5 = ((bf16[8,128,256]{2,1,0:T(8,128)(2,1)}), bf16[8,128,256]{2,1,0:T(8,128)(2,1)S(1)}, u32[]{:S(2)}, u32[]{:S(2)}) async-start(bf16[8,128,256]{2,1,0:T(8,128)(2,1)} %get-tuple-element.156), calls=%async_computation.6 | async-start | bytes 1048576 | tf_op jit(solution)/shard_map/all_to_all | solution.py:862
  220.9 49.8 %collective-permute-start.31 = (bf16[4,128,1024]{2,1,0:T(8,128)(2,1)S(1)}, bf16[4,128,1024]{2,1,0:T(8,128)(2,1)}, u32[]{:S(2)}, u32[]{:S(2)}) collective-permute-start(bf16[4,128,1024]{2,1,0:T(8,128)(2,1)S(1)} %copy-done.10), channel_id=1, source_target_pairs={{0,4},{4,0},{8,12},{12,8},{16,20},{20,16},{24,28},{28,24},{1,5},{5... | collective-permute-start | bytes 3145736 | tf_op jit(solution)/shard_map/ppermute | solution.py:789
  227.0 49.3 %collective-permute-start.23 = (bf16[4,128,1024]{2,1,0:T(8,128)(2,1)}, bf16[4,128,1024]{2,1,0:T(8,128)(2,1)S(1)}, u32[]{:S(2)}, u32[]{:S(2)}) collective-permute-start(bf16[4,128,1024]{2,1,0:T(8,128)(2,1)} %get-tuple-element.134), channel_id=1, source_target_pairs={{0,4},{4,0},{8,12},{12,8},{16,20},{20,16},{24,28},{28,24},{1,5},{5... | collective-permute-start | bytes 3145736 | tf_op jit(solution)/shard_map/ppermute | solution.py:789
  229.9 9.3 %collective-permute-start.25 = (bf16[128,1024]{1,0:T(8,128)(2,1)}, bf16[128,1024]{1,0:T(8,128)(2,1)S(1)}, u32[]{:S(2)}, u32[]{:S(2)}) collective-permute-start(bf16[128,1024]{1,0:T(8,128)(2,1)} %get-tuple-element.142), channel_id=1, source_target_pairs={{0,8},{4,12},{8,0},{12,4},{16,24},{20,28},{24,16},{28,20},{1,9},{5... | collective-permute-start | bytes 786440 | tf_op jit(solution)/shard_map/ppermute | solution.py:789
  231.8 15.5 %collective-permute-start.26 = (bf16[128,1024]{1,0:T(8,128)(2,1)}, bf16[128,1024]{1,0:T(8,128)(2,1)}, u32[]{:S(2)}, u32[]{:S(2)}) collective-permute-start(bf16[128,1024]{1,0:T(8,128)(2,1)} %get-tuple-element.143), channel_id=1, source_target_pairs={{0,16},{4,20},{8,24},{12,28},{16,0},{20,4},{24,8},{28,12},{1,17},{... | collective-permute-start | bytes 786440 | tf_op jit(solution)/shard_map/ppermute | solution.py:789
  233.3 14.0 %collective-permute-start.27 = (bf16[128,1024]{1,0:T(8,128)(2,1)}, bf16[128,1024]{1,0:T(8,128)(2,1)}, u32[]{:S(2)}, u32[]{:S(2)}) collective-permute-start(bf16[128,1024]{1,0:T(8,128)(2,1)} %get-tuple-element.144), channel_id=1, source_target_pairs={{0,24},{4,28},{8,16},{12,20},{16,8},{20,12},{24,0},{28,4},{1,25},{... | collective-permute-start | bytes 786440 | tf_op jit(solution)/shard_map/ppermute | solution.py:789
  234.2 21.8 %all-to-all-start.7 = ((bf16[8,32,768]{2,1,0:T(8,128)(2,1)}), bf16[8,32,768]{2,1,0:T(8,128)(2,1)S(1)}, u32[]{:S(2)}, u32[]{:S(2)}) async-start(bf16[8,32,768]{2,1,0:T(8,128)(2,1)} %bitcast.57), calls=%async_computation.9 | async-start | bytes 786432 | tf_op jit(solution)/shard_map/all_to_all | solution.py:862
  238.3 95.2 %all-gather.10.cloned.1.call-start = ((), (), s32[]{:S(2)}) async-start(), calls=%async_computation.14 | async-start | bytes 1966080 | tf_op jit(solution)/shard_map/all_gather | solution.py:961
  239.2 43.9 %collective-permute-start.35 = (bf16[8,128,256]{2,1,0:T(8,128)(2,1)}, bf16[8,128,256]{2,1,0:T(8,128)(2,1)S(1)}, u32[]{:S(2)}, u32[]{:S(2)}) collective-permute-start(bf16[8,128,256]{2,1,0:T(8,128)(2,1)} %get-tuple-element.159), channel_id=1, source_target_pairs={{0,1},{3,2},{4,5},{7,6},{8,9},{11,10},{12,13},{15,14},{16,17},{19,... | collective-permute-start | bytes 1572872 | tf_op jit(solution)/shard_map/ppermute | solution.py:817
  255.4 3.7 %collective-permute-start.42 = (f32[17,128]{1,0:T(8,128)S(1)}, f32[17,128]{1,0:T(8,128)S(1)}, u32[]{:S(2)}, u32[]{:S(2)}) collective-permute-start(f32[17,128]{1,0:T(8,128)S(1)} %bitcast_add_fusion), channel_id=1, source_target_pairs={{0,8},{4,12},{8,0},{12,4},{16,24},{20,28},{24,16},{28,20},{1,9},{5... | collective-permute-start | bytes 26120 | tf_op jit(solution)/shard_map/ppermute | solution.py:789
  259.1 4.9 %collective-permute-start.43 = (f32[17,128]{1,0:T(8,128)S(1)}, f32[17,128]{1,0:T(8,128)S(1)}, u32[]{:S(2)}, u32[]{:S(2)}) collective-permute-start(f32[17,128]{1,0:T(8,128)S(1)} %fusion.2), channel_id=1, source_target_pairs={{0,16},{4,20},{8,24},{12,28},{16,0},{20,4},{24,8},{28,12},{1,17},{... | collective-permute-start | bytes 26120 | tf_op jit(solution)/shard_map/ppermute | solution.py:789
  264.0 3.7 %collective-permute-start.44 = (f32[17,128]{1,0:T(8,128)S(1)}, f32[17,128]{1,0:T(8,128)S(1)}, u32[]{:S(2)}, u32[]{:S(2)}) collective-permute-start(f32[17,128]{1,0:T(8,128)S(1)} %add.75), channel_id=1, source_target_pairs={{0,1},{1,0},{2,3},{3,2},{4,5},{5,4},{6,7},{7,6},{8,9},{9,8},{10,11... | collective-permute-start | bytes 26120 | tf_op jit(solution)/shard_map/ppermute | solution.py:839
  267.7 12.3 %collective-permute-start.45 = (f32[17,128]{1,0:T(8,128)S(1)}, f32[17,128]{1,0:T(8,128)S(1)}, u32[]{:S(2)}, u32[]{:S(2)}) collective-permute-start(f32[17,128]{1,0:T(8,128)S(1)} %add.76), channel_id=1, source_target_pairs={{0,2},{1,3},{2,0},{3,1},{4,6},{5,7},{6,4},{7,5},{8,10},{9,11},{10,... | collective-permute-start | bytes 26120 | tf_op jit(solution)/shard_map/ppermute | solution.py:839
  273.5 16.9 %collective-permute-start.32 = (bf16[128,1024]{1,0:T(8,128)(2,1)}, bf16[128,1024]{1,0:T(8,128)(2,1)}, u32[]{:S(2)}, u32[]{:S(2)}) collective-permute-start(bf16[128,1024]{1,0:T(8,128)(2,1)} %get-tuple-element.151), channel_id=1, source_target_pairs={{0,8},{4,12},{8,0},{12,4},{16,24},{20,28},{24,16},{28,20},{1,9},{5... | collective-permute-start | bytes 786440 | tf_op jit(solution)/shard_map/ppermute | solution.py:789
  274.8 17.2 %collective-permute-start.33 = (bf16[128,1024]{1,0:T(8,128)(2,1)}, bf16[128,1024]{1,0:T(8,128)(2,1)}, u32[]{:S(2)}, u32[]{:S(2)}) collective-permute-start(bf16[128,1024]{1,0:T(8,128)(2,1)} %get-tuple-element.152), channel_id=1, source_target_pairs={{0,16},{4,20},{8,24},{12,28},{16,0},{20,4},{24,8},{28,12},{1,17},{... | collective-permute-start | bytes 786440 | tf_op jit(solution)/shard_map/ppermute | solution.py:789
  276.3 17.2 %collective-permute-start.34 = (bf16[128,1024]{1,0:T(8,128)(2,1)}, bf16[128,1024]{1,0:T(8,128)(2,1)}, u32[]{:S(2)}, u32[]{:S(2)}) collective-permute-start(bf16[128,1024]{1,0:T(8,128)(2,1)} %get-tuple-element.153), channel_id=1, source_target_pairs={{0,24},{4,28},{8,16},{12,20},{16,8},{20,12},{24,0},{28,4},{1,25},{... | collective-permute-start | bytes 786440 | tf_op jit(solution)/shard_map/ppermute | solution.py:789
  280.0 9.4 %collective-permute-start.38 = (bf16[128,1024]{1,0:T(8,128)(2,1)S(1)}, bf16[128,1024]{1,0:T(8,128)(2,1)S(1)}, u32[]{:S(2)}, u32[]{:S(2)}) collective-permute-start(bf16[128,1024]{1,0:T(8,128)(2,1)S(1)} %copy-done.29), channel_id=1, source_target_pairs={{0,1},{3,2},{4,5},{7,6},{8,9},{11,10},{12,13},{15,14},{16,17},{19,... | collective-permute-start | bytes 786440 | tf_op jit(solution)/shard_map/ppermute | solution.py:817
  283.3 13.5 %collective-permute-start.36 = (bf16[8,128,256]{2,1,0:T(8,128)(2,1)S(1)}, bf16[8,128,256]{2,1,0:T(8,128)(2,1)S(1)}, u32[]{:S(2)}, u32[]{:S(2)}) collective-permute-start(bf16[8,128,256]{2,1,0:T(8,128)(2,1)S(1)} %add_convert_fusion.1), channel_id=1, source_target_pairs={{1,2},{2,1},{5,6},{6,5},{9,10},{10,9},{13,14},{14,13},{17,18},{18,... | collective-permute-start | bytes 1572872 | tf_op jit(solution)/shard_map/ppermute | solution.py:821
  289.4 10.2 %collective-permute-start.28 = (bf16[128,1024]{1,0:T(8,128)(2,1)}, bf16[128,1024]{1,0:T(8,128)(2,1)S(1)}, u32[]{:S(2)}, u32[]{:S(2)}) collective-permute-start(bf16[128,1024]{1,0:T(8,128)(2,1)} %get-tuple-element.147), channel_id=1, source_target_pairs={{0,8},{4,12},{8,0},{12,4},{16,24},{20,28},{24,16},{28,20},{1,9},{5... | collective-permute-start | bytes 786440 | tf_op jit(solution)/shard_map/ppermute | solution.py:789
  290.4 9.2 %collective-permute-start.29 = (bf16[128,1024]{1,0:T(8,128)(2,1)}, bf16[128,1024]{1,0:T(8,128)(2,1)S(1)}, u32[]{:S(2)}, u32[]{:S(2)}) collective-permute-start(bf16[128,1024]{1,0:T(8,128)(2,1)} %get-tuple-element.148), channel_id=1, source_target_pairs={{0,16},{4,20},{8,24},{12,28},{16,0},{20,4},{24,8},{28,12},{1,17},{... | collective-permute-start | bytes 786440 | tf_op jit(solution)/shard_map/ppermute | solution.py:789
  292.0 8.7 %collective-permute-start.30 = (bf16[128,1024]{1,0:T(8,128)(2,1)}, bf16[128,1024]{1,0:T(8,128)(2,1)S(1)}, u32[]{:S(2)}, u32[]{:S(2)}) collective-permute-start(bf16[128,1024]{1,0:T(8,128)(2,1)} %get-tuple-element.149), channel_id=1, source_target_pairs={{0,24},{4,28},{8,16},{12,20},{16,8},{20,12},{24,0},{28,4},{1,25},{... | collective-permute-start | bytes 786440 | tf_op jit(solution)/shard_map/ppermute | solution.py:789
  293.6 4.7 %collective-permute-start.39 = (bf16[128,1024]{1,0:T(8,128)(2,1)S(1)}, bf16[128,1024]{1,0:T(8,128)(2,1)S(1)}, u32[]{:S(2)}, u32[]{:S(2)}) collective-permute-start(bf16[128,1024]{1,0:T(8,128)(2,1)S(1)} %add_convert_fusion.3), channel_id=1, source_target_pairs={{1,2},{2,1},{5,6},{6,5},{9,10},{10,9},{13,14},{14,13},{17,18},{18,... | collective-permute-start | bytes 786440 | tf_op jit(solution)/shard_map/ppermute | solution.py:821
  296.9 35.7 %collective-permute-start.37 = (bf16[8,128,256]{2,1,0:T(8,128)(2,1)S(1)}, bf16[8,128,256]{2,1,0:T(8,128)(2,1)S(1)}, u32[]{:S(2)}, u32[]{:S(2)}) collective-permute-start(bf16[8,128,256]{2,1,0:T(8,128)(2,1)S(1)} %add_convert_fusion), channel_id=1, source_target_pairs={{1,0},{2,3},{5,4},{6,7},{9,8},{10,11},{13,12},{14,15},{17,16},{18,... | collective-permute-start | bytes 1572872 | tf_op jit(solution)/shard_map/ppermute | solution.py:826
  298.3 33.6 %collective-permute-start.40 = (bf16[128,1024]{1,0:T(8,128)(2,1)S(1)}, bf16[128,1024]{1,0:T(8,128)(2,1)S(1)}, u32[]{:S(2)}, u32[]{:S(2)}) collective-permute-start(bf16[128,1024]{1,0:T(8,128)(2,1)S(1)} %add_convert_fusion.2), channel_id=1, source_target_pairs={{1,0},{2,3},{5,4},{6,7},{9,8},{10,11},{13,12},{14,15},{17,16},{18,... | collective-permute-start | bytes 786440 | tf_op jit(solution)/shard_map/ppermute | solution.py:826
  (51 other events, 229.9 us)
Sparse Core Ops, SparseCore 0:
  31.8 39.0 all-gather.5
  136.9 44.6 reduce-scatter.4
  184.0 34.5 reduce-scatter.2
  220.1 53.0 all-gather.7
  275.3 48.7 all-gather.9

commit v3 on v2

--- a/solution.py
+++ b/solution.py
@@ -368,6 +368,51 @@
         return outputs[0] if len(shapes) == 1 else outputs
 
     return apply
+
+
+def moving(kernel, out_shape, scratch_shapes, copies, token=False):
+    anywhere = pl.BlockSpec(memory_space=pl.ANY)
+    shapes = tuple(out_shape) + ((array(jnp.float32, 8, LANES),) if token else ())
+    specs = (anywhere,) * len(out_shape) + ((pl.BlockSpec(memory_space=pltpu.VMEM),) if token else ())
+
+    def apply(*operands, smem=0, tokens=()):
+        given = len(operands)
+        results = given + len(tokens) + len(shapes)
+
+        def body(*refs):
+            if token:
+                refs[results - 1][...] = jnp.zeros((8, LANES), jnp.float32)
+            kernel(*refs[:given], *refs[given + len(tokens) : results - token], *refs[results:])
+
+        outputs = pl.pallas_call(
+            body,
+            out_shape=shapes,
+            in_specs=[pl.BlockSpec(memory_space=pltpu.SMEM)] * smem + [anywhere] * (given - smem + len(tokens)),
+            out_specs=specs,
+            scratch_shapes=[*scratch_shapes, pltpu.SemaphoreType.DMA((copies,))],
+            compiler_params=pltpu.CompilerParams(vmem_limit_bytes=VMEM_LIMIT),
+        )(*operands, *tokens)
+        return outputs[0] if len(shapes) == 1 else outputs
+
+    return apply
+
+
+class Copies:
+    def __init__(self, sems):
+        self.sems, self.used, self.open = sems, 0, []
+
+    def start(self, source, target):
+        copy = pltpu.make_async_copy(source, target, self.sems.at[self.used])
+        self.used += 1
+        copy.start()
+        return copy
+
+    def store(self, source, target):
+        self.open.append(self.start(source, target))
+
+    def finish(self):
+        for copy in self.open:
+            copy.wait()
 
 
 def after(values, *tokens):
@@ -568,7 +613,7 @@
 
 def residual_kernel(me_ref, x_ref, *refs):
     attn_refs = refs[:KV_HEADS]
-    out_weight_ref, gain_ref, residual_ref, attn_own_ref, normed_ref, attn_scratch, scratch = refs[KV_HEADS:]
+    out_weight_ref, gain_ref, residual_ref, normed_ref, attn_scratch, scratch = refs[KV_HEADS:]
     total, width = x_ref.shape
     tok_rows = total // KV_HEADS
     for partner in range(KV_HEADS):
@@ -580,7 +625,6 @@
         factor = lax.rsqrt(jnp.mean(residual * residual, axis=-1, keepdims=True) + EPSILON)
         normed_ref[rows, :] = (residual * factor * gain_ref[...]).astype(jnp.bfloat16)
     residual_ref[...] = scratch[block_rows(me_ref, 0, tok_rows), :]
-    attn_own_ref[...] = attn_scratch[block_rows(me_ref, 0, tok_rows), :]
 
 
 def unit_share(gate, up, upstream):
@@ -591,34 +635,64 @@
 
 
 def first_units_kernel(me_ref, slot_ref, normed_ref, *refs):
-    dout_refs = refs[:KV_HEADS]
-    own_ref, other_ref, dout_ref, weight_ref, hidden_ref, dgate_up_ref = refs[KV_HEADS:]
-    total = normed_ref.shape[0]
-    block = hidden_ref.shape[1] - LANES
-    units = 2 * block + LANES
-    depth, half = 2 * own_ref.shape[1], own_ref.shape[1]
+    dout_refs, refs = refs[:KV_HEADS], refs[KV_HEADS:]
+    halves, outs, refs = refs[:2], refs[2:7], refs[7:]
+    dout_out, weight_out, hidden_out, dgate_out, grads_out = outs
+    normed, dout, weight, hidden, dgate, grads, sems = refs
+    copies = Copies(sems)
+    total, width = normed.shape
+    half = halves[0].shape[1]
+    slots, _, rows_each, _ = grads.shape
+    owners = ROW_BLOCK // (slots * rows_each)
+    block = hidden.shape[1] - LANES
+    units = dgate.shape[1]
     odd = jnp.bitwise_and(slot_ref[0], 1)
+    starts = range(0, total, ROW_BLOCK)
+    loads = []
     for index in range(KV_HEADS):
-        weight_ref[pl.ds(pl.multiple_of(index * depth + odd * half, half), half), :] = own_ref[index]
-        weight_ref[pl.ds(pl.multiple_of(index * depth + (1 - odd) * half, half), half), :] = other_ref[index]
-    for partner in range(KV_HEADS):
-        dout_ref[block_rows(me_ref, partner, depth), :] = dout_refs[partner][...]
+        for place, ref in ((odd, halves[0]), (1 - odd, halves[1])):
+            rows = pl.ds(pl.multiple_of((2 * index + place) * half, half), half)
+            loads.append(copies.start(ref.at[index], weight.at[rows, :]))
+    normed_loads = [copies.start(normed_ref.at[pl.ds(start, ROW_BLOCK), :], normed.at[pl.ds(start, ROW_BLOCK), :]) for start in starts]
+    dout_loads = [
+        copies.start(dout_refs[partner], dout.at[block_rows(me_ref, partner, 2 * half), :]) for partner in range(KV_HEADS)
+    ]
+    for load in loads:
+        load.wait()
+    copies.store(weight, weight_out)
     low = lane_is_low((ROW_BLOCK, LANES))
-    for start in range(0, total, ROW_BLOCK):
+    for step, start in enumerate(starts):
         rows = pl.ds(start, ROW_BLOCK)
-        both = dot_nn(normed_ref[rows, :], weight_ref[:, :units])
-        dhidden = dot_nn(dout_ref[rows, :], weight_ref[:, units:])
-        hidden, dgate, dup = unit_share(both[:, :block], both[:, block : 2 * block], dhidden[:, :block])
+        normed_loads[step].wait()
+        both = dot_nn(normed[rows, :], weight[:, :units])
+        if step == 0:
+            for load in dout_loads:
+                load.wait()
+            copies.store(dout, dout_out)
+        dhidden = dot_nn(dout[rows, :], weight[:, units:])
+        share = unit_share(both[:, :block], both[:, block : 2 * block], dhidden[:, :block])
         rest = both[:, 2 * block :]
         swapped = pltpu.roll(rest, HEAD_DIM, 1)
-        rest_hidden, rest_dgate, rest_dup = unit_share(
-            jnp.where(low, rest, swapped), jnp.where(low, swapped, rest), dhidden[:, block:]
-        )
-        hidden_ref[rows, :block] = hidden.astype(jnp.bfloat16)
-        hidden_ref[rows, block:] = jnp.where(low, rest_hidden, 0.0).astype(jnp.bfloat16)
-        dgate_up_ref[rows, :block] = dgate.astype(jnp.bfloat16)
-        dgate_up_ref[rows, block : 2 * block] = dup.astype(jnp.bfloat16)
-        dgate_up_ref[rows, 2 * block :] = jnp.where(low, rest_dgate, rest_dup).astype(jnp.bfloat16)
+        rest_share = unit_share(jnp.where(low, rest, swapped), jnp.where(low, swapped, rest), dhidden[:, block:])
+        hidden[rows, :block] = share[0].astype(jnp.bfloat16)
+        hidden[rows, block:] = jnp.where(low, rest_share[0], 0.0).astype(jnp.bfloat16)
+        dgate[rows, :block] = share[1].astype(jnp.bfloat16)
+        dgate[rows, block : 2 * block] = share[2].astype(jnp.bfloat16)
+        dgate[rows, 2 * block :] = jnp.where(low, rest_share[1], rest_share[2]).astype(jnp.bfloat16)
+    copies.store(hidden, hidden_out)
+    copies.store(dgate, dgate_out)
+    for step, start in enumerate(range(0, width, ROW_BLOCK)):
+        lanes = pl.ds(start, ROW_BLOCK)
+        gate_up = dot_tn(normed[:, lanes], dgate[...]).astype(jnp.bfloat16)
+        down = dot_tn(dout[:, lanes], hidden[...])[:, : block + HEAD_DIM].astype(jnp.bfloat16)
+        for owner in range(owners):
+            for slot in range(slots):
+                piece = (owner * slots + slot) * rows_each
+                grads[slot, step * owners + owner, :, :units] = gate_up[piece : piece + rows_each]
+                grads[slot, step * owners + owner, :, units:] = down[piece : piece + rows_each]
+        done = pl.ds(step * owners, owners)
+        copies.store(grads.at[:, done], grads_out.at[:, done])
+    copies.finish()
 
 
 def second_units_kernel(
@@ -680,8 +754,11 @@
     return (first + second) + (third + fourth)
 
 
-def four_sum_kernel(*refs):
-    refs[4][...] = four_sum([ref[...] for ref in refs[:4]]).astype(refs[4].dtype)
+def join_kernel(left_ref, *refs):
+    joined_ref = refs[4]
+    split = left_ref.shape[2]
+    joined_ref[:, :, :split] = left_ref[...]
+    joined_ref[:, :, split:] = four_sum([ref[...] for ref in refs[:4]]).astype(joined_ref.dtype)
 
 
 def residual_back_kernel(
@@ -722,47 +799,49 @@
     terms_ref[...] = terms
 
 
-def projection_grads_kernel(normed_ref, dproj_ref, grads_ref):
-    width = normed_ref.shape[1]
-    depth = grads_ref.shape[1]
-    for start in range(0, width, ROW_BLOCK):
-        blocks = pl.ds(start // depth, ROW_BLOCK // depth)
-        grads = dot_tn(normed_ref[:, pl.ds(start, ROW_BLOCK)], dproj_ref[...]).astype(jnp.bfloat16)
-        grads_ref[blocks] = grads.reshape(-1, depth, 2 * LANES)
-
-
-def out_grads_kernel(me_ref, dbranch_ref, attn_ref, own_ref, other_ref):
-    width = dbranch_ref.shape[1]
-    for start in range(0, width, ROW_BLOCK):
-        grads = dot_tn(dbranch_ref[:, pl.ds(start, ROW_BLOCK)], attn_ref[...])
-        store_pair(me_ref, start // ROW_BLOCK, grads, own_ref, other_ref)
-
-
-def rows_kernel(attn_ref, attn_out_ref, first_ref, second_ref, *out_refs):
+def attention_weights_kernel(me_ref, slot_ref, normed_ref, dproj_ref, attn_low_ref, *refs):
+    dbranch_refs, quarters, grads, dbranch = refs[:KV_HEADS], refs[KV_HEADS:-2], refs[-2], refs[-1]
+    slots, _, rows_each, _ = grads.shape
+    tok_rows = dbranch_refs[0].shape[0]
+    for partner in range(KV_HEADS):
+        dbranch[block_rows(me_ref, partner, tok_rows), :] = dbranch_refs[partner][...]
+    for start in range(0, normed_ref.shape[1], ROW_BLOCK):
+        lanes = pl.ds(start, ROW_BLOCK)
+        proj = dot_tn(normed_ref[:, lanes], dproj_ref[...]).astype(jnp.bfloat16)
+        out = dot_tn(dbranch[:, lanes], attn_low_ref[...]).astype(jnp.bfloat16)
+        for piece in range(0, ROW_BLOCK, rows_each):
+            owner, slot = divmod((start + piece) // rows_each, slots)
+            grads[slot, owner, :, : 2 * LANES] = proj[piece : piece + rows_each]
+            grads[slot, owner, :, 2 * LANES :] = out[piece : piece + rows_each]
+    for partner, quarter in enumerate(quarters):
+        quarter[...] = grads[jnp.bitwise_xor(slot_ref[0], partner)]
+
+
+def rows_kernel(first_ref, second_ref, *out_refs):
     query_ref, key_ref, value_ref, out_ref, gate_ref, up_ref, down_ref = out_refs
     f32 = jnp.float32
-    block = second_ref.shape[3] // 3
+    block = (first_ref.shape[3] - LANES - HEAD_DIM) // 3
     cut = KV_HEADS * block
-    out_ref[...] = attn_out_ref[...].astype(f32)
-    for index in range(KV_HEADS):
-        query_ref[:, pl.ds(index * LANES, LANES)] = attn_ref[index, :, :LANES].astype(f32)
-    low = lane_is_low((attn_ref.shape[1], LANES))
-    for index in range(0, KV_HEADS, 2):
-        lanes = pl.ds(index * HEAD_DIM, LANES)
-        even = attn_ref[index, :, LANES : 2 * LANES].astype(f32)
-        odd = attn_ref[index + 1, :, LANES : 2 * LANES].astype(f32)
-        key_ref[:, lanes] = jnp.where(low, even, pair_swap(odd))
-        value_ref[:, lanes] = jnp.where(low, pair_swap(even), odd)
-    low = lane_is_low((first_ref.shape[2], LANES))
+    heads = 3 * block
+    rows_each = first_ref.shape[2]
+    low = lane_is_low((rows_each, LANES))
     for slot in range(first_ref.shape[0]):
-        rows = pl.ds(slot * first_ref.shape[2], first_ref.shape[2])
+        rows = pl.ds(slot * rows_each, rows_each)
         for index in range(KV_HEADS):
             for place, ref in enumerate((gate_ref, up_ref, down_ref)):
                 start = place * block + (LANES if place == 2 else 0)
                 ref[rows, pl.ds(index * block, block)] = first_ref[slot, index, :, start : start + block].astype(f32)
                 start = place * block
                 ref[rows, pl.ds(cut + index * block, block)] = second_ref[slot, index, :, start : start + block].astype(f32)
+            lanes = pl.ds(index * LANES, LANES)
+            query_ref[rows, lanes] = second_ref[slot, index, :, heads : heads + LANES].astype(f32)
+            out_ref[rows, lanes] = second_ref[slot, index, :, heads + 2 * LANES :].astype(f32)
         for index in range(0, KV_HEADS, 2):
+            lanes = pl.ds(index * HEAD_DIM, LANES)
+            even = second_ref[slot, index, :, heads + LANES : heads + 2 * LANES].astype(f32)
+            odd = second_ref[slot, index + 1, :, heads + LANES : heads + 2 * LANES].astype(f32)
+            key_ref[rows, lanes] = jnp.where(low, even, pair_swap(odd))
+            value_ref[rows, lanes] = jnp.where(low, pair_swap(even), odd)
             lanes = pl.ds(2 * cut + index * HEAD_DIM, LANES)
             even = first_ref[slot, index, :, 2 * block : 2 * block + LANES].astype(f32)
             odd = first_ref[slot, index + 1, :, 2 * block : 2 * block + LANES].astype(f32)
@@ -803,41 +882,24 @@
 
 
 def sum_partners(me, own, other, *tokens):
-    parts = call(add_kernel, (array(own.dtype, *own.shape[1:]),) * own.shape[0])(
+    *parts, added = call(add_kernel, (array(own.dtype, *own.shape[1:]),) * own.shape[0], token=True)(
         me, own, to_partner(other, 1), smem=1, tokens=tokens
     )
-    return [parts[0]] + [to_partner(parts[i], 2 * i) for i in (1, 2, 3)]
-
-
-def add(left, right):
-    return (left.astype(jnp.float32) + right.astype(jnp.float32)).astype(left.dtype)
-
-
-def inward(part):
-    return lax.ppermute(part, "slot", [(0, 1), (3, 2)])
-
-
-def across(part):
-    return lax.ppermute(part, "slot", [(1, 2), (2, 1)])
-
-
-def outward(total):
-    slot = lax.axis_index("slot")
-    return jnp.where((slot == 1) | (slot == 2), total, lax.ppermute(total, "slot", [(1, 0), (2, 3)]))
-
-
-def sum_slots(*parts):
-    parts = [add(part, inward(part)) for part in parts]
-    parts = [add(part, across(part)) for part in parts]
-    return [outward(part) for part in parts]
+    return [parts[0]] + [to_partner(parts[i], 2 * i) for i in (1, 2, 3)], added
+
+
+def to_slot(block, partner):
+    return lax.ppermute(block, "slot", [(i, i ^ partner) for i in range(SLOTS_BY_HEADS)])
+
+
+def send_quarters(quarters):
+    return [quarters[0]] + [to_slot(quarters[partner], partner) for partner in (1, 2, 3)]
 
 
 def sum_devices(values):
     for partner in (1, 2, 4):
         values = values + to_partner(values, partner)
-    for partner in (1, 2):
-        values = values + lax.ppermute(values, "slot", [(i, i ^ partner) for i in range(SLOTS_BY_HEADS)])
-    return values
+    return four_sum([values] + [to_slot(values, partner) for partner in (1, 2, 3)])
 
 
 def heads_body(
@@ -871,7 +933,7 @@
         (array(bf16, count, depth // 2, 3 * block + 2 * LANES), array(bf16, count, depth, 3 * block)),
     )(slot, gate_weight, up_weight, down_weight, smem=1, tokens=(packed,))
     upstream = jnp.where(row_valid, out_grad[0], jnp.zeros_like(out_grad[0]))
-    first_owned, out_weight = after((first_owned, out_weight), *x_parts, attn_weight)
+    (first_owned,) = after((first_owned,), *x_parts, attn_weight)
     first_own = swap(first_owned)
     out_full = lax.all_gather(out_weight, "seq", axis=0, tiled=True)
 
@@ -888,27 +950,48 @@
         token=True,
     )(lengths, me, *x_parts, attn_weight, attn_norm[None], q_gain, k_gain, cosine, sine, smem=2)
 
-    attn_parts = gather_cores(gather_chips(attn_low))
-    first_own, upstream = after((first_own, upstream), attended)
-    first_other = lax.ppermute(first_own, "slot", [(i, i ^ 1) for i in range(SLOTS_BY_HEADS)])
+    attn_parts = gather_chips(attn_low)
+    (second_owned,) = after((second_owned,), attended)
+    second_weight = swap(second_owned).reshape(width, -1)
+    first_own, upstream = after((first_own, upstream), *attn_parts[1:])
+    first_other = to_slot(first_own, 1)
     dout_parts = gather_chips(upstream)
-    (second_owned,) = after((second_owned,), *attn_parts, first_own)
-    residual, attn_own, normed_two, normed_ready = call(
+    attn_parts = gather_cores(attn_parts)
+    residual, normed_two, normed_ready = call(
         residual_kernel,
-        (array(f32, tok_rows, width), array(bf16, tok_rows, width), array(bf16, total, width)),
+        (array(f32, tok_rows, width), array(bf16, total, width)),
         scratch_shapes=[pltpu.VMEM((total, width), bf16), pltpu.VMEM((total, width), f32)],
         token=True,
     )(me, x_all, *attn_parts, out_full, ffn_norm[None], smem=1, tokens=(second_owned,))
-    second_weight = swap(second_owned).reshape(width, -1)
 
     dout_parts = gather_cores(after(tuple(dout_parts), normed_ready, first_other))
-    dout_all, first_weight, hidden_first, dgate_up_first = call(
+    first_cols, second_cols = 3 * block + 2 * LANES, 3 * block
+    units_first, units_second = 2 * block + LANES, 2 * block
+    halves = (array(bf16, count // 2, tok_rows, width),) * 2
+    quarter = depth // SLOTS_BY_HEADS
+    first_arrays = (
+        array(bf16, total, width), array(bf16, width, first_cols), array(bf16, total, block + LANES),
+        array(bf16, total, units_first), array(bf16, SLOTS_BY_HEADS, count, quarter, first_cols - HEAD_DIM),
+    )
+    dout_all, first_weight, hidden_first, dgate_up_first, first_grads, first_done = moving(
         first_units_kernel,
-        (
-            array(bf16, total, width), array(bf16, width, 3 * block + 2 * LANES), array(bf16, total, block + LANES),
-            array(bf16, total, 2 * block + LANES),
-        ),
-    )(me, slot, normed_two, *dout_parts, first_own, first_other, smem=2)
+        first_arrays,
+        [pltpu.VMEM((total, width), bf16)] + [pltpu.VMEM(shape.shape, shape.dtype) for shape in first_arrays],
+        64,
+        token=True,
+    )(me, slot, normed_two, *dout_parts, first_own, first_other, smem=2, tokens=(second_weight,))
+    first_sums = lax.psum_scatter(
+        first_grads.reshape(width, first_cols - HEAD_DIM), "slot", scatter_dimension=0, tiled=True
+    )
+    hidden_second, dgate_up_second, *normed_two_grad, summed = call(
+        second_units_kernel,
+        (array(bf16, total, block), array(bf16, total, units_second), *halves),
+        token=True,
+    )(
+        me, normed_two, dout_all, first_weight, second_weight, dgate_up_first, smem=1,
+        tokens=(first_done,),
+    )
+
     def unit_grads(hidden, dgate_up, cols, *tokens):
         grads, done = call(unit_grads_kernel, array(bf16, SLOTS_BY_HEADS, count, depth // SLOTS_BY_HEADS, cols), token=True)(
             normed_two, dout_all, hidden, dgate_up, tokens=tokens
@@ -918,15 +1001,8 @@
     def to_owners(sums):
         return swap(sums.reshape(count, -1, sums.shape[1]))
 
-    halves = (array(bf16, count // 2, tok_rows, width),) * 2
-    hidden_second, dgate_up_second, *normed_two_grad, summed = call(
-        second_units_kernel, (array(bf16, total, block), array(bf16, total, 2 * block), *halves), token=True
-    )(me, normed_two, dout_all, first_weight, second_weight, dgate_up_first, smem=1)
-    first_grads, first_sums = unit_grads(
-        hidden_first, dgate_up_first, 3 * block + LANES + HEAD_DIM, summed
-    )
     normed_two_sum = call(add_blocks_kernel, halves[0])(
-        normed_two_grad[0], to_partner(normed_two_grad[1], 1), tokens=(first_grads,)
+        normed_two_grad[0], to_partner(normed_two_grad[1], 1)
     )
     residual_grad, attn_out_low, dattn, ffn_terms, branched = call(
         residual_back_kernel,
@@ -938,34 +1014,41 @@
     )(swap_chips(normed_two_sum), residual, upstream, ffn_norm[None], out_full)
     second_grads, second_sums = unit_grads(hidden_second, dgate_up_second, 3 * block, branched)
     dattn = swap(dattn)
-    dnormed_own, dnormed_other, dproj, terms = call(
+    dbranch_parts = gather_chips(*after((attn_out_low,), dattn))
+    dnormed_own, dnormed_other, dproj, terms, passed = call(
         attention_backward_kernel,
         (*halves, array(bf16, total, 2 * LANES), array(f32, 2, LANES)),
         scratch_shapes=[pltpu.VMEM((total, LANES), f32)] * 3,
+        token=True,
     )(
         lengths, me, dattn.reshape(total, LANES), attn_weight, q_gain, k_gain, cosine, sine, q_proj, kv_proj, q_low, k_pair,
         v_pair, attn, weight_inv, smem=2, tokens=(second_grads,),
     )
-    proj_grads, projected = call(projection_grads_kernel, array(bf16, count, depth, 2 * LANES), token=True)(normed, dproj)
-    proj_part = swap(proj_grads)
+    dbranch_parts = gather_cores(after(tuple(dbranch_parts), passed))
+    *quarters, projected = call(
+        attention_weights_kernel,
+        (array(bf16, count, quarter, 3 * LANES),) * SLOTS_BY_HEADS,
+        scratch_shapes=[pltpu.VMEM((SLOTS_BY_HEADS, count, quarter, 3 * LANES), bf16), pltpu.VMEM((total, width), bf16)],
+        token=True,
+    )(me, slot, normed, dproj, attn_low, *dbranch_parts, smem=2)
+    attention_parts = send_quarters(quarters)
     (first_sums,) = after((first_sums,), projected)
     first_rows = to_owners(first_sums)
     first_all = lax.all_gather(first_rows, "slot", axis=0)
 
-    mixed_halves = call(mixed_kernel, halves)(
-        me, hidden_first, hidden_second, first_weight, second_weight, smem=1, tokens=(projected,)
-    )
-
-    *out_grads, out_ready = call(out_grads_kernel, halves, token=True)(me, attn_out_low, attn_own, smem=1, tokens=(projected,))
-    second_sums, proj_part = after((second_sums, proj_part), out_ready, first_rows)
-    second_all = lax.all_gather(to_owners(second_sums), "slot", axis=0)
-    out_part, out_summed = call(four_sum_kernel, array(bf16, tok_rows, width), token=True)(*sum_partners(me, *out_grads))
-    attn_terms = call(attention_gain_kernel, array(f32, 1, width))(
-        me, x_all, dnormed_own, dnormed_other, smem=1, tokens=(out_summed,)
-    )
-    proj_rows, out_rows = sum_slots(proj_part, out_part)
-    dnormed_parts = sum_partners(me, dnormed_own, dnormed_other, attn_terms)
-    mixed_parts = sum_partners(me, *mixed_halves, attn_terms)
+    dnormed_parts, added = sum_partners(me, dnormed_own, dnormed_other, first_rows)
+    *mixed_halves, mixed_done = call(mixed_kernel, halves, token=True)(
+        me, hidden_first, hidden_second, first_weight, second_weight, smem=1, tokens=(added,)
+    )
+    attn_terms, gained = call(attention_gain_kernel, array(f32, 1, width), token=True)(
+        me, x_all, dnormed_own, dnormed_other, smem=1, tokens=(mixed_done,)
+    )
+    (second_sums,) = after((second_sums,), gained)
+    joined = call(join_kernel, array(bf16, count, quarter, second_cols + 3 * LANES))(
+        second_sums.reshape(count, quarter, second_cols), *attention_parts
+    )
+    second_all = lax.all_gather(swap(joined), "slot", axis=0)
+    mixed_parts, _ = sum_partners(me, *mixed_halves, gained)
     input_grad = call(input_back_kernel, array(bf16, tok_rows, width))(
         *dnormed_parts, tokens[0], residual_grad, attn_norm[None]
     )
@@ -973,7 +1056,7 @@
     mixed = jnp.where(row_valid, result, 0.0).astype(bf16)[None]
     shapes = (query_weight, key_weight, value_weight, out_weight, gate_weight, up_weight, down_weight)
     weight_grads = call(rows_kernel, tuple(array(f32, *weight.shape) for weight in shapes))(
-        proj_rows, out_rows, first_all, second_all
+        first_all, second_all
     )
 
     half = HEAD_DIM

time: 352 us -> 333 us (0.946)
  waiting for transfers between devices: 97.6 us -> 75.2 us
  blocking collectives: 43 us -> 57.9 us
  Pallas kernels: 106 us -> 97.9 us
    ppermute x9 -> x7, waiting for transfers between devices: 36.5 us -> 10.4 us  [to_slot(): lax.ppermute(block, 'slot', [(i, i ^ partner) for i in range(SLOTS_BY_HEA...]
    ppermute x37 -> x40, waiting for transfers between devices: 60.6 us -> 40.4 us  [to_partner(): lax.ppermute(block, 'seq', [(i, i ^ partner) for i in range(KV_HEADS)])]
    pallas_call x21 -> x17, Pallas kernels: 106 us -> 86.3 us  [apply(): pl.pallas_call(whole, out_shape=shapes, in_specs=in_specs, out_specs=(vme...]
    all_gather x1, waiting for transfers between devices: 0.01 us -> 15.7 us  [heads_body(): second_all = lax.all_gather(swap(joined), 'slot', axis=0)]
    all_to_all x2 -> x3, blocking collectives: 24 us -> 38.9 us  [swap(): return lax.all_to_all(blocks, 'seq', 0, 0, tiled=True)]
    pallas_call x0 -> x1, Pallas kernels: none -> 11.6 us  [apply(): pl.pallas_call(body, out_shape=shapes, in_specs=[pl.BlockSpec(memory_spac...]
    all_to_all x5 -> x3, waiting for transfers between devices: 0.45 us -> 7.9 us  [swap(): return lax.all_to_all(blocks, 'seq', 0, 0, tiled=True)]
    all_to_all x5 -> x3, starting transfers between devices: 19.4 us -> 15.1 us  [swap(): return lax.all_to_all(blocks, 'seq', 0, 0, tiled=True)]
  transfers between devices with their start and end apart: 56 -> 55, of which waited for: 23 -> 31; matrix products, arithmetic and copies ran while one was open for 2% -> 2% of each run, Pallas kernels for 24% -> 25%
where the time goes in v3:
time: 333 us; the launch traced here: 327 us
  Pallas kernels  97.9 us (29%)
  waiting for transfers between devices  75.2 us (23%)
  starting transfers between devices  63.8 us (19%)
  blocking collectives  57.9 us (17%)
  between operations  15.1 us (5%)
  local copies, waits for them, and re-layouts  13.7 us (4%)
  other arithmetic  3.36 us (1%)
    pallas_call x17, Pallas kernels, apply(): pl.pallas_call(whole, out_shape=shapes, in_specs=in_specs, out_specs=(vme...  86.3 us
    ppermute x40, waiting for transfers between devices, to_partner(): lax.ppermute(block, 'seq', [(i, i ^ partner) for i in range(KV_HEADS)])  40.4 us
    all_to_all x3, blocking collectives, swap(): return lax.all_to_all(blocks, 'seq', 0, 0, tiled=True)  38.9 us
    ppermute x40, starting transfers between devices, to_partner(): lax.ppermute(block, 'seq', [(i, i ^ partner) for i in range(KV_HEADS)])  26.2 us
    ppermute x7, starting transfers between devices, to_slot(): lax.ppermute(block, 'slot', [(i, i ^ partner) for i in range(SLOTS_BY_HEA...  21.3 us
    all_to_all x1, blocking collectives, swap_chips(): lax.all_to_all(blocks, 'seq', 0, 0, axis_index_groups=cores, tiled=True)  19 us
    all_gather x1, waiting for transfers between devices, heads_body(): second_all = lax.all_gather(swap(joined), 'slot', axis=0)  15.7 us
    all_to_all x3, starting transfers between devices, swap(): return lax.all_to_all(blocks, 'seq', 0, 0, tiled=True)  15.1 us
  transfers between devices with their start and end apart: 55, of which 31 were waited for; matrix products, arithmetic and copies ran while one was open for 2% of the time, Pallas kernels for 25%

profile of v3, /device:TPU:0, one launch (start us, length us, event | category | flops | bytes accessed | tf_op | source)
XLA Modules:
  0.0 327.0 jit_solution(8891872586689949233)
XLA Ops:
  7.9 4.0 %collective-permute-start.5 = (bf16[128,1024]{1,0:T(8,128)(2,1)}, bf16[128,1024]{1,0:T(8,128)(2,1)S(1)}, u32[]{:S(2)}, u32[]{:S(2)}) collective-permute-start(bf16[128,1024]{1,0:T(8,128)(2,1)} %bitcast.48), channel_id=1, source_target_pairs={{0,24},{4,28},{8,16},{12,20},{16,8},{20,12},{24,0},{28,4},{1,25},{... | collective-permute-start | bytes 786440 | tf_op jit(solution)/shard_map/ppermute | solution.py:868
  12.5 2.0 shard_map.255
  14.5 4.1 %all-to-all-start = ((bf16[8,128,256]{2,1,0:T(8,128)(2,1)}), bf16[8,128,256]{2,1,0:T(8,128)(2,1)S(1)}, u32[]{:S(2)}, u32[]{:S(2)}) async-start(bf16[8,128,256]{2,1,0:T(8,128)(2,1)} %get-tuple-element.89), calls=%async_computation | async-start | bytes 1048576 | tf_op jit(solution)/shard_map/all_to_all | solution.py:924
  19.3 6.4 %collective-permute-done.3.refs_6_.refs_5_ = bf16[128,1024]{1,0:T(8,128)(2,1)S(1)} collective-permute-done((bf16[128,1024]{1,0:T(8,128)(2,1)}, bf16[128,1024]{1,0:T(8,128)(2,1)S(1)}, u32[]{:S(2)}, u32[]{:S(2)}) %collective-permute-start.3) | collective-permute-done | bytes 262176 | tf_op jit(solution)/shard_map/ppermute | solution.py:868
  25.7 2.4 collective-permute-done.1.refs_4_.refs_3_
  28.1 3.8 %shard_map.257 = (bf16[8,64,1024]{2,1,0:T(8,128)(2,1)}, bf16[8,128,768]{2,1,0:T(8,128)(2,1)}) custom-call(s32[1]{0:T(128)} %bitcast.8.refs_0_.refs_1_, bf16[128,4608]{1,0:T(8,128)(2,1)} %refs_1_.3, bf16[128,4608]{1,0:T(8,128)(2,1)} %refs_2_.3, bf16[128,4608]{1,0:T(8,128)(2,1)} %refs_3_.1, f32[8,128]{1,0:T(8,128)} %get-tuple-element.92.refs_4_), custom_call_target="tpu_custom_call" | custom-call | tf_op jit(solution)/shard_map/pallas_call | solution.py:360
  33.5 3.8 %all-to-all-start.1 = ((bf16[8,64,1024]{2,1,0:T(8,128)(2,1)}), bf16[8,64,1024]{2,1,0:T(8,128)(2,1)S(1)}, u32[]{:S(2)}, u32[]{:S(2)}) async-start(bf16[8,64,1024]{2,1,0:T(8,128)(2,1)} %shard_map.260), calls=%async_computation.1 | async-start | bytes 2097152 | tf_op jit(solution)/shard_map/all_to_all | solution.py:924
  38.6 6.9 %shard_map.256 = (bf16[1024,1024]{1,0:T(8,128)(2,1)}, bf16[1024,1024]{1,0:T(8,128)(2,1)}, f32[1024,128]{1,0:T(8,128)}, f32[1024,128]{1,0:T(8,128)}, bf16[1024,12...) custom-call(s32[1]{0:T(128)} %copy.59.refs_0_, ...), custom_call_target="tpu_custom_call" | custom-call | tf_op jit(solution)/shard_map/pallas_call | solution.py:360
  45.5 2.9 collective-permute-start.12
  49.1 7.3 %all-to-all-done.1.refs_0_ = bf16[8,64,1024]{2,1,0:T(8,128)(2,1)S(1)} async-done(((bf16[8,64,1024]{2,1,0:T(8,128)(2,1)}), bf16[8,64,1024]{2,1,0:T(8,128)(2,1)S(1)}, u32[]{:S(2)}, u32[]{:S(2)}) %all-to-all-start.1) | async-done | bytes 1048608 | tf_op jit(solution)/shard_map/all_to_all | solution.py:924
  56.4 7.2 %all-to-all-start.2 = ((bf16[8,128,768]{2,1,0:T(8,128)(2,1)}), bf16[8,128,768]{2,1,0:T(8,128)(2,1)S(1)}, u32[]{:S(2)}, u32[]{:S(2)}) async-start(bf16[8,128,768]{2,1,0:T(8,128)(2,1)} %shard_map.258.refs_12_), calls=%async_computation.2 | async-start | bytes 3145728 | tf_op jit(solution)/shard_map/all_to_all | solution.py:924
  64.2 1.8 bitcast_select_fusion.refs_1_
  67.8 1.7 collective-permute-start.17
  72.7 1.6 collective-permute-start.15
  75.5 1.7 copy.48.refs_0_
  77.2 7.5 %shard_map.259 = (f32[128,1024]{1,0:T(8,128)}, bf16[1024,1024]{1,0:T(8,128)(2,1)}, f32[8,128]{1,0:T(8,128)}) custom-call(s32[1]{0:T(128)} %bitcast.1.refs_1_.refs_0_, bf16[1024,1024]{1,0:T(8,128)(2,1)} %get-tuple-element.90.refs_1_, bf16[1024,128]{1,0:T(8,128)(2,1)} %get-tuple-element.91.refs_2_.refs_4_, bf16[1024,128]{1,0:T(8,128)(2,1)} %copy-done.25, ...), custom_call_target="tpu_custom_call" | custom-call | tf_op jit(solution)/shard_map/pallas_call | solution.py:360
  84.7 6.1 %collective-permute-done.16.refs_3_ = bf16[128,1024]{1,0:T(8,128)(2,1)S(1)} collective-permute-done((bf16[128,1024]{1,0:T(8,128)(2,1)}, bf16[128,1024]{1,0:T(8,128)(2,1)S(1)}, u32[]{:S(2)}, u32[]{:S(2)}) %collective-permute-start.16) | collective-permute-done | bytes 262176 | tf_op jit(solution)/shard_map/ppermute | solution.py:868
  90.8 4.2 %collective-permute-done.15.refs_2_ = bf16[128,1024]{1,0:T(8,128)(2,1)S(1)} collective-permute-done((bf16[128,1024]{1,0:T(8,128)(2,1)}, bf16[128,1024]{1,0:T(8,128)(2,1)S(1)}, u32[]{:S(2)}, u32[]{:S(2)}) %collective-permute-start.15) | collective-permute-done | bytes 262176 | tf_op jit(solution)/shard_map/ppermute | solution.py:868
  99.7 11.6 %shard_map.263 = (bf16[1024,1024]{1,0:T(8,128)(2,1)}, bf16[1024,1024]{1,0:T(8,128)(2,1)}, bf16[1024,384]{1,0:T(8,128)(2,1)}, bf16[1024,640]{1,0:T(8,128)(2,1)}, ...) custom-call(s32[1]{0:T(128)} %bitcast.1.refs_1_.refs_0_, s32[1]{0:T(128)} %bitcast.8.refs_0_.refs_1_, ...), custom_call_target="tpu_custom_call" | custom-call | tf_op jit(solution)/shard_map/pallas_call | solution.py:387
  111.5 9.6 %shard_map.264 = (bf16[1024,256]{1,0:T(8,128)(2,1)}, bf16[1024,512]{1,0:T(8,128)(2,1)}, bf16[4,128,1024]{2,1,0:T(8,128)(2,1)}, bf16[4,128,1024]{2,1,0:T(8,128)(2,1)}, f32[8,128]{1,0:T(8,128)}) custom-call(s32[1]{0:T(128)} %bitcast.1.refs_1_.refs_0_, bf16[1024,1024]{1,0:T(8,128)(2,1)} %get-tuple-element.96.refs_2_.refs_1_.refs_0_, ...), custom_call_target="tpu_custom_call" | custom-call | tf_op jit(solution)/shard_map/pallas_call | solution.py:360
  121.2 2.7 collective-permute-done.22.refs_1_
  125.0 2.8 shard_map.265
  127.7 19.0 %all_to_all.35.refs_0_ = bf16[4,128,1024]{2,1,0:T(8,128)(2,1)} all-to-all(bf16[4,128,1024]{2,1,0:T(8,128)(2,1)} %shard_map.265), channel_id=1, replica_groups={{0,8,16,24},{4,12,20,28},{1,9,17,25},{5,13,21,29},{2,10,18,26},{6,14,22..., dimensions={0} | all-to-all | bytes 2097152 | tf_op jit(solution)/shard_map/all_to_all | solution.py:881
  146.8 3.7 %shard_map.266 = (f32[128,1024]{1,0:T(8,128)}, bf16[128,1024]{1,0:T(8,128)(2,1)}, bf16[8,128,128]{2,1,0:T(8,128)(2,1)}, f32[1,1024]{1,0:T(1,128)}, f32[8,128]{1,0:T(8,128)}) custom-call(bf16[4,128,1024]{2,1,0:T(8,128)(2,1)} %all_to_all.35.refs_0_, f32[128,1024]{1,0:T(8,128)} %get-tuple-element.95.refs_1_, bf16[128,1024]{1,0:T(8,128)(2,1)} %get-tuple-element.98.refs_2_, ...), custom_call_target="tpu_custom_call" | custom-call | tf_op jit(solution)/shard_map/pallas_call | solution.py:360
  150.5 5.7 %shard_map.267 = (bf16[4,8,32,768]{3,2,1,0:T(8,128)(2,1)}, f32[8,128]{1,0:T(8,128)}) custom-call(bf16[1024,1024]{1,0:T(8,128)(2,1)} %get-tuple-element.96.refs_2_.refs_1_.refs_0_, bf16[1024,1024]{1,0:T(8,128)(2,1)} %get-tuple-element.106.refs_2_.refs_1_, bf16[1024,256]{1,0:T(8,128)(2,1)} %get-tuple-element.110.refs_2_, ...), custom_call_target="tpu_custom_call" | custom-call | tf_op jit(solution)/shard_map/pallas_call | solution.py:360
  156.2 10.2 %all_to_all.36.refs_1_ = bf16[8,128,128]{2,1,0:T(8,128)(2,1)} all-to-all(bf16[8,128,128]{2,1,0:T(8,128)(2,1)S(1)} %copy-done.32), channel_id=1, replica_groups=mesh['seq'=8,'slot'=4] {'seq'}, dimensions={0} | all-to-all | bytes 524288 | tf_op jit(solution)/shard_map/all_to_all | solution.py:924
  170.0 13.7 %shard_map.268 = (bf16[4,128,1024]{2,1,0:T(8,128)(2,1)}, bf16[4,128,1024]{2,1,0:T(8,128)(2,1)}, bf16[1024,256]{1,0:T(8,128)(2,1)}, f32[2,128]{1,0:T(2,128)}, f32[8,128]{1,0:T(8,128)}) custom-call(s32[1]{0:T(128)} %copy.59.refs_0_, s32[1]{0:T(128)} %bitcast.1.refs_1_.refs_0_, bf16[1024,128]{1,0:T(8,128)(2,1)} %bitcast.46, bf16[1024,256]{1,0:T(8,128)(2,1)} %bitcast.45, ...), custom_call_target="tpu_custom_call" | custom-call | tf_op jit(solution)/shard_map/pallas_call | solution.py:360
  188.2 4.8 %shard_map.271 = (bf16[8,32,384]{2,1,0:T(8,128)(2,1)}, bf16[8,32,384]{2,1,0:T(8,128)(2,1)}, bf16[8,32,384]{2,1,0:T(8,128)(2,1)}, bf16[8,32,384]{2,1,0:T(8,128)(2,1)}, f32[8,128]{1,0:T(8,128)}) custom-call(s32[1]{0:T(128)} %bitcast.1.refs_1_.refs_0_, s32[1]{0:T(128)} %bitcast.8.refs_0_.refs_1_, bf16[1024,1024]{1,0:T(8,128)(2,1)} %get-tuple-element.127.refs_2_, ...), custom_call_target="tpu_custom_call" | custom-call | tf_op jit(solution)/shard_map/pallas_call | solution.py:360
  193.0 14.0 %all_to_all.37.refs_3_ = bf16[8,32,960]{2,1,0:T(8,128)(2,1)} all-to-all(bf16[8,32,960]{2,1,0:T(8,128)(2,1)} %bitcast.57), channel_id=1, replica_groups=mesh['seq'=8,'slot'=4] {'seq'}, dimensions={0} | all-to-all | bytes 983040 | tf_op jit(solution)/shard_map/all_to_all | solution.py:924
  208.6 2.3 collective-permute-start.39
  212.9 2.7 shard_map.273
  215.6 5.6 %shard_map.274 = (bf16[4,128,1024]{2,1,0:T(8,128)(2,1)}, bf16[4,128,1024]{2,1,0:T(8,128)(2,1)}, f32[8,128]{1,0:T(8,128)}) custom-call(s32[1]{0:T(128)} %bitcast.1.refs_1_.refs_0_, bf16[1024,384]{1,0:T(8,128)(2,1)} %get-tuple-element.105.refs_1_, bf16[1024,256]{1,0:T(8,128)(2,1)} %get-tuple-element.110.refs_2_, ...), custom_call_target="tpu_custom_call" | custom-call | tf_op jit(solution)/shard_map/pallas_call | solution.py:360
  221.2 4.1 %shard_map.275 = (f32[1,1024]{1,0:T(1,128)}, f32[8,128]{1,0:T(8,128)}) custom-call(s32[1]{0:T(128)} %bitcast.1.refs_1_.refs_0_, bf16[1024,1024]{1,0:T(8,128)(2,1)} %get-tuple-element.90.refs_1_, bf16[4,128,1024]{2,1,0:T(8,128)(2,1)} %get-tuple-element.124.refs_1_.refs_2_, bf16[4,128,1024]{2,1,0:T(8,128)(2,1)} %get-tuple-element.125.refs_3_, ...), custom_call_target="tpu_custom_call" | custom-call | tf_op jit(solution)/shard_map/pallas_call | solution.py:360
  225.3 2.4 collective-permute-done.39.refs_3_
  227.8 4.2 %collective-permute-done.40.refs_4_ = bf16[8,32,384]{2,1,0:T(8,128)(2,1)S(1)} collective-permute-done((bf16[8,32,384]{2,1,0:T(8,128)(2,1)S(1)}, bf16[8,32,384]{2,1,0:T(8,128)(2,1)S(1)}, u32[]{:S(2)}, u32[]{:S(2)}) %collective-permute-start.40) | collective-permute-done | bytes 196640 | tf_op jit(solution)/shard_map/ppermute | solution.py:892
  232.7 2.3 shard_map.279
  234.9 14.6 %all_to_all.38 = bf16[8,32,1152]{2,1,0:T(8,128)(2,1)} all-to-all(bf16[8,32,1152]{2,1,0:T(8,128)(2,1)} %shard_map.279), channel_id=1, replica_groups=mesh['seq'=8,'slot'=4] {'seq'}, dimensions={0} | all-to-all | bytes 1179648 | tf_op jit(solution)/shard_map/all_to_all | solution.py:924
  250.3 2.0 collective-permute-done.41
  254.4 1.8 collective-permute-done.42
  256.7 3.1 collective-permute-done.43
  259.9 2.6 collective-permute-start.46
  262.5 12.1 %collective-permute-start.45 = (f32[17,128]{1,0:T(8,128)S(1)}, f32[17,128]{1,0:T(8,128)S(1)}, u32[]{:S(2)}, u32[]{:S(2)}) collective-permute-start(f32[17,128]{1,0:T(8,128)S(1)} %add.62), channel_id=1, source_target_pairs={{0,2},{1,3},{2,0},{3,1},{4,6},{5,7},{6,4},{7,5},{8,10},{9,11},{10,... | collective-permute-start | bytes 26120 | tf_op jit(solution)/shard_map/ppermute | solution.py:892
  275.6 2.2 collective-permute-done.45
  280.4 2.7 shard_map.276
  289.5 2.5 shard_map.277
  292.9 4.7 %collective-permute-done.33 = bf16[128,1024]{1,0:T(8,128)(2,1)S(1)} collective-permute-done((bf16[128,1024]{1,0:T(8,128)(2,1)}, bf16[128,1024]{1,0:T(8,128)(2,1)S(1)}, u32[]{:S(2)}, u32[]{:S(2)}) %collective-permute-start.33) | collective-permute-done | bytes 262176 | tf_op jit(solution)/shard_map/ppermute | solution.py:868
  298.5 15.7 %all-gather.10.cloned.1.call-done = bf16[32,32,1152]{2,1,0:T(8,128)(2,1)} async-done(((bf16[8,32,1152]{2,1,0:T(8,128)(2,1)}), bf16[32,32,1152]{2,1,0:T(8,128)(2,1)}) %all-gather.10.cloned.1.call-update) | async-done | bytes 2359312 | tf_op jit(solution)/shard_map/all_gather | solution.py:1050
  314.2 6.0 %shard_map.280 = (f32[128,1024]{1,0:T(8,128)}, f32[128,512]{1,0:T(8,128)}, f32[128,512]{1,0:T(8,128)}, f32[128,1024]{1,0:T(8,128)}, f32[128,4608]{1,0:T(8,128)},...) custom-call(bf16[4,8,32,960]{3,2,1,0:T(8,128)(2,1)} %bitcast.55, bf16[4,8,32,1152]{3,2,1,0:T(8,128)(2,1)} %bitcast.47), custom_call_target="tpu_custom_call" | custom-call | tf_op jit(solution)/shard_map/pallas_call | solution.py:360
  (214 shorter events, 45.1 us)
Async XLA Ops:
  7.2 70.0 %all-gather.6.cloned.1.call-start = ((), (), s32[]{:S(2)}) async-start(), calls=%async_computation.9 | async-start | bytes 2359296 | tf_op jit(solution)/shard_map/all_gather | solution.py:938
  7.9 11.3 %collective-permute-start.5 = (bf16[128,1024]{1,0:T(8,128)(2,1)}, bf16[128,1024]{1,0:T(8,128)(2,1)S(1)}, u32[]{:S(2)}, u32[]{:S(2)}) collective-permute-start(bf16[128,1024]{1,0:T(8,128)(2,1)} %bitcast.48), channel_id=1, source_target_pairs={{0,24},{4,28},{8,16},{12,20},{16,8},{20,12},{24,0},{28,4},{1,25},{... | collective-permute-start | bytes 786440 | tf_op jit(solution)/shard_map/ppermute | solution.py:868
  11.9 13.8 %collective-permute-start.3 = (bf16[128,1024]{1,0:T(8,128)(2,1)}, bf16[128,1024]{1,0:T(8,128)(2,1)S(1)}, u32[]{:S(2)}, u32[]{:S(2)}) collective-permute-start(bf16[128,1024]{1,0:T(8,128)(2,1)} %bitcast.49), channel_id=1, source_target_pairs={{0,16},{4,20},{8,24},{12,28},{16,0},{20,4},{24,8},{28,12},{1,17},{... | collective-permute-start | bytes 786440 | tf_op jit(solution)/shard_map/ppermute | solution.py:868
  12.4 15.7 %collective-permute-start.1 = (bf16[128,1024]{1,0:T(8,128)(2,1)}, bf16[128,1024]{1,0:T(8,128)(2,1)S(1)}, u32[]{:S(2)}, u32[]{:S(2)}) collective-permute-start(bf16[128,1024]{1,0:T(8,128)(2,1)} %bitcast.50), channel_id=1, source_target_pairs={{0,8},{4,12},{8,0},{12,4},{16,24},{20,28},{24,16},{28,20},{1,9},{5... | collective-permute-start | bytes 786440 | tf_op jit(solution)/shard_map/ppermute | solution.py:868
  14.5 18.0 %all-to-all-start = ((bf16[8,128,256]{2,1,0:T(8,128)(2,1)}), bf16[8,128,256]{2,1,0:T(8,128)(2,1)S(1)}, u32[]{:S(2)}, u32[]{:S(2)}) async-start(bf16[8,128,256]{2,1,0:T(8,128)(2,1)} %get-tuple-element.89), calls=%async_computation | async-start | bytes 1048576 | tf_op jit(solution)/shard_map/all_to_all | solution.py:924
  18.6 13.2 %collective-permute-start = (bf16[128,1024]{1,0:T(8,128)(2,1)}, bf16[128,1024]{1,0:T(8,128)(2,1)S(1)}, u32[]{:S(2)}, u32[]{:S(2)}) collective-permute-start(bf16[128,1024]{1,0:T(8,128)(2,1)} %bitcast.51), channel_id=1, source_target_pairs={{0,4},{4,0},{8,12},{12,8},{16,20},{20,16},{24,28},{28,24},{1,5},{5... | collective-permute-start | bytes 786440 | tf_op jit(solution)/shard_map/ppermute | solution.py:868
  19.3 13.2 %collective-permute-start.6 = (bf16[128,1024]{1,0:T(8,128)(2,1)S(1)}, bf16[128,1024]{1,0:T(8,128)(2,1)S(1)}, u32[]{:S(2)}, u32[]{:S(2)}) collective-permute-start(bf16[128,1024]{1,0:T(8,128)(2,1)S(1)} %collective-permute-done.5.refs_8_.refs_7_), channel_id=1, source_target_pairs={{0,4},{4,0},{8,12},{12,8},{16,20},{20,16},{24,28},{28,24},{1,5},{5... | collective-permute-start | bytes 786440 | tf_op jit(solution)/shard_map/ppermute | solution.py:868
  25.6 6.8 %collective-permute-start.4 = (bf16[128,1024]{1,0:T(8,128)(2,1)S(1)}, bf16[128,1024]{1,0:T(8,128)(2,1)S(1)}, u32[]{:S(2)}, u32[]{:S(2)}) collective-permute-start(bf16[128,1024]{1,0:T(8,128)(2,1)S(1)} %collective-permute-done.3.refs_6_.refs_5_), channel_id=1, source_target_pairs={{0,4},{4,0},{8,12},{12,8},{16,20},{20,16},{24,28},{28,24},{1,5},{5... | collective-permute-start | bytes 786440 | tf_op jit(solution)/shard_map/ppermute | solution.py:868
  28.1 4.4 %collective-permute-start.2 = (bf16[128,1024]{1,0:T(8,128)(2,1)S(1)}, bf16[128,1024]{1,0:T(8,128)(2,1)S(1)}, u32[]{:S(2)}, u32[]{:S(2)}) collective-permute-start(bf16[128,1024]{1,0:T(8,128)(2,1)S(1)} %collective-permute-done.1.refs_4_.refs_3_), channel_id=1, source_target_pairs={{0,4},{4,0},{8,12},{12,8},{16,20},{20,16},{24,28},{28,24},{1,5},{5... | collective-permute-start | bytes 786440 | tf_op jit(solution)/shard_map/ppermute | solution.py:868
  33.5 22.9 %all-to-all-start.1 = ((bf16[8,64,1024]{2,1,0:T(8,128)(2,1)}), bf16[8,64,1024]{2,1,0:T(8,128)(2,1)S(1)}, u32[]{:S(2)}, u32[]{:S(2)}) async-start(bf16[8,64,1024]{2,1,0:T(8,128)(2,1)} %shard_map.260), calls=%async_computation.1 | async-start | bytes 2097152 | tf_op jit(solution)/shard_map/all_to_all | solution.py:924
  45.5 20.4 %collective-permute-start.12 = (bf16[1024,128]{1,0:T(8,128)(2,1)}, bf16[1024,128]{1,0:T(8,128)(2,1)S(1)}, u32[]{:S(2)}, u32[]{:S(2)}) collective-permute-start(bf16[1024,128]{1,0:T(8,128)(2,1)} %get-tuple-element.91.refs_2_.refs_4_), channel_id=1, source_target_pairs={{0,24},{4,28},{8,16},{12,20},{16,8},{20,12},{24,0},{28,4},{1,25},{... | collective-permute-start | bytes 786440 | tf_op jit(solution)/shard_map/ppermute | solution.py:868
  48.5 18.0 %collective-permute-start.10 = (bf16[1024,128]{1,0:T(8,128)(2,1)}, bf16[1024,128]{1,0:T(8,128)(2,1)S(1)}, u32[]{:S(2)}, u32[]{:S(2)}) collective-permute-start(bf16[1024,128]{1,0:T(8,128)(2,1)} %get-tuple-element.91.refs_2_.refs_4_), channel_id=1, source_target_pairs={{0,16},{4,20},{8,24},{12,28},{16,0},{20,4},{24,8},{28,12},{1,17},{... | collective-permute-start | bytes 786440 | tf_op jit(solution)/shard_map/ppermute | solution.py:868
  49.0 17.5 %collective-permute-start.8 = (bf16[1024,128]{1,0:T(8,128)(2,1)}, bf16[1024,128]{1,0:T(8,128)(2,1)S(1)}, u32[]{:S(2)}, u32[]{:S(2)}) collective-permute-start(bf16[1024,128]{1,0:T(8,128)(2,1)} %get-tuple-element.91.refs_2_.refs_4_), channel_id=1, source_target_pairs={{0,8},{4,12},{8,0},{12,4},{16,24},{20,28},{24,16},{28,20},{1,9},{5... | collective-permute-start | bytes 786440 | tf_op jit(solution)/shard_map/ppermute | solution.py:868
  56.4 40.7 %all-to-all-start.2 = ((bf16[8,128,768]{2,1,0:T(8,128)(2,1)}), bf16[8,128,768]{2,1,0:T(8,128)(2,1)S(1)}, u32[]{:S(2)}, u32[]{:S(2)}) async-start(bf16[8,128,768]{2,1,0:T(8,128)(2,1)} %shard_map.258.refs_12_), calls=%async_computation.2 | async-start | bytes 3145728 | tf_op jit(solution)/shard_map/all_to_all | solution.py:924
  63.6 129.3 %reduce-scatter.3.cloned.1.call-start = ((), (), s32[]{:S(2)}) async-start(), calls=%async_computation.10 | async-start | bytes 2621440 | tf_op jit(solution)/shard_map/reduce_scatter | solution.py:983
  67.8 27.2 %collective-permute-start.17 = (bf16[8,64,1024]{2,1,0:T(8,128)(2,1)}, bf16[8,64,1024]{2,1,0:T(8,128)(2,1)S(1)}, u32[]{:S(2)}, u32[]{:S(2)}) collective-permute-start(bf16[8,64,1024]{2,1,0:T(8,128)(2,1)} %get-tuple-element.100.refs_11_), channel_id=1, source_target_pairs={{0,1},{1,0},{2,3},{3,2},{4,5},{5,4},{6,7},{7,6},{8,9},{9,8},{10,11... | collective-permute-start | bytes 3145736 | tf_op jit(solution)/shard_map/ppermute | solution.py:892
  69.5 3.2 collective-permute-start.13
  70.0 4.3 %collective-permute-start.11 = (bf16[1024,128]{1,0:T(8,128)(2,1)}, bf16[1024,128]{1,0:T(8,128)(2,1)S(1)}, u32[]{:S(2)}, u32[]{:S(2)}) collective-permute-start(bf16[1024,128]{1,0:T(8,128)(2,1)} %copy-done.13), channel_id=1, source_target_pairs={{0,4},{4,0},{8,12},{12,8},{16,20},{20,16},{24,28},{28,24},{1,5},{5... | collective-permute-start | bytes 786440 | tf_op jit(solution)/shard_map/ppermute | solution.py:868
  70.0 7.1 %collective-permute-start.9 = (bf16[1024,128]{1,0:T(8,128)(2,1)}, bf16[1024,128]{1,0:T(8,128)(2,1)}, u32[]{:S(2)}, u32[]{:S(2)}) collective-permute-start(bf16[1024,128]{1,0:T(8,128)(2,1)} %copy-done.14), channel_id=1, source_target_pairs={{0,4},{4,0},{8,12},{12,8},{16,20},{20,16},{24,28},{28,24},{1,5},{5... | collective-permute-start | bytes 786440 | tf_op jit(solution)/shard_map/ppermute | solution.py:868
  71.2 19.5 %collective-permute-start.16 = (bf16[128,1024]{1,0:T(8,128)(2,1)}, bf16[128,1024]{1,0:T(8,128)(2,1)S(1)}, u32[]{:S(2)}, u32[]{:S(2)}) collective-permute-start(bf16[128,1024]{1,0:T(8,128)(2,1)} %get-tuple-element.98.refs_2_), channel_id=1, source_target_pairs={{0,24},{4,28},{8,16},{12,20},{16,8},{20,12},{24,0},{28,4},{1,25},{... | collective-permute-start | bytes 786440 | tf_op jit(solution)/shard_map/ppermute | solution.py:868
  72.7 22.3 %collective-permute-start.15 = (bf16[128,1024]{1,0:T(8,128)(2,1)}, bf16[128,1024]{1,0:T(8,128)(2,1)S(1)}, u32[]{:S(2)}, u32[]{:S(2)}) collective-permute-start(bf16[128,1024]{1,0:T(8,128)(2,1)} %get-tuple-element.98.refs_2_), channel_id=1, source_target_pairs={{0,16},{4,20},{8,24},{12,28},{16,0},{20,4},{24,8},{28,12},{1,17},{... | collective-permute-start | bytes 786440 | tf_op jit(solution)/shard_map/ppermute | solution.py:868
  75.0 20.0 %collective-permute-start.14 = (bf16[128,1024]{1,0:T(8,128)(2,1)}, bf16[128,1024]{1,0:T(8,128)(2,1)S(1)}, u32[]{:S(2)}, u32[]{:S(2)}) collective-permute-start(bf16[128,1024]{1,0:T(8,128)(2,1)} %get-tuple-element.98.refs_2_), channel_id=1, source_target_pairs={{0,8},{4,12},{8,0},{12,4},{16,24},{20,28},{24,16},{28,20},{1,9},{5... | collective-permute-start | bytes 786440 | tf_op jit(solution)/shard_map/ppermute | solution.py:868
  96.6 2.4 collective-permute-start.21
  111.3 114.0 %reduce-scatter.5.cloned.1.call-start = ((), (), s32[]{:S(2)}) async-start(), calls=%async_computation.11 | async-start | bytes 1966080 | tf_op jit(solution)/shard_map/reduce_scatter | solution.py:999
  121.1 2.9 collective-permute-start.22
  156.2 142.3 %all-gather.8.cloned.1.call-start = ((), (), s32[]{:S(2)}) async-start(), calls=%async_computation.12 | async-start | bytes 2621440 | tf_op jit(solution)/shard_map/all_gather | solution.py:1037
  166.5 17.2 %collective-permute-start.26 = (bf16[128,1024]{1,0:T(8,128)(2,1)}, bf16[128,1024]{1,0:T(8,128)(2,1)S(1)}, u32[]{:S(2)}, u32[]{:S(2)}) collective-permute-start(bf16[128,1024]{1,0:T(8,128)(2,1)} %shard_map.269.refs_0_), channel_id=1, source_target_pairs={{0,24},{4,28},{8,16},{12,20},{16,8},{20,12},{24,0},{28,4},{1,25},{... | collective-permute-start | bytes 786440 | tf_op jit(solution)/shard_map/ppermute | solution.py:868
  167.0 16.7 %collective-permute-start.25 = (bf16[128,1024]{1,0:T(8,128)(2,1)}, bf16[128,1024]{1,0:T(8,128)(2,1)S(1)}, u32[]{:S(2)}, u32[]{:S(2)}) collective-permute-start(bf16[128,1024]{1,0:T(8,128)(2,1)} %shard_map.269.refs_0_), channel_id=1, source_target_pairs={{0,16},{4,20},{8,24},{12,28},{16,0},{20,4},{24,8},{28,12},{1,17},{... | collective-permute-start | bytes 786440 | tf_op jit(solution)/shard_map/ppermute | solution.py:868
  168.5 15.2 %collective-permute-start.24 = (bf16[128,1024]{1,0:T(8,128)(2,1)}, bf16[128,1024]{1,0:T(8,128)(2,1)S(1)}, u32[]{:S(2)}, u32[]{:S(2)}) collective-permute-start(bf16[128,1024]{1,0:T(8,128)(2,1)} %shard_map.269.refs_0_), channel_id=1, source_target_pairs={{0,8},{4,12},{8,0},{12,4},{16,24},{20,28},{24,16},{28,20},{1,9},{5... | collective-permute-start | bytes 786440 | tf_op jit(solution)/shard_map/ppermute | solution.py:868
  185.1 2.4 collective-permute-start.30
  207.0 107.1 %all-gather.10.cloned.1.call-start = ((), (), s32[]{:S(2)}) async-start(), calls=%async_computation.13 | async-start | bytes 2949120 | tf_op jit(solution)/shard_map/all_gather | solution.py:1050
  207.3 4.5 %collective-permute-start.23 = (bf16[4,128,1024]{2,1,0:T(8,128)(2,1)S(1)}, bf16[4,128,1024]{2,1,0:T(8,128)(2,1)S(1)}, u32[]{:S(2)}, u32[]{:S(2)}) collective-permute-start(bf16[4,128,1024]{2,1,0:T(8,128)(2,1)S(1)} %copy-done.5), channel_id=1, source_target_pairs={{0,4},{4,0},{8,12},{12,8},{16,20},{20,16},{24,28},{28,24},{1,5},{5... | collective-permute-start | bytes 3145736 | tf_op jit(solution)/shard_map/ppermute | solution.py:868
  207.4 17.9 %collective-permute-start.38 = (bf16[8,32,384]{2,1,0:T(8,128)(2,1)}, bf16[8,32,384]{2,1,0:T(8,128)(2,1)S(1)}, u32[]{:S(2)}, u32[]{:S(2)}) collective-permute-start(bf16[8,32,384]{2,1,0:T(8,128)(2,1)} %get-tuple-element.152), channel_id=1, source_target_pairs={{0,1},{1,0},{2,3},{3,2},{4,5},{5,4},{6,7},{7,6},{8,9},{9,8},{10,11... | collective-permute-start | bytes 589832 | tf_op jit(solution)/shard_map/ppermute | solution.py:892
  208.6 19.1 %collective-permute-start.39 = (bf16[8,32,384]{2,1,0:T(8,128)(2,1)}, bf16[8,32,384]{2,1,0:T(8,128)(2,1)S(1)}, u32[]{:S(2)}, u32[]{:S(2)}) collective-permute-start(bf16[8,32,384]{2,1,0:T(8,128)(2,1)} %get-tuple-element.153), channel_id=1, source_target_pairs={{0,2},{1,3},{2,0},{3,1},{4,6},{5,7},{6,4},{7,5},{8,10},{9,11},{10,... | collective-permute-start | bytes 589832 | tf_op jit(solution)/shard_map/ppermute | solution.py:892
  211.0 21.0 %collective-permute-start.40 = (bf16[8,32,384]{2,1,0:T(8,128)(2,1)S(1)}, bf16[8,32,384]{2,1,0:T(8,128)(2,1)S(1)}, u32[]{:S(2)}, u32[]{:S(2)}) collective-permute-start(bf16[8,32,384]{2,1,0:T(8,128)(2,1)S(1)} %copy-done.51), channel_id=1, source_target_pairs={{0,3},{1,2},{2,1},{3,0},{4,7},{5,6},{6,5},{7,4},{8,11},{9,10},{10,... | collective-permute-start | bytes 589832 | tf_op jit(solution)/shard_map/ppermute | solution.py:892
  249.6 29.8 %collective-permute-start.31 = (bf16[4,128,1024]{2,1,0:T(8,128)(2,1)}, bf16[4,128,1024]{2,1,0:T(8,128)(2,1)S(1)}, u32[]{:S(2)}, u32[]{:S(2)}) collective-permute-start(bf16[4,128,1024]{2,1,0:T(8,128)(2,1)} %get-tuple-element.138), channel_id=1, source_target_pairs={{0,4},{4,0},{8,12},{12,8},{16,20},{20,16},{24,28},{28,24},{1,5},{5... | collective-permute-start | bytes 3145736 | tf_op jit(solution)/shard_map/ppermute | solution.py:868
  249.8 2.5 collective-permute-start.41
  252.3 3.8 %collective-permute-start.42 = (f32[17,128]{1,0:T(8,128)S(1)}, f32[17,128]{1,0:T(8,128)S(1)}, u32[]{:S(2)}, u32[]{:S(2)}) collective-permute-start(f32[17,128]{1,0:T(8,128)S(1)} %bitcast_add_fusion), channel_id=1, source_target_pairs={{0,8},{4,12},{8,0},{12,4},{16,24},{20,28},{24,16},{28,20},{1,9},{5... | collective-permute-start | bytes 26120 | tf_op jit(solution)/shard_map/ppermute | solution.py:868
  252.9 32.2 %collective-permute-start.35 = (bf16[128,1024]{1,0:T(8,128)(2,1)}, bf16[128,1024]{1,0:T(8,128)(2,1)S(1)}, u32[]{:S(2)}, u32[]{:S(2)}) collective-permute-start(bf16[128,1024]{1,0:T(8,128)(2,1)} %get-tuple-element.146), channel_id=1, source_target_pairs={{0,8},{4,12},{8,0},{12,4},{16,24},{20,28},{24,16},{28,20},{1,9},{5... | collective-permute-start | bytes 786440 | tf_op jit(solution)/shard_map/ppermute | solution.py:868
  256.2 3.7 %collective-permute-start.43 = (f32[17,128]{1,0:T(8,128)S(1)}, f32[17,128]{1,0:T(8,128)S(1)}, u32[]{:S(2)}, u32[]{:S(2)}) collective-permute-start(f32[17,128]{1,0:T(8,128)S(1)} %fusion.2), channel_id=1, source_target_pairs={{0,16},{4,20},{8,24},{12,28},{16,0},{20,4},{24,8},{28,12},{1,17},{... | collective-permute-start | bytes 26120 | tf_op jit(solution)/shard_map/ppermute | solution.py:868
  259.9 15.2 %collective-permute-start.46 = (f32[17,128]{1,0:T(8,128)S(1)}, f32[17,128]{1,0:T(8,128)S(1)}, u32[]{:S(2)}, u32[]{:S(2)}) collective-permute-start(f32[17,128]{1,0:T(8,128)S(1)} %add.62), channel_id=1, source_target_pairs={{0,3},{1,2},{2,1},{3,0},{4,7},{5,6},{6,5},{7,4},{8,11},{9,10},{10,... | collective-permute-start | bytes 26120 | tf_op jit(solution)/shard_map/ppermute | solution.py:892
  262.5 15.4 %collective-permute-start.45 = (f32[17,128]{1,0:T(8,128)S(1)}, f32[17,128]{1,0:T(8,128)S(1)}, u32[]{:S(2)}, u32[]{:S(2)}) collective-permute-start(f32[17,128]{1,0:T(8,128)S(1)} %add.62), channel_id=1, source_target_pairs={{0,2},{1,3},{2,0},{3,1},{4,6},{5,7},{6,4},{7,5},{8,10},{9,11},{10,... | collective-permute-start | bytes 26120 | tf_op jit(solution)/shard_map/ppermute | solution.py:892
  274.5 4.9 %collective-permute-start.44 = (f32[17,128]{1,0:T(8,128)S(1)}, f32[17,128]{1,0:T(8,128)S(1)}, u32[]{:S(2)}, u32[]{:S(2)}) collective-permute-start(f32[17,128]{1,0:T(8,128)S(1)} %add.62), channel_id=1, source_target_pairs={{0,1},{1,0},{2,3},{3,2},{4,5},{5,4},{6,7},{7,6},{8,9},{9,8},{10,11... | collective-permute-start | bytes 26120 | tf_op jit(solution)/shard_map/ppermute | solution.py:892
  275.1 13.6 %collective-permute-start.36 = (bf16[128,1024]{1,0:T(8,128)(2,1)S(1)}, bf16[128,1024]{1,0:T(8,128)(2,1)S(1)}, u32[]{:S(2)}, u32[]{:S(2)}) collective-permute-start(bf16[128,1024]{1,0:T(8,128)(2,1)S(1)} %copy-done.50), channel_id=1, source_target_pairs={{0,16},{4,20},{8,24},{12,28},{16,0},{20,4},{24,8},{28,12},{1,17},{... | collective-permute-start | bytes 786440 | tf_op jit(solution)/shard_map/ppermute | solution.py:868
  277.9 10.8 %collective-permute-start.37 = (bf16[128,1024]{1,0:T(8,128)(2,1)S(1)}, bf16[128,1024]{1,0:T(8,128)(2,1)S(1)}, u32[]{:S(2)}, u32[]{:S(2)}) collective-permute-start(bf16[128,1024]{1,0:T(8,128)(2,1)S(1)} %copy-done.49), channel_id=1, source_target_pairs={{0,24},{4,28},{8,16},{12,20},{16,8},{20,12},{24,0},{28,4},{1,25},{... | collective-permute-start | bytes 786440 | tf_op jit(solution)/shard_map/ppermute | solution.py:868
  283.1 9.9 %collective-permute-start.32 = (bf16[128,1024]{1,0:T(8,128)(2,1)}, bf16[128,1024]{1,0:T(8,128)(2,1)S(1)}, u32[]{:S(2)}, u32[]{:S(2)}) collective-permute-start(bf16[128,1024]{1,0:T(8,128)(2,1)} %get-tuple-element.142), channel_id=1, source_target_pairs={{0,8},{4,12},{8,0},{12,4},{16,24},{20,28},{24,16},{28,20},{1,9},{5... | collective-permute-start | bytes 786440 | tf_op jit(solution)/shard_map/ppermute | solution.py:868
  284.1 13.5 %collective-permute-start.33 = (bf16[128,1024]{1,0:T(8,128)(2,1)}, bf16[128,1024]{1,0:T(8,128)(2,1)S(1)}, u32[]{:S(2)}, u32[]{:S(2)}) collective-permute-start(bf16[128,1024]{1,0:T(8,128)(2,1)} %get-tuple-element.143), channel_id=1, source_target_pairs={{0,16},{4,20},{8,24},{12,28},{16,0},{20,4},{24,8},{28,12},{1,17},{... | collective-permute-start | bytes 786440 | tf_op jit(solution)/shard_map/ppermute | solution.py:868
  285.1 12.5 %collective-permute-start.34 = (bf16[128,1024]{1,0:T(8,128)(2,1)}, bf16[128,1024]{1,0:T(8,128)(2,1)S(1)}, u32[]{:S(2)}, u32[]{:S(2)}) collective-permute-start(bf16[128,1024]{1,0:T(8,128)(2,1)} %get-tuple-element.144), channel_id=1, source_target_pairs={{0,24},{4,28},{8,16},{12,20},{16,8},{20,12},{24,0},{28,4},{1,25},{... | collective-permute-start | bytes 786440 | tf_op jit(solution)/shard_map/ppermute | solution.py:868
  (59 other events, 351.9 us)
Sparse Core Ops, SparseCore 0:
  9.9 39.6 all-gather.5
  111.4 43.5 reduce-scatter.2
  157.4 34.5 reduce-scatter.4
  207.2 56.4 all-gather.7
  265.2 48.9 all-gather.9
